TPU v7x, 32 devices: a whole 2x2x4 slice. The times are simulated.
32 devices in a mesh: blk: 16 (over z, x, core), head: 2 (over y).
Axes of the slice: x: 2, y: 2, z: 4, core: 2. Of those that a mesh axis runs over, the one named last changes fastest.
Arguments:
- queries: bfloat16 [2, 2048, 32, 128], P(None, 'blk', 'head'), may hold values from -30 to 30
- new_keys: bfloat16 [2, 2048, 16, 128], P(None, 'blk', 'head'), may hold values from -30 to 30
- new_values: bfloat16 [2, 2048, 16, 128], P(None, 'blk', 'head'), may hold values from -6 to 6
- pool_keys: bfloat16 [32, 128, 16, 128], P('blk', None, 'head'), may hold values from -30 to 30
- pool_values: bfloat16 [32, 128, 16, 128], P('blk', None, 'head'), may hold values from -6 to 6
- page_table: int32 [2, 16], replicated, may hold values from 0 to 31, as said below
- cache_len: int32 [2], replicated, may hold values from 512 to 2048, as said below
- out_weight: bfloat16 [32, 128, 4608], P('head'), may hold values from -0.09375 to 0.09375
- residual: bfloat16 [2, 2048, 4608], P(None, ('blk', 'head')), may hold values from -6 to 6
- post_gain: float32 [4608], replicated, may hold values from 0.1 to 1.9
Outputs:
- mixed: bfloat16 [2, 2048, 4608], P(None, ('blk', 'head'))
Inputs may be any that keep to these rules, and one draw needn't show every extreme that they name: `page_table`: every pool page appears exactly once in the table. `cache_len`: one request has exactly 2048 cached tokens.
All inputs are finite; a program needn't handle non-finite values.
Results may differ from a plain program's by a relative error of at most 0.015.
Values may be sent and summed in bfloat16 or wider, within the bound.
No kernel may reach another device: no remote copies, remote signals or barrier semaphores. Data moves between devices by JAX's collectives and lax.ppermute only.
A program may use at most 128 MiB of HBM per device.

v0:
```python
import jax
import jax.numpy as jnp
from jax import lax
from jax.sharding import PartitionSpec as P

soft_cap = 50.0
score_scale = 144.0 ** (-0.5)
norm_eps = 1e-06


def group_pages(page_count, page_len):
    width = max(1, min(page_count, 2048 // page_len))
    while page_count % width:
        width -= 1
    return width


def attend_pages(running, grouped, key_pages, value_pages, valid_keys):
    page_count, page_len, kv_heads, head_dim = key_pages.shape
    tok_rows = valid_keys.shape[1]
    width = group_pages(page_count, page_len)
    groups = page_count // width
    key_groups = key_pages.reshape(groups, width * page_len, kv_heads, head_dim)
    value_groups = value_pages.reshape(groups, width * page_len, kv_heads, head_dim)
    valid_groups = (
        valid_keys.reshape(groups, width, tok_rows, page_len)
        .transpose(0, 2, 1, 3)
        .reshape(groups, tok_rows, width * page_len)
    )

    def compute(carry_in, key_block, value_block, valid_block):
        numerator, denominator = carry_in
        scores = (
            jnp.einsum("tkgd,skd->kgts", grouped, key_block, preferred_element_type=jnp.float32)
            * score_scale
        )
        capped = soft_cap * jnp.tanh(scores / soft_cap)
        weights = jnp.where(valid_block[None, None], jnp.exp(capped), 0.0).astype(jnp.bfloat16)
        numerator = numerator + jnp.einsum(
            "kgts,skd->tkgd", weights, value_block, preferred_element_type=jnp.float32
        )
        denominator = denominator + jnp.sum(weights.astype(jnp.float32), axis=-1)
        return (numerator, denominator)

    def one_group(carry_in, inputs):
        key_block, value_block, valid_block = inputs
        carry_out = compute(carry_in, key_block, value_block, valid_block)
        return (carry_out, None)

    result, _ = lax.scan(one_group, running, (key_groups, value_groups, valid_groups))
    return result


def shards(
    queries,
    new_keys,
    new_values,
    pool_keys,
    pool_values,
    page_table,
    cache_len,
    out_weight,
    residual,
    post_gain,
):
    req_count, per_req, heads_here, head_dim = queries.shape
    tok_dev = req_count * per_req
    kv_here = new_keys.shape[2]
    page_len = pool_keys.shape[1]
    slot_count = page_table.shape[1]
    blk_place = lax.axis_index("blk")
    row_ids = jnp.arange(tok_dev, dtype=jnp.int32)
    row_request = row_ids // per_req
    row_offset = blk_place * per_req + row_ids % per_req
    grouped = queries.reshape(tok_dev, kv_here, heads_here // kv_here, head_dim)
    page_rows = jnp.arange(page_len, dtype=jnp.int32)
    request_ids = jnp.arange(req_count, dtype=jnp.int32)
    row_onehot = row_request[:, None] == request_ids[None, :]
    start_carry = (
        jnp.zeros((tok_dev, kv_here, heads_here // kv_here, head_dim), jnp.float32),
        jnp.zeros((kv_here, heads_here // kv_here, tok_dev), jnp.float32),
    )
    pieces = (
        lax.all_gather(pool_keys, "blk", axis=0, tiled=True),
        lax.all_gather(pool_values, "blk", axis=0, tiled=True),
    )
    page_ids = jnp.arange(pieces[0].shape[0], dtype=jnp.int32)
    matches = page_ids[:, None, None] == page_table[None, :, :]
    slot_index = jnp.sum(
        jnp.where(matches, jnp.arange(slot_count, dtype=jnp.int32)[None, None, :], 0), axis=2
    )
    owned_page = jnp.any(matches, axis=2)
    position = slot_index[:, :, None] * page_len + page_rows[None, None, :]
    keep_keys = owned_page[:, :, None] & (position < cache_len[None, :, None])
    running = attend_pages(
        start_carry,
        grouped,
        pieces[0],
        pieces[1],
        jnp.any(keep_keys[:, None, :, :] & row_onehot[None, :, :, None], axis=2),
    )
    pieces = (
        lax.all_gather(new_keys, "blk", axis=1, tiled=True),
        lax.all_gather(new_values, "blk", axis=1, tiled=True),
    )
    piece_pages = pieces[0].shape[1] // page_len
    page_index = jnp.arange(req_count * piece_pages, dtype=jnp.int32)
    firsts = page_index % piece_pages * page_len
    key_pages = pieces[0].reshape(req_count * piece_pages, page_len, kv_here, head_dim)
    value_pages = pieces[1].reshape(req_count * piece_pages, page_len, kv_here, head_dim)
    offsets = firsts[:, None] + page_rows[None, :]
    same_request = (page_index // piece_pages)[:, None] == row_request[None, :]
    running = attend_pages(
        running,
        grouped,
        key_pages,
        value_pages,
        same_request[:, :, None] & (offsets[:, None, :] <= row_offset[None, :, None]),
    )
    numerator, denominator = running
    attended = (numerator / jnp.transpose(denominator, (2, 0, 1))[..., None]).astype(jnp.bfloat16)
    head_count = lax.axis_size("head")
    share = per_req // head_count
    feature_len = heads_here * head_dim
    attended = (
        attended.reshape(req_count, head_count, share, feature_len)
        .transpose(1, 0, 2, 3)
        .reshape(tok_dev, feature_len)
    )
    weight_rows = out_weight.reshape(feature_len, out_weight.shape[2])
    projected = lax.psum_scatter(
        jnp.dot(attended, weight_rows, preferred_element_type=jnp.float32).astype(jnp.bfloat16),
        "head",
        scatter_dimension=0,
        tiled=True,
    ).astype(jnp.float32)
    projected = projected.reshape(req_count, share, projected.shape[1])
    inv_rms = lax.rsqrt(jnp.mean(projected * projected, axis=-1, keepdims=True) + norm_eps)
    mixed_out = residual.astype(jnp.float32) + post_gain * projected * inv_rms
    return mixed_out.astype(jnp.bfloat16)


def solution(mesh):
    placed = (
        P(None, "blk", "head", None),
        P(None, "blk", "head", None),
        P(None, "blk", "head", None),
        P("blk", None, "head", None),
        P("blk", None, "head", None),
        P(),
        P(),
        P("head", None, None),
        P(None, ("blk", "head"), None),
        P(),
    )
    return jax.shard_map(
        shards,
        mesh=mesh,
        in_specs=placed,
        out_specs=P(None, ("blk", "head"), None),
        check_vma=False,
    )
```

profile of v0, /device:TPU:0, one launch (start us, length us, event | category | flops | bytes accessed | tf_op | source)
XLA Modules:
  0.0 426.3 jit_solution(8385932960749628797)
XLA Ops:
  6.5 0.7 all-gather.7.cloned.1.call-update
  7.3 0.7 all-gather.5.cloned.1.call-update
  8.1 1.9 copy.43
  10.1 2.1 copy.42
  12.8 1.1 and_reduce_fusion
  14.0 2.8 copy.38
  16.8 2.5 copy.39
  19.4 1.7 bitcast_and_fusion
  21.1 66.1 %all-gather.7.cloned.1.call-done = bf16[32,128,8,128]{3,2,1,0:T(8,128)(2,1)} async-done(((bf16[2,128,8,128]{3,2,1,0:T(8,128)(2,1)}), bf16[32,128,8,128]{3,2,1,0:T(8,128)(2,1)}) %all-gather.7.cloned.1.call-update) | async-done | bytes 8388624 | tf_op jit(solution)/shard_map/all_gather | solution.py:84
  87.2 75.3 %all-gather.5.cloned.1.call-done = bf16[32,128,8,128]{3,2,1,0:T(8,128)(2,1)} async-done(((bf16[2,128,8,128]{3,2,1,0:T(8,128)(2,1)}), bf16[32,128,8,128]{3,2,1,0:T(8,128)(2,1)}) %all-gather.5.cloned.1.call-update) | async-done | bytes 8388624 | tf_op jit(solution)/shard_map/all_gather | solution.py:85
  162.5 69.9 %while.30 = (s32[]{:T(128)}, f32[256,8,2,128]{0,3,2,1:T(8,128)S(1)}, f32[8,2,256]{2,1,0:T(2,128)S(1)}, bf16[2,2048,8,128]{3,2,1,0:T(8,128)(2,1)}, pred[2,256,204...) while((s32[]{:T(128)}, ...), condition=%wide.region_5.6_spmd.clone, body=%wide.region_3.5_spmd.clone.sunk | while | flops 4346351616 | bytes 82378912 | solution.py:50
  162.5 5.2 %constant_dynamic-slice_fusion.3 = (bf16[1,2048,8,128]{3,2,1,0:T(8,128)(2,1)S(1)}, bf16[1,2048,8,128]{3,2,1,0:T(8,128)(2,1)}) fusion(bf16[2,2048,8,128]{3,2,1,0:T(8,128)(2,1)} %get-tuple-element.389, s32[]{:T(128)} %get-tuple-element.375, bf16[2,2048,8,128]{3,2,1,0:T(8,128)(2,1)} %get-tuple-element.387), kind=kLoop, calls=%fused_computation.21.clone.1 | loop fusion | bytes 16777220 | tf_op jit(solution)/shard_map/while/body/jit(dynamic_index_in_dim)/dynamic_slice | solution.py:50
  168.0 12.9 %convert_reduce_fusion.5 = (f32[8,2,256]{2,1,0:T(2,128)S(1)}, bf16[8,2,256,2048]{2,3,1,0:T(8,128)(2,1)}) fusion(bf16[256,8,2,128]{3,0,2,1:T(8,128)(2,1)S(1)} %copy-done.3, bf16[1,2048,8,128]{3,2,1,0:T(8,128)(2,1)S(1)} %get-tuple-element.362, pred[256,2048]{0,1:T(8,128)(4,1)S(1)} %dynamic-slice_bitcast_fusion.5), kind=kOutput, calls=%fused_computation.14.clone.1 | convolution fusion | flops 2197811200 | bytes 22560768 | tf_op jit(solution)/shard_map/while/body/eval_jaxpr/tkgd,skd->kgts/dot_general | solution.py:34
  180.9 6.7 %copy.63 = bf16[1,2048,8,128]{1,3,2,0:T(8,128)(2,1)} copy(bf16[1,2048,8,128]{3,2,1,0:T(8,128)(2,1)} %get-tuple-element.364) | data formatting | bytes 8388608 | tf_op jit(solution)/shard_map/while/body/jit(dynamic_index_in_dim)/dynamic_slice | solution.py:50
  187.6 9.8 %bitcast_add_fusion.6 = f32[256,8,2,128]{0,3,2,1:T(8,128)S(1)} fusion(f32[256,8,2,128]{0,3,2,1:T(8,128)S(1)} %get-tuple-element.376, bf16[8,2,256,2048]{2,3,1,0:T(8,128)(2,1)} %get-tuple-element.363, bf16[1,2048,8,128]{1,3,2,0:T(8,128)(2,1)} %copy.63, pred[]{:T(512)S(6)} %compare.15), kind=kOutput, calls=%fused_computation.18.clone.1 | convolution fusion | flops 2148532224 | bytes 25165824 | tf_op jit(solution)/shard_map/while/body/eval_jaxpr/kgts,skd->tkgd/dot_general | solution.py:39
  197.5 5.3 %constant_dynamic-slice_fusion.3 = (bf16[1,2048,8,128]{3,2,1,0:T(8,128)(2,1)S(1)}, bf16[1,2048,8,128]{3,2,1,0:T(8,128)(2,1)}) fusion(bf16[2,2048,8,128]{3,2,1,0:T(8,128)(2,1)} %get-tuple-element.389, s32[]{:T(128)} %get-tuple-element.375, bf16[2,2048,8,128]{3,2,1,0:T(8,128)(2,1)} %get-tuple-element.387), kind=kLoop, calls=%fused_computation.21.clone.1 | loop fusion | bytes 16777220 | tf_op jit(solution)/shard_map/while/body/jit(dynamic_index_in_dim)/dynamic_slice | solution.py:50
  202.9 12.9 %convert_reduce_fusion.5 = (f32[8,2,256]{2,1,0:T(2,128)S(1)}, bf16[8,2,256,2048]{2,3,1,0:T(8,128)(2,1)}) fusion(bf16[256,8,2,128]{3,0,2,1:T(8,128)(2,1)S(1)} %copy-done.3, bf16[1,2048,8,128]{3,2,1,0:T(8,128)(2,1)S(1)} %get-tuple-element.362, pred[256,2048]{0,1:T(8,128)(4,1)S(1)} %dynamic-slice_bitcast_fusion.5), kind=kOutput, calls=%fused_computation.14.clone.1 | convolution fusion | flops 2197811200 | bytes 22560768 | tf_op jit(solution)/shard_map/while/body/eval_jaxpr/tkgd,skd->kgts/dot_general | solution.py:34
  215.9 6.7 %copy.63 = bf16[1,2048,8,128]{1,3,2,0:T(8,128)(2,1)} copy(bf16[1,2048,8,128]{3,2,1,0:T(8,128)(2,1)} %get-tuple-element.364) | data formatting | bytes 8388608 | tf_op jit(solution)/shard_map/while/body/jit(dynamic_index_in_dim)/dynamic_slice | solution.py:50
  222.5 9.8 %bitcast_add_fusion.6 = f32[256,8,2,128]{0,3,2,1:T(8,128)S(1)} fusion(f32[256,8,2,128]{0,3,2,1:T(8,128)S(1)} %get-tuple-element.376, bf16[8,2,256,2048]{2,3,1,0:T(8,128)(2,1)} %get-tuple-element.363, bf16[1,2048,8,128]{1,3,2,0:T(8,128)(2,1)} %copy.63, pred[]{:T(512)S(6)} %compare.15), kind=kOutput, calls=%fused_computation.18.clone.1 | convolution fusion | flops 2148532224 | bytes 25165824 | tf_op jit(solution)/shard_map/while/body/eval_jaxpr/kgts,skd->tkgd/dot_general | solution.py:39
  232.4 5.5 %all-gather.11.cloned.1.call-done = bf16[2,2048,8,128]{3,1,2,0:T(8,128)(2,1)} async-done(((bf16[2,128,8,128]{3,1,2,0:T(8,128)(2,1)}), bf16[2,2048,8,128]{3,1,2,0:T(8,128)(2,1)}) %all-gather.11.cloned.1.call-update) | async-done | bytes 8388624 | tf_op jit(solution)/shard_map/all_gather | solution.py:103
  237.9 78.4 %all-gather.9.cloned.1.call-done = bf16[2,2048,8,128]{1,3,2,0:T(8,128)(2,1)} async-done(((bf16[2,128,8,128]{1,3,2,0:T(8,128)(2,1)}), bf16[2,2048,8,128]{1,3,2,0:T(8,128)(2,1)}) %all-gather.9.cloned.1.call-update) | async-done | bytes 8388624 | tf_op jit(solution)/shard_map/all_gather | solution.py:104
  316.3 50.9 %while.29 = (s32[]{:T(128)}, f32[256,8,2,128]{0,3,2,1:T(8,128)S(1)}, f32[8,2,256]{2,1,0:T(2,128)S(1)}, bf16[2,2048,8,128]{1,3,2,0:T(8,128)(2,1)}, pred[2,256,204...) while((s32[]{:T(128)}, ...), condition=%wide.region_8.9_spmd, body=%wide.region_6.8_spmd.sunk | while | flops 4345823232 | bytes 48825432 | solution.py:50
  316.5 15.2 %convert_reduce_fusion.4 = (f32[8,2,256]{2,1,0:T(2,128)S(1)}, bf16[8,2,256,2048]{2,3,1,0:T(8,128)(2,1)}) fusion(bf16[256,8,2,128]{3,0,2,1:T(8,128)(2,1)} %get-tuple-element.415, bf16[2,2048,8,128]{3,1,2,0:T(8,128)(2,1)} %get-tuple-element.414, s32[]{:T(128)} %get-tuple-element.401, pred[256,2048]{0,1:T(8,128)(4,1)S(1)} %dynamic-slice_bitcast_fusion.4), kind=kOutput, calls=%fused_computation.2.clone.1 | convolution fusion | flops 2197811200 | bytes 22561280 | tf_op jit(solution)/shard_map/while/body/eval_jaxpr/tkgd,skd->kgts/dot_general | solution.py:34
  331.7 10.0 %bitcast_add_fusion.5 = f32[256,8,2,128]{0,3,2,1:T(8,128)S(1)} fusion(f32[256,8,2,128]{0,3,2,1:T(8,128)S(1)} %get-tuple-element.402, bf16[8,2,256,2048]{2,3,1,0:T(8,128)(2,1)} %get-tuple-element.353, bf16[2,2048,8,128]{1,3,2,0:T(8,128)(2,1)} %get-tuple-element.412, s32[]{:T(128)} %get-tuple-element.401), kind=kOutput, calls=%fused_computation.8.clone.1 | convolution fusion | flops 2148007936 | bytes 25166336 | tf_op jit(solution)/shard_map/while/body/eval_jaxpr/kgts,skd->tkgd/dot_general | solution.py:39
  342.0 15.2 %convert_reduce_fusion.4 = (f32[8,2,256]{2,1,0:T(2,128)S(1)}, bf16[8,2,256,2048]{2,3,1,0:T(8,128)(2,1)}) fusion(bf16[256,8,2,128]{3,0,2,1:T(8,128)(2,1)} %get-tuple-element.415, bf16[2,2048,8,128]{3,1,2,0:T(8,128)(2,1)} %get-tuple-element.414, s32[]{:T(128)} %get-tuple-element.401, pred[256,2048]{0,1:T(8,128)(4,1)S(1)} %dynamic-slice_bitcast_fusion.4), kind=kOutput, calls=%fused_computation.2.clone.1 | convolution fusion | flops 2197811200 | bytes 22561280 | tf_op jit(solution)/shard_map/while/body/eval_jaxpr/tkgd,skd->kgts/dot_general | solution.py:34
  357.2 10.0 %bitcast_add_fusion.5 = f32[256,8,2,128]{0,3,2,1:T(8,128)S(1)} fusion(f32[256,8,2,128]{0,3,2,1:T(8,128)S(1)} %get-tuple-element.402, bf16[8,2,256,2048]{2,3,1,0:T(8,128)(2,1)} %get-tuple-element.353, bf16[2,2048,8,128]{1,3,2,0:T(8,128)(2,1)} %get-tuple-element.412, s32[]{:T(128)} %get-tuple-element.401), kind=kOutput, calls=%fused_computation.8.clone.1 | convolution fusion | flops 2148007936 | bytes 25166336 | tf_op jit(solution)/shard_map/while/body/eval_jaxpr/kgts,skd->tkgd/dot_general | solution.py:39
  367.5 1.1 copy.44
  368.6 0.8 reshape.208
  369.5 12.7 %convolution_convert_fusion = bf16[256,4608]{1,0:T(8,128)(2,1)} fusion(bf16[256,2048]{1,0:T(8,128)(2,1)S(1)} %bitcast.107, bf16[2048,4608]{1,0:T(8,128)(2,1)} %bitcast.108), kind=kOutput, calls=%fused_computation.24 | convolution fusion | flops 4833017856 | bytes 22282240 | tf_op jit(solution)/shard_map/dot_general | solution.py:132
  382.2 33.1 %reduce-scatter.2.cloned.1.call-done = bf16[128,4608]{1,0:T(8,128)(2,1)} async-done(((bf16[256,4608]{1,0:T(8,128)(2,1)}), bf16[128,4608]{1,0:T(8,128)(2,1)}) %reduce-scatter.2.cloned.1.call-update) | async-done | bytes 1179664 | tf_op jit(solution)/shard_map/reduce_scatter | solution.py:131
  415.3 1.6 multiply_reduce_fusion
  417.0 2.8 add_convert_fusion
  (55 shorter events, 2.2 us)
Async XLA Ops:
  6.5 5.7 %copy-start.5 = (s32[2,16]{1,0:T(2,128)S(1)}, s32[2,16]{1,0:T(2,128)}, u32[]{:S(2)}) copy-start(s32[2,16]{1,0:T(2,128)} %param.19) | copy-start | bytes 388
  6.5 6.2 %copy-start.6 = (s32[2]{0:T(128)S(1)}, s32[2]{0:T(128)}, u32[]{:S(2)}) copy-start(s32[2]{0:T(128)} %param.20) | copy-start | bytes 28
  6.5 80.6 %all-gather.7.cloned.1.call-start = ((), (), s32[]{:S(2)}) async-start(), calls=%async_computation.2 | async-start | bytes 8912896 | tf_op jit(solution)/shard_map/all_gather | solution.py:84
  7.3 155.3 %all-gather.5.cloned.1.call-start = ((), (), s32[]{:S(2)}) async-start(), calls=%async_computation.1 | async-start | bytes 8912896 | tf_op jit(solution)/shard_map/all_gather | solution.py:85
  8.0 229.9 %all-gather.11.cloned.1.call-start = ((), (), s32[]{:S(2)}) async-start(), calls=%async_computation.4 | async-start | bytes 8912896 | tf_op jit(solution)/shard_map/all_gather | solution.py:103
  10.0 306.3 %all-gather.9.cloned.1.call-start = ((), (), s32[]{:S(2)}) async-start(), calls=%async_computation.3 | async-start | bytes 8912896 | tf_op jit(solution)/shard_map/all_gather | solution.py:104
  12.2 403.1 %reduce-scatter.2.cloned.1.call-start = ((), (), s32[]{:S(2)}) async-start(), calls=%async_computation.5 | async-start | bytes 3538944 | tf_op jit(solution)/shard_map/reduce_scatter | solution.py:131
  162.5 153.8 %copy-start = (pred[2,256,2048]{1,2,0:T(8,128)(4,1)S(1)}, pred[2,256,2048]{1,2,0:T(8,128)(4,1)}, u32[]{:S(2)}) copy-start(pred[2,256,2048]{1,2,0:T(8,128)(4,1)} %bitcast_and_fusion) | copy-start | bytes 3145732
  162.5 5.3 %copy-start.1 = (pred[2,256,2048]{1,2,0:T(8,128)(4,1)S(1)}, pred[2,256,2048]{1,2,0:T(8,128)(4,1)}, u32[]{:S(2)}) copy-start(pred[2,256,2048]{1,2,0:T(8,128)(4,1)} %get-tuple-element.388) | copy-start | bytes 3145732 | tf_op jit(solution)/shard_map/while
  162.5 5.4 %copy-start.3 = (bf16[256,8,2,128]{3,0,2,1:T(8,128)(2,1)S(1)}, bf16[256,8,2,128]{3,0,2,1:T(8,128)(2,1)}, u32[]{:S(2)}) copy-start(bf16[256,8,2,128]{3,0,2,1:T(8,128)(2,1)} %get-tuple-element.390) | copy-start | bytes 3145732 | tf_op jit(solution)/shard_map/while
  197.4 5.3 %copy-start.1 = (pred[2,256,2048]{1,2,0:T(8,128)(4,1)S(1)}, pred[2,256,2048]{1,2,0:T(8,128)(4,1)}, u32[]{:S(2)}) copy-start(pred[2,256,2048]{1,2,0:T(8,128)(4,1)} %get-tuple-element.388) | copy-start | bytes 3145732 | tf_op jit(solution)/shard_map/while
  197.5 5.5 %copy-start.3 = (bf16[256,8,2,128]{3,0,2,1:T(8,128)(2,1)S(1)}, bf16[256,8,2,128]{3,0,2,1:T(8,128)(2,1)}, u32[]{:S(2)}) copy-start(bf16[256,8,2,128]{3,0,2,1:T(8,128)(2,1)} %get-tuple-element.390) | copy-start | bytes 3145732 | tf_op jit(solution)/shard_map/while
  369.5 47.4 %copy-start.4 = (f32[4608]{0:T(1024)S(1)}, f32[4608]{0:T(1024)}, u32[]{:S(2)}) copy-start(f32[4608]{0:T(1024)} %param.23) | copy-start | bytes 55300
  382.2 34.8 %copy-start.2 = (bf16[2,64,4608]{2,1,0:T(8,128)(2,1)S(1)}, bf16[2,64,4608]{2,1,0:T(8,128)(2,1)}, u32[]{:S(2)}) copy-start(bf16[2,64,4608]{2,1,0:T(8,128)(2,1)} %param.22) | copy-start | bytes 3538948
Sparse Core Ops, SparseCore 0:
  9.5 77.6 all-gather.6
  89.3 73.1 all-gather.4
  164.7 73.1 all-gather.10
  239.9 76.3 all-gather.8
  382.4 32.8 reduce-scatter.1
where the time goes:
time: 427 us; the launch traced here: 426 us
  waiting for transfers between devices  260 us (61%)
  matrix products  109 us (26%)
  local copies, waits for them, and re-layouts  36.4 us (9%)
  between operations  13.3 us (3%)
  other arithmetic  7.9 us (2%)
    all_gather x1, waiting for transfers between devices, shards(): lax.all_gather(new_values, 'blk', axis=1, tiled=True)  78.4 us
    all_gather x1, waiting for transfers between devices, shards(): lax.all_gather(pool_values, 'blk', axis=0, tiled=True)  75.3 us
    all_gather x1, waiting for transfers between devices, shards(): lax.all_gather(pool_keys, 'blk', axis=0, tiled=True)  66.1 us
    dot_general x4, matrix products, compute(): jnp.einsum('tkgd,skd->kgts', grouped, key_block, preferred_element_type=j...  56.3 us
    dot_general x4, matrix products, compute(): jnp.einsum('kgts,skd->tkgd', weights, value_block, preferred_element_type...  39.7 us
    reduce_scatter x1, waiting for transfers between devices, shards(): lax.psum_scatter(jnp.dot(attended, weight_rows, preferred_element_type=jn...  33.1 us
    dynamic_slice x4, local copies, waits for them, and re-layouts, attend_pages(): lax.scan(one_group, running, (key_groups, value_groups, valid_groups))  23.9 us
    dot_general x1, matrix products, shards(): jnp.dot(attended, weight_rows, preferred_element_type=jnp.float32)  12.7 us
  transfers between devices with their start and end apart: 5, of which 5 were waited for; matrix products, arithmetic and copies ran while one was open for 19% of the time, Pallas kernels for 0%

commit v1 on v0

--- a/solution.py
+++ b/solution.py
@@ -1,11 +1,203 @@
 import jax
 import jax.numpy as jnp
 from jax import lax
+from jax.experimental import pallas as pl
+from jax.experimental.pallas import tpu as pltpu
 from jax.sharding import PartitionSpec as P
 
 soft_cap = 50.0
 score_scale = 144.0 ** (-0.5)
 norm_eps = 1e-06
+log2_e = 1.4426950408889634
+key_chunk = 512
+
+
+def split_heads(source, heads, staged):
+    rows = source.shape[0]
+    count = source.shape[1]
+    staged[0 : rows * count, :] = source[...].reshape(rows * count, source.shape[2]).astype(jnp.float32)
+    for head in heads:
+        yield staged[pl.ds(head, rows, stride=count), :].astype(jnp.bfloat16)
+
+
+def pack_message_kernel(pool_k, pool_v, new_k, new_v, out, staged):
+    step = pl.program_id(0)
+    kv_heads = pool_k.shape[2]
+    for head, rows in enumerate(split_heads(pool_k[0], range(kv_heads), staged)):
+        out[head, 0, step] = rows
+    for head, rows in enumerate(split_heads(pool_v[0], range(kv_heads), staged)):
+        out[head, 1, step] = rows
+    for head, rows in enumerate(split_heads(new_k[0], range(kv_heads), staged)):
+        out[head, step, 2] = rows
+    for head, rows in enumerate(split_heads(new_v[0], range(kv_heads), staged)):
+        out[head, step, 3] = rows
+
+
+def pack_message(pool_keys, pool_values, new_keys, new_values):
+    steps, rows, kv_heads, head_dim = pool_keys.shape
+    source = pl.BlockSpec((1, rows, kv_heads, head_dim), lambda i: (i, 0, 0, 0))
+    return pl.pallas_call(
+        pack_message_kernel,
+        grid=(steps,),
+        in_specs=[source] * 4,
+        out_specs=pl.BlockSpec((kv_heads, 2, 4, rows, head_dim), lambda i: (0, 0, 0, 0, 0)),
+        out_shape=jax.ShapeDtypeStruct((kv_heads, 2, 4, rows, head_dim), jnp.bfloat16),
+        scratch_shapes=[pltpu.VMEM((rows * kv_heads, head_dim), jnp.float32)],
+        compiler_params=pltpu.CompilerParams(vmem_limit_bytes=24 * 1024 * 1024),
+        cost_estimate=pl.CostEstimate(flops=0, bytes_accessed=4 * 1024 * 1024, transcendentals=0),
+        name="pack_message",
+    )(pool_keys, pool_values, new_keys, new_values)
+
+
+def pack_queries_kernel(queries, out, staged):
+    group = out.shape[2]
+    for head, rows in enumerate(split_heads(queries[0], range(queries.shape[2]), staged)):
+        out[head // group, 0, head % group] = rows
+
+
+def pack_queries(queries, kv_heads):
+    steps, rows, heads, head_dim = queries.shape
+    group = heads // kv_heads
+    return pl.pallas_call(
+        pack_queries_kernel,
+        grid=(steps,),
+        in_specs=[pl.BlockSpec((1, rows, heads, head_dim), lambda i: (i, 0, 0, 0))],
+        out_specs=pl.BlockSpec((kv_heads, 1, group, rows, head_dim), lambda i: (0, i, 0, 0, 0)),
+        out_shape=jax.ShapeDtypeStruct((kv_heads, steps, group, rows, head_dim), jnp.bfloat16),
+        scratch_shapes=[pltpu.VMEM((rows * heads, head_dim), jnp.float32)],
+        compiler_params=pltpu.CompilerParams(vmem_limit_bytes=24 * 1024 * 1024),
+        cost_estimate=pl.CostEstimate(flops=0, bytes_accessed=2 * 1024 * 1024, transcendentals=0),
+        name="pack_queries",
+    )(queries)
+
+
+def attend_kernel(core_ref, pages_ref, len_ref, message, other, queries, out, cache_k, cache_v, new_v):
+    blocks, _, rows, head_dim = message.shape
+    group = queries.shape[1]
+    slots = pages_ref.shape[1]
+    core = core_ref[0]
+    cached = len_ref[core]
+    for slot in range(slots):
+        page = pages_ref[core, slot]
+        mine = message[page // 2, page % 2]
+        theirs = other[page // 2, page % 2]
+        seen = slot * rows + lax.broadcasted_iota(jnp.int32, (rows, head_dim), 0) < cached
+        here = pl.ds(slot * rows, rows)
+        keys = jnp.where(core == 0, mine, theirs)
+        values = jnp.where(core == 0, theirs, mine).astype(jnp.float32)
+        cache_k[here, :] = keys
+        cache_v[here, 0:head_dim] = jnp.where(seen, values, 0.0).astype(jnp.bfloat16)
+        cache_v[here, head_dim : 2 * head_dim] = jnp.where(seen, 1.0, 0.0).astype(jnp.bfloat16)
+    for block in range(blocks):
+        here = pl.ds(block * rows, rows)
+        new_v[here, 0:head_dim] = message[block, 3]
+    new_v[:, head_dim : 2 * head_dim] = jnp.ones((blocks * rows, head_dim), jnp.bfloat16)
+
+    chunk = min(key_chunk, blocks * rows)
+    chunk_blocks = chunk // rows
+
+    def weights_of(query, keys):
+        scores = lax.dot_general(query, keys, (((1,), (1,)), ((), ())), preferred_element_type=jnp.float32)
+        return jnp.exp2((soft_cap * log2_e) * jnp.tanh(scores * (score_scale / soft_cap)))
+
+    def new_keys_of(part):
+        return message[pl.ds(part * chunk_blocks, chunk_blocks), 2].reshape(chunk, head_dim)
+
+    @pl.loop(0, blocks)
+    def _(block):
+        query = queries[block].reshape(group * rows, head_dim)
+        total = jnp.zeros((group * rows, 2 * head_dim), jnp.float32)
+        for part in range(slots * rows // chunk):
+            here = pl.ds(part * chunk, chunk)
+            weights = weights_of(query, cache_k[here, :]).astype(jnp.bfloat16)
+            total += jnp.dot(weights, cache_v[here, :], preferred_element_type=jnp.float32)
+
+        def full(part, total):
+            weights = weights_of(query, new_keys_of(part)).astype(jnp.bfloat16)
+            here = pl.ds(pl.multiple_of(part * chunk, chunk), chunk)
+            return total + jnp.dot(weights, new_v[here, :], preferred_element_type=jnp.float32)
+
+        last = block // chunk_blocks
+        total = lax.fori_loop(0, last, full, total)
+        key_at = last * chunk + lax.broadcasted_iota(jnp.int32, (rows, chunk), 1)
+        query_at = block * rows + lax.broadcasted_iota(jnp.int32, (rows, chunk), 0)
+        seen = jnp.concatenate([key_at <= query_at] * group, axis=0)
+        weights = jnp.where(seen, weights_of(query, new_keys_of(last)), 0.0).astype(jnp.bfloat16)
+        here = pl.ds(pl.multiple_of(last * chunk, chunk), chunk)
+        total += jnp.dot(weights, new_v[here, :], preferred_element_type=jnp.float32)
+        attended = (total[:, 0:head_dim] / total[:, head_dim : 2 * head_dim]).astype(jnp.bfloat16)
+        for head in range(group):
+            out[block, :, head * head_dim : (head + 1) * head_dim] = attended[head * rows : (head + 1) * rows, :]
+
+
+def attend(core, page_table, cache_len, message, other, queries):
+    blocks, _, rows, head_dim = message.shape
+    group = queries.shape[1]
+    slots = page_table.shape[1]
+    in_smem = pl.BlockSpec(memory_space=pltpu.SMEM)
+    in_vmem = pl.BlockSpec(memory_space=pltpu.VMEM)
+    seen = blocks * rows * (slots * rows + blocks * rows // 2) * group
+    return pl.pallas_call(
+        attend_kernel,
+        in_specs=[in_smem] * 3 + [in_vmem] * 3,
+        out_specs=in_vmem,
+        out_shape=jax.ShapeDtypeStruct((blocks, rows, group * head_dim), jnp.bfloat16),
+        scratch_shapes=[
+            pltpu.VMEM((slots * rows, head_dim), jnp.bfloat16),
+            pltpu.VMEM((slots * rows, 2 * head_dim), jnp.bfloat16),
+            pltpu.VMEM((blocks * rows, 2 * head_dim), jnp.bfloat16),
+        ],
+        compiler_params=pltpu.CompilerParams(vmem_limit_bytes=32 * 1024 * 1024),
+        cost_estimate=pl.CostEstimate(
+            flops=4 * seen * head_dim, bytes_accessed=message.size * 4 + queries.size * 4, transcendentals=2 * seen
+        ),
+        name="attend",
+    )(core, page_table, cache_len, message, other, queries)
+
+
+def by_heads(
+    queries,
+    new_keys,
+    new_values,
+    pool_keys,
+    pool_values,
+    page_table,
+    cache_len,
+    out_weight,
+    residual,
+    post_gain,
+):
+    req_count, per_req, heads_here, head_dim = queries.shape
+    kv_here = new_keys.shape[2]
+    blk_count = lax.axis_size("blk")
+    group = heads_here // kv_here
+    core = lax.axis_index("blk") % 2
+    message = pack_message(pool_keys, pool_values, new_keys, new_values)
+    message = message.reshape(blk_count, 4, per_req, head_dim)
+    message = lax.all_to_all(message, "blk", 0, 0, tiled=True)
+    packed = pack_queries(queries, kv_here).reshape(blk_count, group, per_req, head_dim)
+    packed = lax.all_to_all(packed, "blk", 0, 0, tiled=True)
+    other = lax.ppermute(message[:, 0:2], "blk", [(i, i ^ 1) for i in range(blk_count)])
+    attended = attend(core[None], page_table, cache_len, message, other, packed)
+    attended = lax.all_to_all(attended, "blk", 0, 0, tiled=True)
+    attended = attended.reshape(kv_here, req_count, per_req, group * head_dim)
+    head_count = lax.axis_size("head")
+    share = per_req // head_count
+    attended = attended.reshape(kv_here, req_count, head_count, share, group * head_dim)
+    weight = out_weight.reshape(kv_here, group * head_dim, out_weight.shape[2])
+
+    def project(rows):
+        rows = rows.transpose(1, 2, 0, 3).reshape(req_count * share, kv_here * group * head_dim)
+        return jnp.dot(rows, weight.reshape(-1, weight.shape[2]), preferred_element_type=jnp.float32)
+
+    mine = lax.axis_index("head")
+    theirs = project(lax.dynamic_index_in_dim(attended, 1 - mine, 2, keepdims=False)).astype(jnp.bfloat16)
+    arrived = lax.ppermute(theirs, "head", [(0, 1), (1, 0)])
+    own = project(lax.dynamic_index_in_dim(attended, mine, 2, keepdims=False))
+    projected = (own + arrived.astype(jnp.float32)).reshape(req_count, share, -1)
+    inv_rms = lax.rsqrt(jnp.mean(projected * projected, axis=-1, keepdims=True) + norm_eps)
+    mixed_out = residual.astype(jnp.float32) + post_gain * projected * inv_rms
+    return mixed_out.astype(jnp.bfloat16)
 
 
 def group_pages(page_count, page_len):
@@ -153,8 +345,13 @@
         P(None, ("blk", "head"), None),
         P(),
     )
+    def one_device(queries, new_keys, *rest):
+        owners = mesh.shape["blk"] == 2 * new_keys.shape[2] and mesh.shape["head"] == 2
+        fits = queries.shape[0] == 2 and rest[1].shape[0] == 2 and rest[1].shape[1] == queries.shape[1]
+        return (by_heads if owners and fits else shards)(queries, new_keys, *rest)
+
     return jax.shard_map(
-        shards,
+        one_device,
         mesh=mesh,
         in_specs=placed,
         out_specs=P(None, ("blk", "head"), None),

time: 427 us -> 204 us (0.48)
  waiting for transfers between devices: 260 us -> 110 us
  matrix products: 109 us -> 17 us
  Pallas kernels: 0 us -> 38.6 us
  local copies, waits for them, and re-layouts: 36.4 us -> 7.17 us
  starting transfers between devices: 0.16 us -> 27.6 us
  between operations: 13.3 us -> 0.12 us
  other arithmetic: 7.9 us -> 2.15 us
    all_gather x4 -> x0, waiting for transfers between devices: 225 us -> none  [the longest x1 78.4 us: shards(): lax.all_gather(new_values, 'blk', axis=1, tiled=True)]
    dot_general x9 -> x2, matrix products: 109 us -> 17 us  [project(): jnp.dot(rows, weight.reshape(-1, weight.shape[2]), preferred_element_type...]
    all_to_all x0 -> x3, waiting for transfers between devices: none -> 83.9 us  [the longest x1 39.5 us: by_heads(): message = lax.all_to_all(message, 'blk', 0, 0, tiled=True)]
    pallas_call x0 -> x3, Pallas kernels: none -> 38.6 us  [the longest x1 34.7 us: attend(): pl.pallas_call(attend_kernel, in_specs=[in_smem] * 3 + [in_vmem] * 3, out...]
    reduce_scatter x1 -> x0, waiting for transfers between devices: 33.1 us -> none  [shards(): lax.psum_scatter(jnp.dot(attended, weight_rows, preferred_element_type=jn...]
    ppermute x0 -> x2, waiting for transfers between devices: none -> 26.6 us  [the longest x1 26.6 us: by_heads(): arrived = lax.ppermute(theirs, 'head', [(0, 1), (1, 0)])]
    all_to_all x0 -> x3, starting transfers between devices: none -> 25.6 us  [the longest x1 11.2 us: by_heads(): packed = lax.all_to_all(packed, 'blk', 0, 0, tiled=True)]
    dynamic_slice x4 -> x3, local copies, waits for them, and re-layouts: 23.9 us -> 0.69 us  [the longest x2 0.39 us: by_heads(): lax.dynamic_index_in_dim(attended, 1 - mine, 2, keepdims=False)]
  transfers between devices with their start and end apart: 5 -> 5, of which waited for: 5 -> 4; matrix products, arithmetic and copies ran while one was open for 19% -> 1% of each run, Pallas kernels for 0% -> 1%
where the time goes in v1:
time: 204 us; the launch traced here: 203 us
  waiting for transfers between devices  110 us (54%)
  Pallas kernels  38.6 us (19%)
  starting transfers between devices  27.6 us (14%)
  matrix products  17 us (8%)
  local copies, waits for them, and re-layouts  7.17 us (4%)
  other arithmetic  2.15 us (1%)
    all_to_all x1, waiting for transfers between devices, by_heads(): message = lax.all_to_all(message, 'blk', 0, 0, tiled=True)  39.5 us
    pallas_call x1, Pallas kernels, attend(): pl.pallas_call(attend_kernel, in_specs=[in_smem] * 3 + [in_vmem] * 3, out...  34.7 us
    ppermute x1, waiting for transfers between devices, by_heads(): arrived = lax.ppermute(theirs, 'head', [(0, 1), (1, 0)])  26.6 us
    all_to_all x1, waiting for transfers between devices, by_heads(): attended = lax.all_to_all(attended, 'blk', 0, 0, tiled=True)  22.9 us
    all_to_all x1, waiting for transfers between devices, by_heads(): packed = lax.all_to_all(packed, 'blk', 0, 0, tiled=True)  21.5 us
    dot_general x2, matrix products, project(): jnp.dot(rows, weight.reshape(-1, weight.shape[2]), preferred_element_type...  17 us
    all_to_all x1, starting transfers between devices, by_heads(): packed = lax.all_to_all(packed, 'blk', 0, 0, tiled=True)  11.2 us
    all_to_all x1, starting transfers between devices, by_heads(): message = lax.all_to_all(message, 'blk', 0, 0, tiled=True)  7.49 us
  transfers between devices with their start and end apart: 5, of which 4 were waited for; matrix products, arithmetic and copies ran while one was open for 1% of the time, Pallas kernels for 1%

profile of v1, /device:TPU:0, one launch (start us, length us, event | category | flops | bytes accessed | tf_op | source)
XLA Modules:
  0.0 203.0 jit_solution(18201931438366614503)
XLA Ops:
  0.0 1.0 copy-done.2
  1.0 1.0 copy-done.3
  2.1 1.0 copy-done.4
  3.1 1.0 copy-done.5
  4.2 2.3 %pack_message.1 = bf16[8,2,4,128,128]{4,3,2,1,0:T(8,128)(2,1)} custom-call(bf16[2,128,8,128]{3,2,1,0:T(8,128)(2,1)S(1)} %copy-done.2, bf16[2,128,8,128]{3,2,1,0:T(8,128)(2,1)S(1)} %copy-done.3, bf16[2,128,8,128]{3,2,1,0:T(8,128)(2,1)S(1)} %copy-done.4, bf16[2,128,8,128]{3,2,1,0:T(8,128)(2,1)S(1)} %copy-done.5), custom_call_target="tpu_custom_call" | custom-call | bytes 4194304 | tf_op jit(solution)/shard_map/pack_message/pallas_call | solution.py:39
  6.4 7.5 %all-to-all-start = ((bf16[16,4,128,128]{3,2,1,0:T(8,128)(2,1)}), bf16[16,4,128,128]{3,2,1,0:T(8,128)(2,1)S(1)}, u32[]{:S(2)}, u32[]{:S(2)}) async-start(bf16[16,4,128,128]{3,2,1,0:T(8,128)(2,1)} %bitcast.1), calls=%async_computation | async-start | bytes 4194304 | tf_op jit(solution)/shard_map/all_to_all | solution.py:177
  13.9 0.0 copy-done
  13.9 1.6 pack_queries.1
  15.6 39.5 %all-to-all-done.message = bf16[16,4,128,128]{3,2,1,0:T(8,128)(2,1)S(1)} async-done(((bf16[16,4,128,128]{3,2,1,0:T(8,128)(2,1)}), bf16[16,4,128,128]{3,2,1,0:T(8,128)(2,1)S(1)}, u32[]{:S(2)}, u32[]{:S(2)}) %all-to-all-start) | async-done | bytes 2097184 | tf_op jit(solution)/shard_map/all_to_all | solution.py:177
  55.0 11.2 %all-to-all-start.1 = ((bf16[16,2,128,128]{3,2,1,0:T(8,128)(2,1)}), bf16[16,2,128,128]{3,2,1,0:T(8,128)(2,1)S(1)}, u32[]{:S(2)}, u32[]{:S(2)}) async-start(bf16[16,2,128,128]{3,2,1,0:T(8,128)(2,1)} %bitcast.2), calls=%async_computation.1 | async-start | bytes 2097152 | tf_op jit(solution)/shard_map/all_to_all | solution.py:179
  66.3 1.0 slice.4
  67.3 0.4 collective-permute-start
  67.7 21.5 %all-to-all-done.1.queries = bf16[16,2,128,128]{3,2,1,0:T(8,128)(2,1)S(1)} async-done(((bf16[16,2,128,128]{3,2,1,0:T(8,128)(2,1)}), bf16[16,2,128,128]{3,2,1,0:T(8,128)(2,1)S(1)}, u32[]{:S(2)}, u32[]{:S(2)}) %all-to-all-start.1) | async-done | bytes 1048608 | tf_op jit(solution)/shard_map/all_to_all | solution.py:179
  89.2 0.0 collective-permute-done.other
  89.2 0.0 copy-done.6
  89.2 0.0 copy-done.7
  89.2 34.7 %attend.1 = bf16[16,128,256]{2,1,0:T(8,128)(2,1)S(1)} custom-call(s32[1]{0:T(128)} %bitcast.core_ref, s32[2,16]{1,0:T(2,128)S(1)} %copy-done.6, s32[2]{0:T(128)S(1)} %copy-done.7, bf16[16,4,128,128]{3,2,1,0:T(8,128)(2,1)S(1)} %all-to-all-done.message, bf16[16,2,128,128]{3,2,1,0:T(8,128)(2,1)} %collective-permute-done.other, ...), custom_call_target="tpu_custom_call" | custom-call | flops 6442450944 | bytes 6291456 | tf_op jit(solution)/shard_map/attend/pallas_call | solution.py:140
  123.9 0.0 copy-start.1
  123.9 1.0 copy-done.1
  124.9 6.9 %all-to-all-start.2 = ((bf16[16,128,256]{2,1,0:T(8,128)(2,1)}), bf16[16,128,256]{2,1,0:T(8,128)(2,1)S(1)}, u32[]{:S(2)}, u32[]{:S(2)}) async-start(bf16[16,128,256]{2,1,0:T(8,128)(2,1)} %copy-done.1), calls=%async_computation.2 | async-start | bytes 2097152 | tf_op jit(solution)/shard_map/all_to_all | solution.py:182
  131.7 22.9 %all-to-all-done.2 = bf16[16,128,256]{2,1,0:T(8,128)(2,1)S(1)} async-done(((bf16[16,128,256]{2,1,0:T(8,128)(2,1)}), bf16[16,128,256]{2,1,0:T(8,128)(2,1)S(1)}, u32[]{:S(2)}, u32[]{:S(2)}) %all-to-all-start.2) | async-done | bytes 1048608 | tf_op jit(solution)/shard_map/all_to_all | solution.py:182
  154.7 0.1 constant_dynamic-slice_fusion
  154.8 0.3 copy.12
  155.1 0.1 copy.14
  155.2 9.0 %convolution_convert_fusion = bf16[128,4608]{1,0:T(8,128)(2,1)S(1)} fusion(bf16[128,2048]{1,0:T(8,128)(2,1)S(1)} %bitcast.26, bf16[2048,4608]{1,0:T(8,128)(2,1)} %bitcast.22), kind=kOutput, calls=%fused_computation | convolution fusion | flops 2416508928 | bytes 20578304 | tf_op jit(solution)/shard_map/dot_general | solution.py:191
  164.2 1.6 collective-permute-start.1
  165.8 0.3 copy.11
  166.1 0.1 copy.13
  166.2 26.6 %collective-permute-done.1 = bf16[128,4608]{1,0:T(8,128)(2,1)S(1)} collective-permute-done((bf16[128,4608]{1,0:T(8,128)(2,1)S(1)}, bf16[128,4608]{1,0:T(8,128)(2,1)S(1)}, u32[]{:S(2)}, u32[]{:S(2)}) %collective-permute-start.1) | collective-permute-done | bytes 1179680 | tf_op jit(solution)/shard_map/ppermute | solution.py:195
  192.8 8.0 %multiply_reduce_fusion = (f32[128]{0:T(128)S(1)}, f32[128,4608]{1,0:T(8,128)S(1)}) fusion(bf16[128,4608]{1,0:T(8,128)(2,1)S(1)} %collective-permute-done.1, bf16[128,2048]{1,0:T(8,128)(2,1)S(1)} %bitcast.27, bf16[2048,4608]{1,0:T(8,128)(2,1)} %bitcast.23), kind=kOutput, calls=%fused_computation.2 | convolution fusion | flops 2418278400 | bytes 22938112 | tf_op jit(solution)/shard_map/dot_general | solution.py:191
  200.8 0.1 rsqrt.12
  200.9 2.1 %add_convert_fusion = bf16[2,64,4608]{2,1,0:T(8,128)(2,1)} fusion(f32[2,64,4608]{2,1,0:T(8,128)S(1)} %bitcast.24, bf16[2,64,4608]{2,1,0:T(8,128)(2,1)S(1)} %copy-done.8, f32[2,64]{1,0:T(2,128)S(1)} %rsqrt.12, f32[4608]{0:T(1024)} %param.19), kind=kLoop, calls=%fused_computation.1 | loop fusion | flops 2949120 | bytes 4737536 | tf_op jit(solution)/shard_map/convert_element_type | solution.py:200
  (10 shorter events, 0.0 us)
Async XLA Ops:
  0.0 1.0 copy-start.2
  1.0 1.0 copy-start.3
  2.1 1.0 copy-start.4
  3.1 1.0 copy-start.5
  6.4 7.5 %copy-start = (bf16[2,128,16,128]{3,2,1,0:T(8,128)(2,1)S(1)}, bf16[2,128,16,128]{3,2,1,0:T(8,128)(2,1)}, u32[]{:S(2)}) copy-start(bf16[2,128,16,128]{3,2,1,0:T(8,128)(2,1)} %queries.1) | copy-start | bytes 3145732
  6.4 48.6 %all-to-all-start = ((bf16[16,4,128,128]{3,2,1,0:T(8,128)(2,1)}), bf16[16,4,128,128]{3,2,1,0:T(8,128)(2,1)S(1)}, u32[]{:S(2)}, u32[]{:S(2)}) async-start(bf16[16,4,128,128]{3,2,1,0:T(8,128)(2,1)} %bitcast.1), calls=%async_computation | async-start | bytes 4194304 | tf_op jit(solution)/shard_map/all_to_all | solution.py:177
  15.6 73.6 %copy-start.6 = (s32[2,16]{1,0:T(2,128)S(1)}, s32[2,16]{1,0:T(2,128)}, u32[]{:S(2)}) copy-start(s32[2,16]{1,0:T(2,128)} %pages_ref.1) | copy-start | bytes 388
  15.6 73.6 %copy-start.7 = (s32[2]{0:T(128)S(1)}, s32[2]{0:T(128)}, u32[]{:S(2)}) copy-start(s32[2]{0:T(128)} %len_ref.1) | copy-start | bytes 28
  55.0 34.2 %all-to-all-start.1 = ((bf16[16,2,128,128]{3,2,1,0:T(8,128)(2,1)}), bf16[16,2,128,128]{3,2,1,0:T(8,128)(2,1)S(1)}, u32[]{:S(2)}, u32[]{:S(2)}) async-start(bf16[16,2,128,128]{3,2,1,0:T(8,128)(2,1)} %bitcast.2), calls=%async_computation.1 | async-start | bytes 2097152 | tf_op jit(solution)/shard_map/all_to_all | solution.py:179
  67.3 21.9 %collective-permute-start = (bf16[16,2,128,128]{3,2,1,0:T(8,128)(2,1)}, bf16[16,2,128,128]{3,2,1,0:T(8,128)(2,1)}, u32[]{:S(2)}, u32[]{:S(2)}) collective-permute-start(bf16[16,2,128,128]{3,2,1,0:T(8,128)(2,1)} %slice.4), channel_id=1, source_target_pairs={{0,2},{2,0},{4,6},{6,4},{8,10},{10,8},{12,14},{14,12},{16,18},{18,... | collective-permute-start | bytes 3145736 | tf_op jit(solution)/shard_map/ppermute | solution.py:180
  123.9 1.0 copy-start.1
  124.9 29.8 %all-to-all-start.2 = ((bf16[16,128,256]{2,1,0:T(8,128)(2,1)}), bf16[16,128,256]{2,1,0:T(8,128)(2,1)S(1)}, u32[]{:S(2)}, u32[]{:S(2)}) async-start(bf16[16,128,256]{2,1,0:T(8,128)(2,1)} %copy-done.1), calls=%async_computation.2 | async-start | bytes 2097152 | tf_op jit(solution)/shard_map/all_to_all | solution.py:182
  164.2 28.5 %collective-permute-start.1 = (bf16[128,4608]{1,0:T(8,128)(2,1)S(1)}, bf16[128,4608]{1,0:T(8,128)(2,1)S(1)}, u32[]{:S(2)}, u32[]{:S(2)}) collective-permute-start(bf16[128,4608]{1,0:T(8,128)(2,1)S(1)} %convolution_convert_fusion), channel_id=1, source_target_pairs={{0,1},{1,0},{2,3},{3,2},{4,5},{5,4},{6,7},{7,6},{8,9},{9,8},{10,11... | collective-permute-start | bytes 3538952 | tf_op jit(solution)/shard_map/ppermute | solution.py:195
  192.8 8.1 %copy-start.8 = (bf16[2,64,4608]{2,1,0:T(8,128)(2,1)S(1)}, bf16[2,64,4608]{2,1,0:T(8,128)(2,1)}, u32[]{:S(2)}) copy-start(bf16[2,64,4608]{2,1,0:T(8,128)(2,1)} %param.18) | copy-start | bytes 3538948

commit v2 on v0

--- a/solution.py
+++ b/solution.py
@@ -1,11 +1,294 @@
+import functools
+
 import jax
 import jax.numpy as jnp
 from jax import lax
+from jax.experimental import pallas as pl
+from jax.experimental.pallas import tpu as pltpu
 from jax.sharding import PartitionSpec as P
 
 soft_cap = 50.0
 score_scale = 144.0 ** (-0.5)
 norm_eps = 1e-06
+log2_e = 1.4426950408889634
+chunks = 2
+key_tile = 256
+mib = 1024 * 1024
+in_vmem = pl.BlockSpec(memory_space=pltpu.VMEM)
+in_smem = pl.BlockSpec(memory_space=pltpu.SMEM)
+
+
+def kernel_params(limit_mib):
+    return pltpu.CompilerParams(vmem_limit_bytes=limit_mib * mib)
+
+
+def split_heads(source, staged):
+    rows, heads, head_dim = source.shape
+    staged[0 : rows * heads, :] = source.reshape(rows * heads, head_dim).astype(jnp.float32)
+    for head in range(heads):
+        yield head, staged[pl.ds(head, rows, stride=heads), :].astype(jnp.bfloat16)
+
+
+def put_queries(queries, out, part, staged):
+    _, shares, _, rows, heads, head_dim = queries.shape
+    group = heads // out.shape[0]
+    source = queries[...].reshape(shares * rows, heads, head_dim)
+    for head, picked in split_heads(source, staged):
+        first = head % group * shares * rows
+        out[head // group, 0, part, first : first + shares * rows, :] = picked
+
+
+def pack_first(pool_keys, pool_values, new_keys, new_values, queries):
+    steps, rows, kv_heads, head_dim = new_keys.shape
+    pages = pool_keys.shape[0]
+    parts = pages + 3
+
+    def kernel(pool_k, pool_v, new_k, new_v, some_queries, out, staged):
+        core = pl.program_id(0)
+
+        @pl.when(core == 0)
+        def _():
+            for page in range(pages):
+                for head, picked in split_heads(pool_k[page], staged):
+                    out[head, 0, page] = picked
+
+        @pl.when(core == 1)
+        def _():
+            for page in range(pages):
+                for head, picked in split_heads(pool_v[page], staged):
+                    out[head, 0, page] = picked
+
+        for head, picked in split_heads(new_k[0], staged):
+            out[head, 0, pages] = picked
+        for head, picked in split_heads(new_v[0], staged):
+            out[head, 0, pages + 1] = picked
+        put_queries(some_queries, out, pages + 2, staged)
+
+    whole = pl.BlockSpec((pages, rows, kv_heads, head_dim), lambda i: (0, 0, 0, 0))
+    one = pl.BlockSpec((1, rows, kv_heads, head_dim), lambda i: (i, 0, 0, 0))
+    _, shares, _, chunk_rows, heads, _ = queries.shape
+    some = pl.BlockSpec((1, shares, 1, chunk_rows, heads, head_dim), lambda i: (i, 0, 0, 0, 0, 0))
+    sources = [pltpu.with_memory_space_constraint(x, pltpu.HBM) for x in (pool_keys, pool_values, new_keys, new_values, queries)]
+    return pl.pallas_call(
+        kernel,
+        grid=(steps,),
+        in_specs=[whole, whole, one, one, some],
+        out_specs=pl.BlockSpec((kv_heads, 1, parts, rows, head_dim), lambda i: (0, i, 0, 0, 0)),
+        out_shape=jax.ShapeDtypeStruct((kv_heads, steps, parts, rows, head_dim), jnp.bfloat16),
+        scratch_shapes=[pltpu.VMEM((rows * kv_heads, head_dim), jnp.float32)],
+        compiler_params=kernel_params(24),
+        cost_estimate=pl.CostEstimate(flops=0, bytes_accessed=6 * mib, transcendentals=0),
+        name="pack_first",
+    )(*sources)
+
+
+def pack_queries(queries, kv_heads, chunk):
+    steps, shares, _, rows, heads, head_dim = queries.shape
+    group = heads // kv_heads
+
+    def kernel(some_queries, out, staged):
+        put_queries(some_queries, out, 0, staged)
+
+    return pl.pallas_call(
+        kernel,
+        grid=(steps,),
+        in_specs=[pl.BlockSpec((1, shares, 1, rows, heads, head_dim), lambda i: (i, 0, chunk, 0, 0, 0))],
+        out_specs=pl.BlockSpec((kv_heads, 1, 1, group * shares * rows, head_dim), lambda i: (0, i, 0, 0, 0)),
+        out_shape=jax.ShapeDtypeStruct((kv_heads, steps, 1, group * shares * rows, head_dim), jnp.bfloat16),
+        scratch_shapes=[pltpu.VMEM((shares * rows * heads, head_dim), jnp.float32)],
+        compiler_params=kernel_params(24),
+        cost_estimate=pl.CostEstimate(flops=0, bytes_accessed=mib, transcendentals=0),
+        name="pack_queries",
+    )(pltpu.with_memory_space_constraint(queries, pltpu.HBM))
+
+
+def attend_kernel(pages, chunk, shares, core_ref, table_ref, len_ref, message, other, *rest):
+    out, cache_k, cache_v, new_v, total = rest[-5:]
+    queries, query_part = (rest[0], 0) if len(rest) > 5 else (message, pages + 2)
+    blocks, _, page_rows, head_dim = message.shape
+    slots = table_ref.shape[1]
+    block_rows = queries.shape[2]
+    group = out.shape[2] // head_dim
+    core = core_ref[0]
+    cached = len_ref[core]
+    for slot in range(slots):
+        page = table_ref[core, slot]
+        mine = message[page // pages, page % pages]
+        theirs = other[page // pages, page % pages]
+        seen = slot * page_rows + lax.broadcasted_iota(jnp.int32, (page_rows, head_dim), 0) < cached
+        here = pl.ds(slot * page_rows, page_rows)
+        cache_k[here, :] = jnp.where(core == 0, mine, theirs)
+        values = jnp.where(core == 0, theirs, mine).astype(jnp.float32)
+        cache_v[here, 0:head_dim] = jnp.where(seen, values, 0.0).astype(jnp.bfloat16)
+        cache_v[here, head_dim : 2 * head_dim] = jnp.where(seen, 1.0, 0.0).astype(jnp.bfloat16)
+    for block in range(blocks):
+        new_v[block * page_rows : (block + 1) * page_rows, 0:head_dim] = message[block, pages + 1]
+    new_v[:, head_dim : 2 * head_dim] = jnp.ones((blocks * page_rows, head_dim), jnp.bfloat16)
+
+    def add(first_block, block_count, keys, values, begin=False, causal=False):
+        rows = block_count * block_rows
+        query = queries[first_block : first_block + block_count, query_part].reshape(rows, head_dim)
+        scores = lax.dot_general(query, keys, (((1,), (1,)), ((), ())), preferred_element_type=jnp.float32)
+        weights = jnp.exp2((soft_cap * log2_e) * jnp.tanh(scores * (score_scale / soft_cap)))
+        if causal:
+            row = lax.broadcasted_iota(jnp.int32, weights.shape, 0)
+            in_chunk = block_rows // (group * shares)
+            offset = row // block_rows * page_rows + row // in_chunk % shares * (page_rows // shares)
+            offset += chunk * in_chunk + row % in_chunk
+            weights = jnp.where(lax.broadcasted_iota(jnp.int32, weights.shape, 1) <= offset, weights, 0.0)
+        product = jnp.dot(weights.astype(jnp.bfloat16), values, preferred_element_type=jnp.float32)
+        here = pl.ds(first_block * block_rows, rows)
+        total[here, :] = product if begin else total[here, :] + product
+
+    half = blocks // 2
+    for first in (0, half):
+        for tile in range(0, slots * page_rows, key_tile):
+            add(first, half, cache_k[tile : tile + key_tile, :], cache_v[tile : tile + key_tile, :], begin=tile == 0)
+    tile_blocks = key_tile // page_rows
+    for block in range(0, blocks, tile_blocks):
+        keys = message[block : block + tile_blocks, pages].reshape(key_tile, head_dim)
+        values = new_v[block * page_rows : block * page_rows + key_tile, :]
+        add(block, tile_blocks, keys, values, causal=True)
+        later = block + tile_blocks
+        while later < blocks:
+            count = min(half, blocks - later)
+            add(later, count, keys, values)
+            later += count
+    per_head = block_rows // group
+    for block in range(blocks):
+        here = pl.ds(block * block_rows, block_rows)
+        attended = (total[here, 0:head_dim] / total[here, head_dim : 2 * head_dim]).astype(jnp.bfloat16)
+        for head in range(group):
+            out[block, :, head * head_dim : (head + 1) * head_dim] = attended[head * per_head : (head + 1) * per_head, :]
+
+
+def attend(core, page_table, cache_len, message, other, queries, chunk, pages, shares, group):
+    blocks, _, page_rows, head_dim = message.shape
+    slots = page_table.shape[1]
+    block_rows = page_rows * group // chunks
+    operands = [message, other] + ([] if queries is None else [queries])
+    seen = blocks * block_rows * (slots + blocks // 2) * page_rows
+    return pl.pallas_call(
+        functools.partial(attend_kernel, pages, chunk, shares),
+        in_specs=[in_smem] * 3 + [in_vmem] * len(operands),
+        out_specs=in_vmem,
+        out_shape=jax.ShapeDtypeStruct((blocks, block_rows // group, group * head_dim), jnp.bfloat16),
+        scratch_shapes=[
+            pltpu.VMEM((slots * page_rows, head_dim), jnp.bfloat16),
+            pltpu.VMEM((slots * page_rows, 2 * head_dim), jnp.bfloat16),
+            pltpu.VMEM((blocks * page_rows, 2 * head_dim), jnp.bfloat16),
+            pltpu.VMEM((blocks * block_rows, 2 * head_dim), jnp.float32),
+        ],
+        compiler_params=kernel_params(24),
+        cost_estimate=pl.CostEstimate(flops=8 * seen * head_dim, bytes_accessed=8 * mib, transcendentals=2 * seen),
+        name="attend",
+    )(core, page_table, cache_len, *operands)
+
+
+def project_kernel(shares, place_ref, attended, weight, own, theirs, rows):
+    place = place_ref[0]
+    sources, share_rows, features = attended.shape
+    requests = 2
+    count = share_rows // shares
+    for source in range(sources):
+        first = source // requests * features
+        for share in range(shares):
+            at = pl.multiple_of((share ^ place) * (requests * count), requests * count) + source % requests * count
+            rows[pl.ds(at, count), first : first + features] = attended[source, share * count : (share + 1) * count, :]
+    width = weight.shape[1]
+    tile = 512 if width % 512 == 0 else width
+    for first in range(0, width, tile):
+        product = jnp.dot(rows[...], weight[:, first : first + tile], preferred_element_type=jnp.float32)
+        own[:, first : first + tile] = product[0 : requests * count, :]
+        theirs[:, first : first + tile] = product[requests * count :, :].astype(jnp.bfloat16)
+
+
+def project(place, attended, weight, shares):
+    sources, share_rows, features = attended.shape
+    depth, width = weight.shape
+    rows = 2 * share_rows
+    return pl.pallas_call(
+        functools.partial(project_kernel, shares),
+        in_specs=[in_smem, in_vmem, in_vmem],
+        out_specs=[in_vmem, in_vmem],
+        out_shape=[
+            jax.ShapeDtypeStruct((rows // shares, width), jnp.float32),
+            jax.ShapeDtypeStruct((rows // shares, width), jnp.bfloat16),
+        ],
+        scratch_shapes=[pltpu.VMEM((rows, depth), jnp.bfloat16)],
+        compiler_params=kernel_params(16),
+        cost_estimate=pl.CostEstimate(flops=2 * rows * depth * width, bytes_accessed=2 * depth * width, transcendentals=0),
+        name="project",
+    )(place, attended, pltpu.with_memory_space_constraint(weight, pltpu.VMEM))
+
+
+def finish(own, arrived, residual, gain, chunk, earlier):
+    requests, per_req, width = residual.shape
+    rows = own.shape[0] // requests
+
+    def kernel(own_ref, arrived_ref, residual_ref, gain_ref, *rest):
+        out = rest[-1]
+        projected = own_ref[...] + arrived_ref[...].astype(jnp.float32)
+        inv_rms = lax.rsqrt(jnp.mean(projected * projected, axis=-1, keepdims=True) + norm_eps)
+        out[0] = (residual_ref[0].astype(jnp.float32) + gain_ref[...] * projected * inv_rms).astype(jnp.bfloat16)
+
+    some = pl.BlockSpec((rows, width), lambda i: (i, 0))
+    place = pl.BlockSpec((1, rows, width), lambda i: (i, chunk, 0))
+    operands = [own, arrived, residual, gain.reshape(1, width)]
+    specs = [some, some, place, pl.BlockSpec((1, width), lambda i: (0, 0))]
+    if earlier is not None:
+        operands.append(earlier)
+        specs.append(pl.BlockSpec(memory_space=pl.ANY))
+    return pl.pallas_call(
+        kernel,
+        grid=(requests,),
+        in_specs=specs,
+        out_specs=place,
+        out_shape=jax.ShapeDtypeStruct(residual.shape, jnp.bfloat16),
+        input_output_aliases={} if earlier is None else {4: 0},
+        compiler_params=kernel_params(16),
+        cost_estimate=pl.CostEstimate(flops=0, bytes_accessed=4 * mib, transcendentals=0),
+        name="finish",
+    )(*operands)
+
+
+def by_heads(
+    queries,
+    new_keys,
+    new_values,
+    pool_keys,
+    pool_values,
+    page_table,
+    cache_len,
+    out_weight,
+    residual,
+    post_gain,
+):
+    req_count, per_req, heads_here, head_dim = queries.shape
+    kv_here = new_keys.shape[2]
+    pages = pool_keys.shape[0]
+    blk_count = lax.axis_size("blk")
+    shares = lax.axis_size("head")
+    group = heads_here // kv_here
+    core = (lax.axis_index("blk") % 2)[None]
+    place = lax.axis_index("head")[None]
+    weight = out_weight.reshape(heads_here * head_dim, out_weight.shape[2])
+    queries = queries.reshape(req_count, shares, chunks, per_req // (shares * chunks), heads_here, head_dim)
+    exchange = functools.partial(lax.all_to_all, axis_name="blk", split_axis=0, concat_axis=0, tiled=True)
+    message = pack_first(pool_keys, pool_values, new_keys, new_values, queries)
+    message = exchange(message.reshape(blk_count, pages + 3, per_req, head_dim))
+    asked = [None]
+    for chunk in range(1, chunks):
+        packed = pack_queries(queries, kv_here, chunk)
+        asked.append(exchange(packed.reshape((blk_count,) + packed.shape[2:])))
+    other = lax.ppermute(message[:, 0:pages], "blk", [(i, i ^ 1) for i in range(blk_count)])
+    mixed_out = None
+    for chunk in range(chunks):
+        attended = attend(core, page_table, cache_len, message, other, asked[chunk], chunk, pages, shares, group)
+        own, theirs = project(place, exchange(attended), weight, shares)
+        arrived = lax.ppermute(theirs, "head", [(0, 1), (1, 0)])
+        mixed_out = finish(own, arrived, residual, post_gain, chunk, mixed_out)
+    return mixed_out
 
 
 def group_pages(page_count, page_len):
@@ -153,8 +436,14 @@
         P(None, ("blk", "head"), None),
         P(),
     )
+    def one_device(queries, new_keys, *rest):
+        requests, per_req = queries.shape[0], queries.shape[1]
+        owners = mesh.shape["blk"] == 2 * new_keys.shape[2] and mesh.shape["head"] == 2 and requests == 2
+        fits = rest[1].shape[1] == per_req == 128 and queries.shape[2] == 2 * new_keys.shape[2]
+        return (by_heads if owners and fits else shards)(queries, new_keys, *rest)
+
     return jax.shard_map(
-        shards,
+        one_device,
         mesh=mesh,
         in_specs=placed,
         out_specs=P(None, ("blk", "head"), None),

time: 427 us -> 156 us (0.37)
  waiting for transfers between devices: 260 us -> 24 us
  matrix products: 109 us -> 0 us
  blocking collectives: 0 us -> 65.7 us
  Pallas kernels: 0 us -> 31.4 us
  local copies, waits for them, and re-layouts: 36.4 us -> 17.2 us
  starting transfers between devices: 0.16 us -> 16.8 us
  between operations: 13.3 us -> 0.14 us
  other arithmetic: 7.9 us -> 0 us
    all_gather x4 -> x0, waiting for transfers between devices: 225 us -> none  [the longest x1 78.4 us: shards(): lax.all_gather(new_values, 'blk', axis=1, tiled=True)]
    dot_general x9 -> x0, matrix products: 109 us -> none  [the longest x4 56.3 us: compute(): jnp.einsum('tkgd,skd->kgts', grouped, key_block, preferred_element_type=j...]
    all_to_all x0 -> x1, blocking collectives: none -> 65.7 us  [by_heads(): message = exchange(message.reshape(blk_count, pages + 3, per_req, head_dim))]
    reduce_scatter x1 -> x0, waiting for transfers between devices: 33.1 us -> none  [shards(): lax.psum_scatter(jnp.dot(attended, weight_rows, preferred_element_type=jn...]
    pallas_call x0 -> x8, Pallas kernels: none -> 31.4 us  [the longest x2 17.8 us: attend(): pl.pallas_call(functools.partial(attend_kernel, pages, chunk, shares), in...]
    dynamic_slice x4 -> x0, local copies, waits for them, and re-layouts: 23.9 us -> none  [attend_pages(): lax.scan(one_group, running, (key_groups, value_groups, valid_groups))]
    all_to_all x0 -> x3, starting transfers between devices: none -> 12.9 us  [the longest x2 8.21 us: by_heads(): own, theirs = project(place, exchange(attended), weight, shares)]
    ppermute x0 -> x3, waiting for transfers between devices: none -> 12.5 us  [the longest x2 12.5 us: by_heads(): arrived = lax.ppermute(theirs, 'head', [(0, 1), (1, 0)])]
  transfers between devices with their start and end apart: 5 -> 6, of which waited for: 5 -> 5; matrix products, arithmetic and copies ran while one was open for 19% -> 0% of each run, Pallas kernels for 0% -> 18%
where the time goes in v2:
time: 156 us; the launch traced here: 155 us
  blocking collectives  65.7 us (42%)
  Pallas kernels  31.4 us (20%)
  waiting for transfers between devices  24 us (15%)
  local copies, waits for them, and re-layouts  17.2 us (11%)
  starting transfers between devices  16.8 us (11%)
    all_to_all x1, blocking collectives, by_heads(): message = exchange(message.reshape(blk_count, pages + 3, per_req, head_dim))  65.7 us
    pallas_call x2, Pallas kernels, attend(): pl.pallas_call(functools.partial(attend_kernel, pages, chunk, shares), in...  17.8 us
    unnamed x20, local copies, waits for them, and re-layouts  16.2 us
    ppermute x2, waiting for transfers between devices, by_heads(): arrived = lax.ppermute(theirs, 'head', [(0, 1), (1, 0)])  12.5 us
    all_to_all x2, starting transfers between devices, by_heads(): own, theirs = project(place, exchange(attended), weight, shares)  8.21 us
    all_to_all x2, waiting for transfers between devices, by_heads(): own, theirs = project(place, exchange(attended), weight, shares)  6.82 us
    pallas_call x2, Pallas kernels, project(): pl.pallas_call(functools.partial(project_kernel, shares), in_specs=[in_sm...  6.12 us
    all_to_all x1, waiting for transfers between devices, by_heads(): asked.append(exchange(packed.reshape((blk_count,) + packed.shape[2:])))  4.72 us
  transfers between devices with their start and end apart: 6, of which 5 were waited for; matrix products, arithmetic and copies ran while one was open for 0% of the time, Pallas kernels for 18%

profile of v2, /device:TPU:0, one launch (start us, length us, event | category | flops | bytes accessed | tf_op | source)
XLA Modules:
  0.0 155.2 jit_solution(530279813050782106)
XLA Ops:
  0.0 2.9 %pack_first.1 = bf16[8,2,5,128,128]{4,3,2,1,0:T(8,128)(2,1)S(1)} custom-call(bf16[2,128,8,128]{3,2,1,0:T(8,128)(2,1)} %pool_k.1, bf16[2,128,8,128]{3,2,1,0:T(8,128)(2,1)} %pool_v.1, bf16[2,128,8,128]{3,2,1,0:T(8,128)(2,1)} %new_k.1, bf16[2,128,8,128]{3,2,1,0:T(8,128)(2,1)} %new_v.1, bf16[2,2,2,32,16,128]{5,4,3,2,1,0:T(8,128)(2,1)} %bitcast.9), custom_call_target="tpu_custom_call" | custom-call | bytes 6291456 | tf_op jit(solution)/shard_map/pack_first/pallas_call | solution.py:72
  2.9 65.7 %all_to_all.20.message = bf16[16,5,128,128]{3,2,1,0:T(8,128)(2,1)S(1)} all-to-all(bf16[16,5,128,128]{3,2,1,0:T(8,128)(2,1)S(1)} %bitcast.8), channel_id=1, replica_groups=mesh['blk'=16,'head'=2] {'blk'}, dimensions={0} | all-to-all | bytes 5242880 | tf_op jit(solution)/shard_map/all_to_all | solution.py:279
  68.7 1.0 slice.4
  69.7 0.8 collective-permute-start
  70.5 2.1 %pack_queries.1 = bf16[8,2,1,128,128]{4,3,2,1,0:T(8,128)(2,1)} custom-call(bf16[2,2,2,32,16,128]{5,4,3,2,1,0:T(8,128)(2,1)} %bitcast.10), custom_call_target="tpu_custom_call" | custom-call | bytes 1048576 | tf_op jit(solution)/shard_map/pack_queries/pallas_call | solution.py:92
  72.6 4.7 %all-to-all-start.1 = ((bf16[16,1,128,128]{3,2,1,0:T(8,128)(2,1)}), bf16[16,1,128,128]{3,2,1,0:T(8,128)(2,1)S(1)}, u32[]{:S(2)}, u32[]{:S(2)}) async-start(bf16[16,1,128,128]{3,2,1,0:T(8,128)(2,1)} %bitcast.4), calls=%async_computation.1 | async-start | bytes 1048576 | tf_op jit(solution)/shard_map/all_to_all | solution.py:283
  77.3 0.0 collective-permute-done.other
  77.3 8.9 %attend.3 = bf16[16,64,256]{2,1,0:T(8,128)(2,1)S(1)} custom-call(s32[1]{0:T(128)} %bitcast.1.core_ref, s32[2,16]{1,0:T(2,128)S(1)} %copy-done.7, s32[2]{0:T(128)S(1)} %copy-done.8, bf16[16,5,128,128]{3,2,1,0:T(8,128)(2,1)S(1)} %all_to_all.20.message, bf16[16,2,128,128]{3,2,1,0:T(8,128)(2,1)} %collective-permute-done.other), custom_call_target="tpu_custom_call" | custom-call | flops 6442450944 | bytes 8388608 | tf_op jit(solution)/shard_map/attend/pallas_call | solution.py:171
  86.2 0.0 copy-start.6
  86.2 0.8 copy-done.6
  87.0 4.7 %all-to-all-done.1.rest_0_ = bf16[16,1,128,128]{3,2,1,0:T(8,128)(2,1)S(1)} async-done(((bf16[16,1,128,128]{3,2,1,0:T(8,128)(2,1)}), bf16[16,1,128,128]{3,2,1,0:T(8,128)(2,1)S(1)}, u32[]{:S(2)}, u32[]{:S(2)}) %all-to-all-start.1) | async-done | bytes 524320 | tf_op jit(solution)/shard_map/all_to_all | solution.py:283
  91.7 0.8 copy-done.3
  92.5 4.1 %all-to-all-start.3 = ((bf16[16,64,256]{2,1,0:T(8,128)(2,1)}), bf16[16,64,256]{2,1,0:T(8,128)(2,1)S(1)}, u32[]{:S(2)}, u32[]{:S(2)}) async-start(bf16[16,64,256]{2,1,0:T(8,128)(2,1)} %copy-done.6), calls=%async_computation.3 | async-start | bytes 1048576 | tf_op jit(solution)/shard_map/all_to_all | solution.py:288
  96.6 0.0 copy-start.4
  96.6 1.0 copy-done.4
  97.7 8.9 %attend.2 = bf16[16,64,256]{2,1,0:T(8,128)(2,1)S(1)} custom-call(s32[1]{0:T(128)} %bitcast.1.core_ref, s32[2,16]{1,0:T(2,128)S(1)} %copy-done.7, s32[2]{0:T(128)S(1)} %copy-done.8, bf16[16,5,128,128]{3,2,1,0:T(8,128)(2,1)S(1)} %all_to_all.20.message, bf16[16,2,128,128]{3,2,1,0:T(8,128)(2,1)} %collective-permute-done.other, ...), custom_call_target="tpu_custom_call" | custom-call | flops 6442450944 | bytes 8388608 | tf_op jit(solution)/shard_map/attend/pallas_call | solution.py:171
  106.6 0.0 copy-start.5
  106.6 0.8 copy-done.5
  107.4 3.7 %all-to-all-done.3.attended = bf16[16,64,256]{2,1,0:T(8,128)(2,1)S(1)} async-done(((bf16[16,64,256]{2,1,0:T(8,128)(2,1)}), bf16[16,64,256]{2,1,0:T(8,128)(2,1)S(1)}, u32[]{:S(2)}, u32[]{:S(2)}) %all-to-all-start.3) | async-done | bytes 524320 | tf_op jit(solution)/shard_map/all_to_all | solution.py:288
  111.1 4.1 %all-to-all-start.2 = ((bf16[16,64,256]{2,1,0:T(8,128)(2,1)}), bf16[16,64,256]{2,1,0:T(8,128)(2,1)S(1)}, u32[]{:S(2)}, u32[]{:S(2)}) async-start(bf16[16,64,256]{2,1,0:T(8,128)(2,1)} %copy-done.5), calls=%async_computation.2 | async-start | bytes 1048576 | tf_op jit(solution)/shard_map/all_to_all | solution.py:288
  115.2 0.0 copy-start
  115.2 6.4 %copy-done = bf16[16,128,4608]{2,1,0:T(8,128)(2,1)S(1)} copy-done((bf16[16,128,4608]{2,1,0:T(8,128)(2,1)S(1)}, bf16[16,128,4608]{2,1,0:T(8,128)(2,1)}, u32[]{:S(2)}) %copy-start) | copy-done | bytes 18874392
  121.6 3.5 %project.3 = (f32[64,4608]{1,0:T(8,128)S(1)}, bf16[64,4608]{1,0:T(8,128)(2,1)}) custom-call(s32[1]{0:T(128)} %bitcast.place_ref, bf16[16,64,256]{2,1,0:T(8,128)(2,1)S(1)} %all-to-all-done.3.attended, bf16[2048,4608]{1,0:T(8,128)(2,1)S(1)} %bitcast.6), custom_call_target="tpu_custom_call" | custom-call | flops 2415919104 | bytes 18874368 | tf_op jit(solution)/shard_map/project/pallas_call | solution.py:210
  125.0 1.5 collective-permute-start.2
  126.6 3.1 %all-to-all-done.2.attended = bf16[16,64,256]{2,1,0:T(8,128)(2,1)S(1)} async-done(((bf16[16,64,256]{2,1,0:T(8,128)(2,1)}), bf16[16,64,256]{2,1,0:T(8,128)(2,1)S(1)}, u32[]{:S(2)}, u32[]{:S(2)}) %all-to-all-start.2) | async-done | bytes 524320 | tf_op jit(solution)/shard_map/all_to_all | solution.py:288
  129.7 6.4 %copy-done.1 = bf16[16,128,4608]{2,1,0:T(8,128)(2,1)S(1)} copy-done((bf16[16,128,4608]{2,1,0:T(8,128)(2,1)S(1)}, bf16[16,128,4608]{2,1,0:T(8,128)(2,1)}, u32[]{:S(2)}) %copy-start.1) | copy-done | bytes 18874392
  136.0 2.6 %project.2 = (f32[64,4608]{1,0:T(8,128)S(1)}, bf16[64,4608]{1,0:T(8,128)(2,1)S(1)}) custom-call(s32[1]{0:T(128)} %bitcast.place_ref, bf16[16,64,256]{2,1,0:T(8,128)(2,1)S(1)} %all-to-all-done.2.attended, bf16[2048,4608]{1,0:T(8,128)(2,1)S(1)} %bitcast.7), custom_call_target="tpu_custom_call" | custom-call | flops 2415919104 | bytes 18874368 | tf_op jit(solution)/shard_map/project/pallas_call | solution.py:210
  138.7 1.6 %collective-permute-start.1 = (bf16[64,4608]{1,0:T(8,128)(2,1)S(1)}, bf16[64,4608]{1,0:T(8,128)(2,1)S(1)}, u32[]{:S(2)}, u32[]{:S(2)}) collective-permute-start(bf16[64,4608]{1,0:T(8,128)(2,1)S(1)} %get-tuple-element.10), channel_id=1, source_target_pairs={{0,1},{1,0},{2,3},{3,2},{4,5},{5,4},{6,7},{7,6},{8,9},{9,8},{10,11... | collective-permute-start | bytes 1769480 | tf_op jit(solution)/shard_map/ppermute | solution.py:289
  140.3 0.6 collective-permute-done.2.arrived_ref
  140.9 1.2 finish.2.rest_0_
  142.1 11.9 %collective-permute-done.1.arrived_ref = bf16[64,4608]{1,0:T(8,128)(2,1)S(1)} collective-permute-done((bf16[64,4608]{1,0:T(8,128)(2,1)S(1)}, bf16[64,4608]{1,0:T(8,128)(2,1)S(1)}, u32[]{:S(2)}, u32[]{:S(2)}) %collective-permute-start.1) | collective-permute-done | bytes 589856 | tf_op jit(solution)/shard_map/ppermute | solution.py:289
  154.0 1.2 finish.3
  (11 shorter events, 0.0 us)
Async XLA Ops:
  69.7 7.6 %copy-start.7 = (s32[2,16]{1,0:T(2,128)S(1)}, s32[2,16]{1,0:T(2,128)}, u32[]{:S(2)}) copy-start(s32[2,16]{1,0:T(2,128)} %table_ref.3) | copy-start | bytes 388
  69.7 7.6 %copy-start.8 = (s32[2]{0:T(128)S(1)}, s32[2]{0:T(128)}, u32[]{:S(2)}) copy-start(s32[2]{0:T(128)} %len_ref.3) | copy-start | bytes 28
  69.7 7.6 %collective-permute-start = (bf16[16,2,128,128]{3,2,1,0:T(8,128)(2,1)}, bf16[16,2,128,128]{3,2,1,0:T(8,128)(2,1)}, u32[]{:S(2)}, u32[]{:S(2)}) collective-permute-start(bf16[16,2,128,128]{3,2,1,0:T(8,128)(2,1)} %slice.4), channel_id=1, source_target_pairs={{0,2},{2,0},{4,6},{6,4},{8,10},{10,8},{12,14},{14,12},{16,18},{18,... | collective-permute-start | bytes 3145736 | tf_op jit(solution)/shard_map/ppermute | solution.py:284
  72.6 19.1 %all-to-all-start.1 = ((bf16[16,1,128,128]{3,2,1,0:T(8,128)(2,1)}), bf16[16,1,128,128]{3,2,1,0:T(8,128)(2,1)S(1)}, u32[]{:S(2)}, u32[]{:S(2)}) async-start(bf16[16,1,128,128]{3,2,1,0:T(8,128)(2,1)} %bitcast.4), calls=%async_computation.1 | async-start | bytes 1048576 | tf_op jit(solution)/shard_map/all_to_all | solution.py:283
  86.2 0.8 copy-start.6
  91.7 0.8 copy-start.3
  92.5 18.6 %all-to-all-start.3 = ((bf16[16,64,256]{2,1,0:T(8,128)(2,1)}), bf16[16,64,256]{2,1,0:T(8,128)(2,1)S(1)}, u32[]{:S(2)}, u32[]{:S(2)}) async-start(bf16[16,64,256]{2,1,0:T(8,128)(2,1)} %copy-done.6), calls=%async_computation.3 | async-start | bytes 1048576 | tf_op jit(solution)/shard_map/all_to_all | solution.py:288
  96.6 1.0 copy-start.4
  106.6 0.8 copy-start.5
  111.1 18.6 %all-to-all-start.2 = ((bf16[16,64,256]{2,1,0:T(8,128)(2,1)}), bf16[16,64,256]{2,1,0:T(8,128)(2,1)S(1)}, u32[]{:S(2)}, u32[]{:S(2)}) async-start(bf16[16,64,256]{2,1,0:T(8,128)(2,1)} %copy-done.5), calls=%async_computation.2 | async-start | bytes 1048576 | tf_op jit(solution)/shard_map/all_to_all | solution.py:288
  115.2 6.4 %copy-start = (bf16[16,128,4608]{2,1,0:T(8,128)(2,1)S(1)}, bf16[16,128,4608]{2,1,0:T(8,128)(2,1)}, u32[]{:S(2)}) copy-start(bf16[16,128,4608]{2,1,0:T(8,128)(2,1)} %param.17) | copy-start | bytes 56623108
  125.0 15.9 %collective-permute-start.2 = (bf16[64,4608]{1,0:T(8,128)(2,1)}, bf16[64,4608]{1,0:T(8,128)(2,1)S(1)}, u32[]{:S(2)}, u32[]{:S(2)}) collective-permute-start(bf16[64,4608]{1,0:T(8,128)(2,1)} %get-tuple-element.12), channel_id=1, source_target_pairs={{0,1},{1,0},{2,3},{3,2},{4,5},{5,4},{6,7},{7,6},{8,9},{9,8},{10,11... | collective-permute-start | bytes 1769480 | tf_op jit(solution)/shard_map/ppermute | solution.py:289
  129.7 6.4 %copy-start.1 = (bf16[16,128,4608]{2,1,0:T(8,128)(2,1)S(1)}, bf16[16,128,4608]{2,1,0:T(8,128)(2,1)}, u32[]{:S(2)}) copy-start(bf16[16,128,4608]{2,1,0:T(8,128)(2,1)} %param.17) | copy-start | bytes 56623108
  136.0 4.2 %copy-start.9 = (f32[4608]{0:T(1024)S(1)}, f32[4608]{0:T(1024)}, u32[]{:S(2)}) copy-start(f32[4608]{0:T(1024)} %param.19) | copy-start | bytes 55300
  136.0 4.9 %copy-start.2 = (bf16[2,64,4608]{2,1,0:T(8,128)(2,1)S(1)}, bf16[2,64,4608]{2,1,0:T(8,128)(2,1)}, u32[]{:S(2)}) copy-start(bf16[2,64,4608]{2,1,0:T(8,128)(2,1)} %residual_ref.3) | copy-start | bytes 3538948
  138.7 15.3 %collective-permute-start.1 = (bf16[64,4608]{1,0:T(8,128)(2,1)S(1)}, bf16[64,4608]{1,0:T(8,128)(2,1)S(1)}, u32[]{:S(2)}, u32[]{:S(2)}) collective-permute-start(bf16[64,4608]{1,0:T(8,128)(2,1)S(1)} %get-tuple-element.10), channel_id=1, source_target_pairs={{0,1},{1,0},{2,3},{3,2},{4,5},{5,4},{6,7},{7,6},{8,9},{9,8},{10,11... | collective-permute-start | bytes 1769480 | tf_op jit(solution)/shard_map/ppermute | solution.py:289

commit v3 on v2

--- a/solution.py
+++ b/solution.py
@@ -12,9 +12,11 @@
 norm_eps = 1e-06
 log2_e = 1.4426950408889634
 chunks = 2
+pieces = 2
 key_tile = 256
 mib = 1024 * 1024
 in_vmem = pl.BlockSpec(memory_space=pltpu.VMEM)
+in_hbm = pl.BlockSpec(memory_space=pltpu.HBM)
 in_smem = pl.BlockSpec(memory_space=pltpu.SMEM)
 
 
@@ -29,54 +31,66 @@
         yield head, staged[pl.ds(head, rows, stride=heads), :].astype(jnp.bfloat16)
 
 
-def put_queries(queries, out, part, staged):
+def pack_first_kernel(pool_k, pool_v, new_k, new_v, queries, out, held_kv, held_q, made, staged, in_sem, out_sem):
+    pages = pool_k.shape[0]
+    cores = new_k.shape[0]
     _, shares, _, rows, heads, head_dim = queries.shape
     group = heads // out.shape[0]
-    source = queries[...].reshape(shares * rows, heads, head_dim)
-    for head, picked in split_heads(source, staged):
-        first = head % group * shares * rows
-        out[head // group, 0, part, first : first + shares * rows, :] = picked
+    tasks = []
+    for core, pool in enumerate((pool_k, pool_v)):
+        tasks += [(pool.at[page], core, page) for page in range(pages)]
+    for part, new in enumerate((new_k, new_v)):
+        tasks += [(new.at[core], core, pages + part) for core in range(cores)]
+    arrivals = [pltpu.make_async_copy(source, held_kv.at[i], in_sem.at[i]) for i, (source, _, _) in enumerate(tasks)]
+    for core in range(cores):
+        at = len(tasks) + core
+        arrivals.append(pltpu.make_async_copy(queries.at[core, :, 0], held_q.at[core], in_sem.at[at]))
+    for arrival in arrivals:
+        arrival.start()
+    leaving = []
+
+    def leave(core, part):
+        here = made.at[:, core, part]
+        leaving.append(pltpu.make_async_copy(here, out.at[:, core, part], out_sem.at[len(leaving)]))
+        leaving[-1].start()
+
+    for i, (_, core, part) in enumerate(tasks):
+        arrivals[i].wait()
+        for head, picked in split_heads(held_kv[i], staged.at[i % 2]):
+            made[head, core, part] = picked
+        leave(core, part)
+    for core in range(cores):
+        arrivals[len(tasks) + core].wait()
+        source = held_q[core].reshape(shares * rows, heads, head_dim)
+        for head, picked in split_heads(source, staged.at[core % 2]):
+            first = head % group * shares * rows
+            made[head // group, core, pages + 2, first : first + shares * rows, :] = picked
+        leave(core, pages + 2)
+    for copy in leaving:
+        copy.wait()
 
 
 def pack_first(pool_keys, pool_values, new_keys, new_values, queries):
-    steps, rows, kv_heads, head_dim = new_keys.shape
+    cores, rows, kv_heads, head_dim = new_keys.shape
     pages = pool_keys.shape[0]
     parts = pages + 3
-
-    def kernel(pool_k, pool_v, new_k, new_v, some_queries, out, staged):
-        core = pl.program_id(0)
-
-        @pl.when(core == 0)
-        def _():
-            for page in range(pages):
-                for head, picked in split_heads(pool_k[page], staged):
-                    out[head, 0, page] = picked
-
-        @pl.when(core == 1)
-        def _():
-            for page in range(pages):
-                for head, picked in split_heads(pool_v[page], staged):
-                    out[head, 0, page] = picked
-
-        for head, picked in split_heads(new_k[0], staged):
-            out[head, 0, pages] = picked
-        for head, picked in split_heads(new_v[0], staged):
-            out[head, 0, pages + 1] = picked
-        put_queries(some_queries, out, pages + 2, staged)
-
-    whole = pl.BlockSpec((pages, rows, kv_heads, head_dim), lambda i: (0, 0, 0, 0))
-    one = pl.BlockSpec((1, rows, kv_heads, head_dim), lambda i: (i, 0, 0, 0))
     _, shares, _, chunk_rows, heads, _ = queries.shape
-    some = pl.BlockSpec((1, shares, 1, chunk_rows, heads, head_dim), lambda i: (i, 0, 0, 0, 0, 0))
+    pieces = 2 * pages + 2 * cores
     sources = [pltpu.with_memory_space_constraint(x, pltpu.HBM) for x in (pool_keys, pool_values, new_keys, new_values, queries)]
     return pl.pallas_call(
-        kernel,
-        grid=(steps,),
-        in_specs=[whole, whole, one, one, some],
-        out_specs=pl.BlockSpec((kv_heads, 1, parts, rows, head_dim), lambda i: (0, i, 0, 0, 0)),
-        out_shape=jax.ShapeDtypeStruct((kv_heads, steps, parts, rows, head_dim), jnp.bfloat16),
-        scratch_shapes=[pltpu.VMEM((rows * kv_heads, head_dim), jnp.float32)],
-        compiler_params=kernel_params(24),
+        pack_first_kernel,
+        in_specs=[in_hbm] * 5,
+        out_specs=in_hbm,
+        out_shape=pltpu.HBM((kv_heads, cores, parts, rows, head_dim), jnp.bfloat16),
+        scratch_shapes=[
+            pltpu.VMEM((pieces, rows, kv_heads, head_dim), jnp.bfloat16),
+            pltpu.VMEM((cores, shares, chunk_rows, heads, head_dim), jnp.bfloat16),
+            pltpu.VMEM((kv_heads, cores, parts, rows, head_dim), jnp.bfloat16),
+            pltpu.VMEM((2, max(rows * kv_heads, shares * chunk_rows * heads), head_dim), jnp.float32),
+            pltpu.SemaphoreType.DMA((pieces + cores,)),
+            pltpu.SemaphoreType.DMA((pieces + cores,)),
+        ],
+        compiler_params=kernel_params(10),
         cost_estimate=pl.CostEstimate(flops=0, bytes_accessed=6 * mib, transcendentals=0),
         name="pack_first",
     )(*sources)
@@ -87,7 +101,10 @@
     group = heads // kv_heads
 
     def kernel(some_queries, out, staged):
-        put_queries(some_queries, out, 0, staged)
+        source = some_queries[...].reshape(shares * rows, heads, head_dim)
+        for head, picked in split_heads(source, staged):
+            first = head % group * shares * rows
+            out[head // group, 0, 0, first : first + shares * rows, :] = picked
 
     return pl.pallas_call(
         kernel,
@@ -96,34 +113,43 @@
         out_specs=pl.BlockSpec((kv_heads, 1, 1, group * shares * rows, head_dim), lambda i: (0, i, 0, 0, 0)),
         out_shape=jax.ShapeDtypeStruct((kv_heads, steps, 1, group * shares * rows, head_dim), jnp.bfloat16),
         scratch_shapes=[pltpu.VMEM((shares * rows * heads, head_dim), jnp.float32)],
-        compiler_params=kernel_params(24),
+        compiler_params=kernel_params(6),
         cost_estimate=pl.CostEstimate(flops=0, bytes_accessed=mib, transcendentals=0),
         name="pack_queries",
     )(pltpu.with_memory_space_constraint(queries, pltpu.HBM))
 
 
 def attend_kernel(pages, chunk, shares, core_ref, table_ref, len_ref, message, other, *rest):
-    out, cache_k, cache_v, new_v, total = rest[-5:]
-    queries, query_part = (rest[0], 0) if len(rest) > 5 else (message, pages + 2)
+    out, cache_k, cache_v, new_v, total, made, held, others, in_sem, other_sem, out_sem = rest[-11:]
+    fetch = pltpu.make_async_copy(other.at[:, 0:pages], others, other_sem)
+    fetch.start()
+    queries, query_part = message, pages + 2
+    if len(rest) > 11:
+        queries, query_part = held, 0
+        arrival = pltpu.make_async_copy(rest[0], held, in_sem)
+        arrival.start()
     blocks, _, page_rows, head_dim = message.shape
     slots = table_ref.shape[1]
-    block_rows = queries.shape[2]
     group = out.shape[2] // head_dim
+    block_rows = out.shape[1] * group
     core = core_ref[0]
     cached = len_ref[core]
+    for block in range(blocks):
+        new_v[block * page_rows : (block + 1) * page_rows, 0:head_dim] = message[block, pages + 1]
+    new_v[:, head_dim : 2 * head_dim] = jnp.ones((blocks * page_rows, head_dim), jnp.bfloat16)
+    fetch.wait()
     for slot in range(slots):
         page = table_ref[core, slot]
         mine = message[page // pages, page % pages]
-        theirs = other[page // pages, page % pages]
+        theirs = others[page // pages, page % pages]
         seen = slot * page_rows + lax.broadcasted_iota(jnp.int32, (page_rows, head_dim), 0) < cached
         here = pl.ds(slot * page_rows, page_rows)
         cache_k[here, :] = jnp.where(core == 0, mine, theirs)
         values = jnp.where(core == 0, theirs, mine).astype(jnp.float32)
         cache_v[here, 0:head_dim] = jnp.where(seen, values, 0.0).astype(jnp.bfloat16)
         cache_v[here, head_dim : 2 * head_dim] = jnp.where(seen, 1.0, 0.0).astype(jnp.bfloat16)
-    for block in range(blocks):
-        new_v[block * page_rows : (block + 1) * page_rows, 0:head_dim] = message[block, pages + 1]
-    new_v[:, head_dim : 2 * head_dim] = jnp.ones((blocks * page_rows, head_dim), jnp.bfloat16)
+    if len(rest) > 11:
+        arrival.wait()
 
     def add(first_block, block_count, keys, values, begin=False, causal=False):
         rows = block_count * block_rows
@@ -155,37 +181,60 @@
             add(later, count, keys, values)
             later += count
     per_head = block_rows // group
+    copies = []
     for block in range(blocks):
         here = pl.ds(block * block_rows, block_rows)
         attended = (total[here, 0:head_dim] / total[here, head_dim : 2 * head_dim]).astype(jnp.bfloat16)
         for head in range(group):
-            out[block, :, head * head_dim : (head + 1) * head_dim] = attended[head * per_head : (head + 1) * per_head, :]
-
-
-def attend(core, page_table, cache_len, message, other, queries, chunk, pages, shares, group):
+            made[block, :, head * head_dim : (head + 1) * head_dim] = attended[head * per_head : (head + 1) * per_head, :]
+        if block % half == half - 1:
+            here = pl.ds(block + 1 - half, half)
+            copies.append(pltpu.make_async_copy(made.at[here], out.at[here], out_sem.at[len(copies)]))
+            copies[-1].start()
+    for copy in copies:
+        copy.wait()
+
+
+def attend(core, page_table, cache_len, message, other, queries, chunk, *, pages, shares, group):
     blocks, _, page_rows, head_dim = message.shape
     slots = page_table.shape[1]
     block_rows = page_rows * group // chunks
-    operands = [message, other] + ([] if queries is None else [queries])
+    operands = [message, pltpu.with_memory_space_constraint(other, pltpu.HBM)]
+    specs = [in_smem] * 3 + [in_vmem, in_hbm]
+    if queries is not None:
+        operands.append(pltpu.with_memory_space_constraint(queries, pltpu.HBM))
+        specs.append(in_hbm)
     seen = blocks * block_rows * (slots + blocks // 2) * page_rows
     return pl.pallas_call(
         functools.partial(attend_kernel, pages, chunk, shares),
-        in_specs=[in_smem] * 3 + [in_vmem] * len(operands),
-        out_specs=in_vmem,
-        out_shape=jax.ShapeDtypeStruct((blocks, block_rows // group, group * head_dim), jnp.bfloat16),
+        in_specs=specs,
+        out_specs=in_hbm,
+        out_shape=pltpu.HBM((blocks, block_rows // group, group * head_dim), jnp.bfloat16),
         scratch_shapes=[
             pltpu.VMEM((slots * page_rows, head_dim), jnp.bfloat16),
             pltpu.VMEM((slots * page_rows, 2 * head_dim), jnp.bfloat16),
             pltpu.VMEM((blocks * page_rows, 2 * head_dim), jnp.bfloat16),
             pltpu.VMEM((blocks * block_rows, 2 * head_dim), jnp.float32),
+            pltpu.VMEM((blocks, block_rows // group, group * head_dim), jnp.bfloat16),
+            pltpu.VMEM((blocks, 1, block_rows, head_dim) if len(operands) > 2 else (8, 128), jnp.bfloat16),
+            pltpu.VMEM((blocks, pages, page_rows, head_dim), jnp.bfloat16),
+            pltpu.SemaphoreType.DMA(()),
+            pltpu.SemaphoreType.DMA(()),
+            pltpu.SemaphoreType.DMA((2,)),
         ],
-        compiler_params=kernel_params(24),
+        compiler_params=kernel_params(12),
         cost_estimate=pl.CostEstimate(flops=8 * seen * head_dim, bytes_accessed=8 * mib, transcendentals=2 * seen),
         name="attend",
     )(core, page_table, cache_len, *operands)
 
 
-def project_kernel(shares, place_ref, attended, weight, own, theirs, rows):
+def project_kernel(shares, begin, place_ref, attended, weight, own, theirs, rows, held, sem):
+    tiles, _, tile = held.shape
+    arrivals = []
+    for i in range(tiles):
+        columns = pl.ds(begin + i * tile, tile)
+        arrivals.append(pltpu.make_async_copy(weight.at[:, columns], held.at[i], sem.at[i]))
+        arrivals[-1].start()
     place = place_ref[0]
     sources, share_rows, features = attended.shape
     requests = 2
@@ -195,47 +244,60 @@
         for share in range(shares):
             at = pl.multiple_of((share ^ place) * (requests * count), requests * count) + source % requests * count
             rows[pl.ds(at, count), first : first + features] = attended[source, share * count : (share + 1) * count, :]
-    width = weight.shape[1]
-    tile = 512 if width % 512 == 0 else width
-    for first in range(0, width, tile):
-        product = jnp.dot(rows[...], weight[:, first : first + tile], preferred_element_type=jnp.float32)
-        own[:, first : first + tile] = product[0 : requests * count, :]
-        theirs[:, first : first + tile] = product[requests * count :, :].astype(jnp.bfloat16)
-
-
-def project(place, attended, weight, shares):
+    for i in range(tiles):
+        arrivals[i].wait()
+        product = jnp.dot(rows[...], held[i], preferred_element_type=jnp.float32)
+        own[:, i * tile : (i + 1) * tile] = product[0 : requests * count, :]
+        theirs[:, i * tile : (i + 1) * tile] = product[requests * count :, :].astype(jnp.bfloat16)
+
+
+def project(place, attended, weight, shares, piece):
     sources, share_rows, features = attended.shape
     depth, width = weight.shape
+    columns = width // pieces
+    tile = columns // 3
     rows = 2 * share_rows
     return pl.pallas_call(
-        functools.partial(project_kernel, shares),
-        in_specs=[in_smem, in_vmem, in_vmem],
+        functools.partial(project_kernel, shares, piece * columns),
+        in_specs=[in_smem, in_vmem, in_hbm],
         out_specs=[in_vmem, in_vmem],
         out_shape=[
-            jax.ShapeDtypeStruct((rows // shares, width), jnp.float32),
-            jax.ShapeDtypeStruct((rows // shares, width), jnp.bfloat16),
+            jax.ShapeDtypeStruct((rows // shares, columns), jnp.float32),
+            jax.ShapeDtypeStruct((rows // shares, columns), jnp.bfloat16),
         ],
-        scratch_shapes=[pltpu.VMEM((rows, depth), jnp.bfloat16)],
+        scratch_shapes=[
+            pltpu.VMEM((rows, depth), jnp.bfloat16),
+            pltpu.VMEM((columns // tile, depth, tile), jnp.bfloat16),
+            pltpu.SemaphoreType.DMA((columns // tile,)),
+        ],
         compiler_params=kernel_params(16),
-        cost_estimate=pl.CostEstimate(flops=2 * rows * depth * width, bytes_accessed=2 * depth * width, transcendentals=0),
+        cost_estimate=pl.CostEstimate(flops=2 * rows * depth * columns, bytes_accessed=2 * depth * columns, transcendentals=0),
         name="project",
-    )(place, attended, pltpu.with_memory_space_constraint(weight, pltpu.VMEM))
+    )(place, attended, pltpu.with_memory_space_constraint(weight, pltpu.HBM))
 
 
 def finish(own, arrived, residual, gain, chunk, earlier):
     requests, per_req, width = residual.shape
-    rows = own.shape[0] // requests
-
-    def kernel(own_ref, arrived_ref, residual_ref, gain_ref, *rest):
-        out = rest[-1]
-        projected = own_ref[...] + arrived_ref[...].astype(jnp.float32)
-        inv_rms = lax.rsqrt(jnp.mean(projected * projected, axis=-1, keepdims=True) + norm_eps)
-        out[0] = (residual_ref[0].astype(jnp.float32) + gain_ref[...] * projected * inv_rms).astype(jnp.bfloat16)
-
-    some = pl.BlockSpec((rows, width), lambda i: (i, 0))
+    rows = own[0].shape[0] // requests
+    columns = width // pieces
+    summed = [a + b.astype(jnp.float32) for a, b in zip(own[:-1], arrived[:-1])]
+
+    def kernel(*refs):
+        arrived_ref, residual_ref, gain_ref = refs[pieces : pieces + 3]
+        out = refs[-1]
+        projected = [ref[...] for ref in refs[0:pieces]]
+        projected[-1] += arrived_ref[...].astype(jnp.float32)
+        squares = sum(jnp.sum(x * x, axis=-1, keepdims=True) for x in projected)
+        inv_rms = lax.rsqrt(squares / width + norm_eps)
+        for i, x in enumerate(projected):
+            here = slice(i * columns, (i + 1) * columns)
+            mixed = residual_ref[0, :, here].astype(jnp.float32) + gain_ref[:, here] * x * inv_rms
+            out[0, :, here] = mixed.astype(jnp.bfloat16)
+
+    some = pl.BlockSpec((rows, columns), lambda i: (i, 0))
     place = pl.BlockSpec((1, rows, width), lambda i: (i, chunk, 0))
-    operands = [own, arrived, residual, gain.reshape(1, width)]
-    specs = [some, some, place, pl.BlockSpec((1, width), lambda i: (0, 0))]
+    operands = [*summed, own[-1], arrived[-1], residual, gain.reshape(1, width)]
+    specs = [some] * (pieces + 1) + [place, pl.BlockSpec((1, width), lambda i: (0, 0))]
     if earlier is not None:
         operands.append(earlier)
         specs.append(pl.BlockSpec(memory_space=pl.ANY))
@@ -245,8 +307,8 @@
         in_specs=specs,
         out_specs=place,
         out_shape=jax.ShapeDtypeStruct(residual.shape, jnp.bfloat16),
-        input_output_aliases={} if earlier is None else {4: 0},
-        compiler_params=kernel_params(16),
+        input_output_aliases={} if earlier is None else {len(operands) - 1: 0},
+        compiler_params=kernel_params(8),
         cost_estimate=pl.CostEstimate(flops=0, bytes_accessed=4 * mib, transcendentals=0),
         name="finish",
     )(*operands)
@@ -277,18 +339,29 @@
     exchange = functools.partial(lax.all_to_all, axis_name="blk", split_axis=0, concat_axis=0, tiled=True)
     message = pack_first(pool_keys, pool_values, new_keys, new_values, queries)
     message = exchange(message.reshape(blk_count, pages + 3, per_req, head_dim))
-    asked = [None]
-    for chunk in range(1, chunks):
-        packed = pack_queries(queries, kv_here, chunk)
-        asked.append(exchange(packed.reshape((blk_count,) + packed.shape[2:])))
-    other = lax.ppermute(message[:, 0:pages], "blk", [(i, i ^ 1) for i in range(blk_count)])
-    mixed_out = None
-    for chunk in range(chunks):
-        attended = attend(core, page_table, cache_len, message, other, asked[chunk], chunk, pages, shares, group)
-        own, theirs = project(place, exchange(attended), weight, shares)
-        arrived = lax.ppermute(theirs, "head", [(0, 1), (1, 0)])
-        mixed_out = finish(own, arrived, residual, post_gain, chunk, mixed_out)
-    return mixed_out
+    packed = pack_queries(queries, kv_here, 1)
+    message, packed = lax.optimization_barrier((message, packed))
+    asked = exchange(packed.reshape((blk_count,) + packed.shape[2:]))
+    other = lax.ppermute(message, "blk", [(i, i ^ 1) for i in range(blk_count)])
+    attend_chunk = functools.partial(attend, core, page_table, cache_len, message, other, pages=pages, shares=shares, group=group)
+
+    def project_piece(gathered, piece):
+        own, theirs = project(place, gathered, weight, shares, piece)
+        return own, lax.ppermute(theirs, "head", [(0, 1), (1, 0)])
+
+    first = attend_chunk(None, 0)
+    first, asked = lax.optimization_barrier((first, asked))
+    first = exchange(first)
+    second = attend_chunk(asked, 1)
+    first, second = lax.optimization_barrier((first, second))
+    second = exchange(second)
+    own, arrived = zip(*[project_piece(first, piece) for piece in range(pieces)])
+    own, second = lax.optimization_barrier((own, second))
+    begun = project_piece(second, 0)
+    mixed_out = finish(own, arrived, residual, post_gain, 0, None)
+    second, mixed_out = lax.optimization_barrier((second, mixed_out))
+    own, arrived = zip(begun, *[project_piece(second, piece) for piece in range(1, pieces)])
+    return finish(own, arrived, residual, post_gain, 1, mixed_out)
 
 
 def group_pages(page_count, page_len):

time: 156 us -> 149 us (0.955)
  blocking collectives: 65.7 us -> 0 us
  waiting for transfers between devices: 24 us -> 65.7 us
  starting transfers between devices: 16.8 us -> 34 us
  local copies, waits for them, and re-layouts: 17.2 us -> 1.78 us
  Pallas kernels: 31.4 us -> 46.1 us
    all_to_all x1 -> x0, blocking collectives: 65.7 us -> none  [by_heads(): message = exchange(message.reshape(blk_count, pages + 3, per_req, head_dim))]
    all_to_all x3 -> x4, waiting for transfers between devices: 11.5 us -> 58.1 us  [the longest x1 48.1 us: by_heads(): message = exchange(message.reshape(blk_count, pages + 3, per_req, head_dim))]
    all_to_all x3 -> x4, starting transfers between devices: 12.9 us -> 28.4 us  [the longest x1 12.8 us: by_heads(): asked = exchange(packed.reshape((blk_count,) + packed.shape[2:]))]
    unnamed x20 -> x14, local copies, waits for them, and re-layouts: 16.2 us -> 1.76 us
    pallas_call x3 -> x5, Pallas kernels: 9.05 us -> 21.5 us  [the longest x4 18.4 us: project(): pl.pallas_call(functools.partial(project_kernel, shares, piece * columns)...]
    ppermute x3 -> x5, waiting for transfers between devices: 12.5 us -> 7.59 us  [the longest x4 7.59 us: project_piece(): return (own, lax.ppermute(theirs, 'head', [(0, 1), (1, 0)]))]
    pallas_call x2, Pallas kernels: 17.8 us -> 20.2 us  [attend(): pl.pallas_call(functools.partial(attend_kernel, pages, chunk, shares), in...]
    ppermute x3 -> x5, starting transfers between devices: 3.88 us -> 5.57 us  [the longest x4 4.8 us: project_piece(): return (own, lax.ppermute(theirs, 'head', [(0, 1), (1, 0)]))]
  transfers between devices with their start and end apart: 6 -> 9, of which waited for: 5 -> 6; matrix products, arithmetic and copies ran while one was open for 0% -> 0% of each run, Pallas kernels for 18% -> 28%
where the time goes in v3:
time: 149 us; the launch traced here: 148 us
  waiting for transfers between devices  65.7 us (44%)
  Pallas kernels  46.1 us (31%)
  starting transfers between devices  34 us (23%)
  local copies, waits for them, and re-layouts  1.78 us (1%)
    all_to_all x1, waiting for transfers between devices, by_heads(): message = exchange(message.reshape(blk_count, pages + 3, per_req, head_dim))  48.1 us
    pallas_call x2, Pallas kernels, attend(): pl.pallas_call(functools.partial(attend_kernel, pages, chunk, shares), in...  20.2 us
    pallas_call x4, Pallas kernels, project(): pl.pallas_call(functools.partial(project_kernel, shares, piece * columns)...  18.4 us
    all_to_all x1, starting transfers between devices, by_heads(): asked = exchange(packed.reshape((blk_count,) + packed.shape[2:]))  12.8 us
    ppermute x4, waiting for transfers between devices, project_piece(): return (own, lax.ppermute(theirs, 'head', [(0, 1), (1, 0)]))  7.59 us
    all_to_all x1, starting transfers between devices, by_heads(): message = exchange(message.reshape(blk_count, pages + 3, per_req, head_dim))  7.37 us
    ppermute x4, starting transfers between devices, project_piece(): return (own, lax.ppermute(theirs, 'head', [(0, 1), (1, 0)]))  4.8 us
    all_to_all x1, waiting for transfers between devices, by_heads(): asked = exchange(packed.reshape((blk_count,) + packed.shape[2:]))  4.36 us
  transfers between devices with their start and end apart: 9, of which 6 were waited for; matrix products, arithmetic and copies ran while one was open for 0% of the time, Pallas kernels for 28%

profile of v3, /device:TPU:0, one launch (start us, length us, event | category | flops | bytes accessed | tf_op | source)
XLA Modules:
  0.0 148.0 jit_solution(16299379769657374959)
XLA Ops:
  0.0 3.2 %pack_first.1 = bf16[8,2,5,128,128]{4,3,2,1,0:T(8,128)(2,1)} custom-call(bf16[2,128,8,128]{3,2,1,0:T(8,128)(2,1)} %pool_k.1, bf16[2,128,8,128]{3,2,1,0:T(8,128)(2,1)} %pool_v.1, bf16[2,128,8,128]{3,2,1,0:T(8,128)(2,1)} %new_k.1, bf16[2,128,8,128]{3,2,1,0:T(8,128)(2,1)} %new_v.1, bf16[2,2,2,32,16,128]{5,4,3,2,1,0:T(8,128)(2,1)} %bitcast.11), custom_call_target="tpu_custom_call" | custom-call | bytes 6291456 | tf_op jit(solution)/shard_map/pack_first/pallas_call | solution.py:80
  3.2 7.4 %all-to-all-start = ((bf16[16,5,128,128]{3,2,1,0:T(8,128)(2,1)}), bf16[16,5,128,128]{3,2,1,0:T(8,128)(2,1)S(1)}, u32[]{:S(2)}, u32[]{:S(2)}) async-start(bf16[16,5,128,128]{3,2,1,0:T(8,128)(2,1)} %bitcast.10), calls=%async_computation | async-start | bytes 5242880 | tf_op jit(solution)/shard_map/all_to_all | solution.py:341
  10.5 0.0 copy-start.3
  10.6 0.0 copy-start.4
  10.6 2.1 %pack_queries.1 = bf16[8,2,1,128,128]{4,3,2,1,0:T(8,128)(2,1)} custom-call(bf16[2,2,2,32,16,128]{5,4,3,2,1,0:T(8,128)(2,1)} %bitcast.12), custom_call_target="tpu_custom_call" | custom-call | bytes 1048576 | tf_op jit(solution)/shard_map/pack_queries/pallas_call | solution.py:109
  12.6 48.1 %all-to-all-done.message = bf16[16,5,128,128]{3,2,1,0:T(8,128)(2,1)S(1)} async-done(((bf16[16,5,128,128]{3,2,1,0:T(8,128)(2,1)}), bf16[16,5,128,128]{3,2,1,0:T(8,128)(2,1)S(1)}, u32[]{:S(2)}, u32[]{:S(2)}) %all-to-all-start) | async-done | bytes 2621472 | tf_op jit(solution)/shard_map/all_to_all | solution.py:341
  60.8 0.8 collective-permute-start
  61.5 12.8 %all-to-all-start.1 = ((bf16[16,1,128,128]{3,2,1,0:T(8,128)(2,1)}), bf16[16,1,128,128]{3,2,1,0:T(8,128)(2,1)S(1)}, u32[]{:S(2)}, u32[]{:S(2)}) async-start(bf16[16,1,128,128]{3,2,1,0:T(8,128)(2,1)} %bitcast.4), calls=%async_computation.1 | async-start | bytes 1048576 | tf_op jit(solution)/shard_map/all_to_all | solution.py:344
  74.4 0.0 collective-permute-done.other
  74.4 10.0 %attend.2 = bf16[16,64,256]{2,1,0:T(8,128)(2,1)} custom-call(s32[1]{0:T(128)} %bitcast.1.core_ref, s32[2,16]{1,0:T(2,128)S(1)} %copy-done.3, s32[2]{0:T(128)S(1)} %copy-done.4, bf16[16,5,128,128]{3,2,1,0:T(8,128)(2,1)S(1)} %all-to-all-done.message, bf16[16,5,128,128]{3,2,1,0:T(8,128)(2,1)} %collective-permute-done.other), custom_call_target="tpu_custom_call" | custom-call | flops 6442450944 | bytes 8388608 | tf_op jit(solution)/shard_map/attend/pallas_call | solution.py:208
  84.5 4.4 %all-to-all-done.1.rest_0_ = bf16[16,1,128,128]{3,2,1,0:T(8,128)(2,1)S(1)} async-done(((bf16[16,1,128,128]{3,2,1,0:T(8,128)(2,1)}), bf16[16,1,128,128]{3,2,1,0:T(8,128)(2,1)S(1)}, u32[]{:S(2)}, u32[]{:S(2)}) %all-to-all-start.1) | async-done | bytes 524320 | tf_op jit(solution)/shard_map/all_to_all | solution.py:344
  88.9 4.1 %all-to-all-start.2 = ((bf16[16,64,256]{2,1,0:T(8,128)(2,1)}), bf16[16,64,256]{2,1,0:T(8,128)(2,1)S(1)}, u32[]{:S(2)}, u32[]{:S(2)}) async-start(bf16[16,64,256]{2,1,0:T(8,128)(2,1)} %attend.2), calls=%async_computation.2 | async-start | bytes 1048576 | tf_op jit(solution)/shard_map/all_to_all | solution.py:354
  93.0 1.7 %copy-done.2 = bf16[16,5,128,128]{3,2,1,0:T(8,128)(2,1)S(1)} copy-done((bf16[16,5,128,128]{3,2,1,0:T(8,128)(2,1)S(1)}, bf16[16,5,128,128]{3,2,1,0:T(8,128)(2,1)}, u32[]{:S(2)}) %copy-start.2) | copy-done | bytes 2621464
  94.7 10.2 %attend.3 = bf16[16,64,256]{2,1,0:T(8,128)(2,1)} custom-call(s32[1]{0:T(128)} %bitcast.1.core_ref, s32[2,16]{1,0:T(2,128)S(1)} %copy-done.3, s32[2]{0:T(128)S(1)} %copy-done.4, bf16[16,5,128,128]{3,2,1,0:T(8,128)(2,1)S(1)} %copy-done.2, bf16[16,5,128,128]{3,2,1,0:T(8,128)(2,1)} %collective-permute-done.other, bf16[16,1,128,128]{3,2,1,0:T(8,128)(2,1)} %copy-done.5), custom_call_target="tpu_custom_call" | custom-call | flops 6442450944 | bytes 8388608 | tf_op jit(solution)/shard_map/attend/pallas_call | solution.py:208
  104.9 2.5 %all-to-all-done.2.attended = bf16[16,64,256]{2,1,0:T(8,128)(2,1)S(1)} async-done(((bf16[16,64,256]{2,1,0:T(8,128)(2,1)}), bf16[16,64,256]{2,1,0:T(8,128)(2,1)S(1)}, u32[]{:S(2)}, u32[]{:S(2)}) %all-to-all-start.2) | async-done | bytes 524320 | tf_op jit(solution)/shard_map/all_to_all | solution.py:354
  107.4 4.1 %all-to-all-start.3 = ((bf16[16,64,256]{2,1,0:T(8,128)(2,1)}), bf16[16,64,256]{2,1,0:T(8,128)(2,1)S(1)}, u32[]{:S(2)}, u32[]{:S(2)}) async-start(bf16[16,64,256]{2,1,0:T(8,128)(2,1)} %attend.3), calls=%async_computation.3 | async-start | bytes 1048576 | tf_op jit(solution)/shard_map/all_to_all | solution.py:357
  111.6 0.0 copy-start.6
  111.6 4.6 %project.4 = (f32[64,2304]{1,0:T(8,128)S(1)}, bf16[64,2304]{1,0:T(8,128)(2,1)S(1)}) custom-call(s32[1]{0:T(128)} %bitcast.place_ref, bf16[16,64,256]{2,1,0:T(8,128)(2,1)S(1)} %all-to-all-done.2.attended, bf16[2048,4608]{1,0:T(8,128)(2,1)} %bitcast.6), custom_call_target="tpu_custom_call" | custom-call | flops 1207959552 | bytes 9437184 | tf_op jit(solution)/shard_map/project/pallas_call | solution.py:260
  116.2 1.6 %collective-permute-start.2 = (bf16[64,2304]{1,0:T(8,128)(2,1)S(1)}, bf16[64,2304]{1,0:T(8,128)(2,1)S(1)}, u32[]{:S(2)}, u32[]{:S(2)}) collective-permute-start(bf16[64,2304]{1,0:T(8,128)(2,1)S(1)} %get-tuple-element.36), channel_id=1, source_target_pairs={{0,1},{1,0},{2,3},{3,2},{4,5},{5,4},{6,7},{7,6},{8,9},{9,8},{10,11... | collective-permute-start | bytes 884744 | tf_op jit(solution)/shard_map/ppermute | solution.py:350
  117.8 4.6 %project.5 = (f32[64,2304]{1,0:T(8,128)S(1)}, bf16[64,2304]{1,0:T(8,128)(2,1)S(1)}) custom-call(s32[1]{0:T(128)} %bitcast.place_ref, bf16[16,64,256]{2,1,0:T(8,128)(2,1)S(1)} %all-to-all-done.2.attended, bf16[2048,4608]{1,0:T(8,128)(2,1)} %bitcast.7), custom_call_target="tpu_custom_call" | custom-call | flops 1207959552 | bytes 9437184 | tf_op jit(solution)/shard_map/project/pallas_call | solution.py:260
  122.4 0.5 collective-permute-start.3
  122.9 3.1 %all-to-all-done.3.attended = bf16[16,64,256]{2,1,0:T(8,128)(2,1)S(1)} async-done(((bf16[16,64,256]{2,1,0:T(8,128)(2,1)}), bf16[16,64,256]{2,1,0:T(8,128)(2,1)S(1)}, u32[]{:S(2)}, u32[]{:S(2)}) %all-to-all-start.3) | async-done | bytes 524320 | tf_op jit(solution)/shard_map/all_to_all | solution.py:357
  126.0 4.7 %project.6 = (f32[64,2304]{1,0:T(8,128)S(1)}, bf16[64,2304]{1,0:T(8,128)(2,1)S(1)}) custom-call(s32[1]{0:T(128)} %bitcast.place_ref, bf16[16,64,256]{2,1,0:T(8,128)(2,1)S(1)} %all-to-all-done.3.attended, bf16[2048,4608]{1,0:T(8,128)(2,1)} %bitcast.8), custom_call_target="tpu_custom_call" | custom-call | flops 1207959552 | bytes 9437184 | tf_op jit(solution)/shard_map/project/pallas_call | solution.py:260
  130.7 1.6 %collective-permute-start.1 = (bf16[64,2304]{1,0:T(8,128)(2,1)S(1)}, bf16[64,2304]{1,0:T(8,128)(2,1)S(1)}, u32[]{:S(2)}, u32[]{:S(2)}) collective-permute-start(bf16[64,2304]{1,0:T(8,128)(2,1)S(1)} %get-tuple-element.34), channel_id=1, source_target_pairs={{0,1},{1,0},{2,3},{3,2},{4,5},{5,4},{6,7},{7,6},{8,9},{9,8},{10,11... | collective-permute-start | bytes 884744 | tf_op jit(solution)/shard_map/ppermute | solution.py:350
  132.3 0.1 convert_add_fusion.refs_0_
  132.3 1.2 finish.2.refs_5_
  133.5 4.6 %project.7 = (f32[64,2304]{1,0:T(8,128)S(1)}, bf16[64,2304]{1,0:T(8,128)(2,1)S(1)}) custom-call(s32[1]{0:T(128)} %bitcast.place_ref, bf16[16,64,256]{2,1,0:T(8,128)(2,1)S(1)} %all-to-all-done.3.attended, bf16[2048,4608]{1,0:T(8,128)(2,1)} %bitcast.9), custom_call_target="tpu_custom_call" | custom-call | flops 1207959552 | bytes 9437184 | tf_op jit(solution)/shard_map/project/pallas_call | solution.py:260
  138.1 1.1 collective-permute-start.4
  139.2 0.5 collective-permute-done.1
  139.7 0.1 convert_add_fusion.1.refs_0_
  139.7 7.1 %collective-permute-done.4.refs_2_ = bf16[64,2304]{1,0:T(8,128)(2,1)S(1)} collective-permute-done((bf16[64,2304]{1,0:T(8,128)(2,1)S(1)}, bf16[64,2304]{1,0:T(8,128)(2,1)S(1)}, u32[]{:S(2)}, u32[]{:S(2)}) %collective-permute-start.4) | collective-permute-done | bytes 294944 | tf_op jit(solution)/shard_map/ppermute | solution.py:350
  146.8 1.1 finish.3
  (13 shorter events, 0.0 us)
Async XLA Ops:
  3.2 57.6 %all-to-all-start = ((bf16[16,5,128,128]{3,2,1,0:T(8,128)(2,1)}), bf16[16,5,128,128]{3,2,1,0:T(8,128)(2,1)S(1)}, u32[]{:S(2)}, u32[]{:S(2)}) async-start(bf16[16,5,128,128]{3,2,1,0:T(8,128)(2,1)} %bitcast.10), calls=%async_computation | async-start | bytes 5242880 | tf_op jit(solution)/shard_map/all_to_all | solution.py:341
  10.5 63.9 %copy-start.3 = (s32[2,16]{1,0:T(2,128)S(1)}, s32[2,16]{1,0:T(2,128)}, u32[]{:S(2)}) copy-start(s32[2,16]{1,0:T(2,128)} %table_ref.3) | copy-start | bytes 388
  10.6 63.9 %copy-start.4 = (s32[2]{0:T(128)S(1)}, s32[2]{0:T(128)}, u32[]{:S(2)}) copy-start(s32[2]{0:T(128)} %len_ref.3) | copy-start | bytes 28
  60.8 23.7 %copy-start.1 = (bf16[16,5,128,128]{3,2,1,0:T(8,128)(2,1)}, bf16[16,5,128,128]{3,2,1,0:T(8,128)(2,1)S(1)}, u32[]{:S(2)}) copy-start(bf16[16,5,128,128]{3,2,1,0:T(8,128)(2,1)S(1)} %all-to-all-done.message) | copy-start | bytes 7864324
  60.8 13.6 %collective-permute-start = (bf16[16,5,128,128]{3,2,1,0:T(8,128)(2,1)S(1)}, bf16[16,5,128,128]{3,2,1,0:T(8,128)(2,1)}, u32[]{:S(2)}, u32[]{:S(2)}) collective-permute-start(bf16[16,5,128,128]{3,2,1,0:T(8,128)(2,1)S(1)} %all-to-all-done.message), channel_id=1, source_target_pairs={{0,2},{2,0},{4,6},{6,4},{8,10},{10,8},{12,14},{14,12},{16,18},{18,... | collective-permute-start | bytes 7864328 | tf_op jit(solution)/shard_map/ppermute | solution.py:345
  61.5 27.3 %all-to-all-start.1 = ((bf16[16,1,128,128]{3,2,1,0:T(8,128)(2,1)}), bf16[16,1,128,128]{3,2,1,0:T(8,128)(2,1)S(1)}, u32[]{:S(2)}, u32[]{:S(2)}) async-start(bf16[16,1,128,128]{3,2,1,0:T(8,128)(2,1)} %bitcast.4), calls=%async_computation.1 | async-start | bytes 1048576 | tf_op jit(solution)/shard_map/all_to_all | solution.py:344
  88.9 4.1 %copy-start.5 = (bf16[16,1,128,128]{3,2,1,0:T(8,128)(2,1)}, bf16[16,1,128,128]{3,2,1,0:T(8,128)(2,1)S(1)}, u32[]{:S(2)}) copy-start(bf16[16,1,128,128]{3,2,1,0:T(8,128)(2,1)S(1)} %all-to-all-done.1.rest_0_) | copy-start | bytes 1572868
  88.9 18.6 %all-to-all-start.2 = ((bf16[16,64,256]{2,1,0:T(8,128)(2,1)}), bf16[16,64,256]{2,1,0:T(8,128)(2,1)S(1)}, u32[]{:S(2)}, u32[]{:S(2)}) async-start(bf16[16,64,256]{2,1,0:T(8,128)(2,1)} %attend.2), calls=%async_computation.2 | async-start | bytes 1048576 | tf_op jit(solution)/shard_map/all_to_all | solution.py:354
  93.0 1.7 %copy-start.2 = (bf16[16,5,128,128]{3,2,1,0:T(8,128)(2,1)S(1)}, bf16[16,5,128,128]{3,2,1,0:T(8,128)(2,1)}, u32[]{:S(2)}) copy-start(bf16[16,5,128,128]{3,2,1,0:T(8,128)(2,1)} %copy-done.1) | copy-start | bytes 7864324
  107.4 18.6 %all-to-all-start.3 = ((bf16[16,64,256]{2,1,0:T(8,128)(2,1)}), bf16[16,64,256]{2,1,0:T(8,128)(2,1)S(1)}, u32[]{:S(2)}, u32[]{:S(2)}) async-start(bf16[16,64,256]{2,1,0:T(8,128)(2,1)} %attend.3), calls=%async_computation.3 | async-start | bytes 1048576 | tf_op jit(solution)/shard_map/all_to_all | solution.py:357
  111.6 6.2 %copy-start.6 = (f32[4608]{0:T(1024)S(1)}, f32[4608]{0:T(1024)}, u32[]{:S(2)}) copy-start(f32[4608]{0:T(1024)} %param.19) | copy-start | bytes 55300
  116.2 16.1 %collective-permute-start.2 = (bf16[64,2304]{1,0:T(8,128)(2,1)S(1)}, bf16[64,2304]{1,0:T(8,128)(2,1)S(1)}, u32[]{:S(2)}, u32[]{:S(2)}) collective-permute-start(bf16[64,2304]{1,0:T(8,128)(2,1)S(1)} %get-tuple-element.36), channel_id=1, source_target_pairs={{0,1},{1,0},{2,3},{3,2},{4,5},{5,4},{6,7},{7,6},{8,9},{9,8},{10,11... | collective-permute-start | bytes 884744 | tf_op jit(solution)/shard_map/ppermute | solution.py:350
  122.4 9.9 %collective-permute-start.3 = (bf16[64,2304]{1,0:T(8,128)(2,1)S(1)}, bf16[64,2304]{1,0:T(8,128)(2,1)S(1)}, u32[]{:S(2)}, u32[]{:S(2)}) collective-permute-start(bf16[64,2304]{1,0:T(8,128)(2,1)S(1)} %get-tuple-element.38), channel_id=1, source_target_pairs={{0,1},{1,0},{2,3},{3,2},{4,5},{5,4},{6,7},{7,6},{8,9},{9,8},{10,11... | collective-permute-start | bytes 884744 | tf_op jit(solution)/shard_map/ppermute | solution.py:350
  126.0 6.3 %copy-start = (bf16[2,64,4608]{2,1,0:T(8,128)(2,1)S(1)}, bf16[2,64,4608]{2,1,0:T(8,128)(2,1)}, u32[]{:S(2)}) copy-start(bf16[2,64,4608]{2,1,0:T(8,128)(2,1)} %refs_3_.3) | copy-start | bytes 3538948
  130.7 9.0 %collective-permute-start.1 = (bf16[64,2304]{1,0:T(8,128)(2,1)S(1)}, bf16[64,2304]{1,0:T(8,128)(2,1)S(1)}, u32[]{:S(2)}, u32[]{:S(2)}) collective-permute-start(bf16[64,2304]{1,0:T(8,128)(2,1)S(1)} %get-tuple-element.34), channel_id=1, source_target_pairs={{0,1},{1,0},{2,3},{3,2},{4,5},{5,4},{6,7},{7,6},{8,9},{9,8},{10,11... | collective-permute-start | bytes 884744 | tf_op jit(solution)/shard_map/ppermute | solution.py:350
  138.1 8.7 %collective-permute-start.4 = (bf16[64,2304]{1,0:T(8,128)(2,1)S(1)}, bf16[64,2304]{1,0:T(8,128)(2,1)S(1)}, u32[]{:S(2)}, u32[]{:S(2)}) collective-permute-start(bf16[64,2304]{1,0:T(8,128)(2,1)S(1)} %get-tuple-element.41), channel_id=1, source_target_pairs={{0,1},{1,0},{2,3},{3,2},{4,5},{5,4},{6,7},{7,6},{8,9},{9,8},{10,11... | collective-permute-start | bytes 884744 | tf_op jit(solution)/shard_map/ppermute | solution.py:350

commit v4 on v3

--- a/solution.py
+++ b/solution.py
@@ -11,8 +11,6 @@
 score_scale = 144.0 ** (-0.5)
 norm_eps = 1e-06
 log2_e = 1.4426950408889634
-chunks = 2
-pieces = 2
 key_tile = 256
 mib = 1024 * 1024
 in_vmem = pl.BlockSpec(memory_space=pltpu.VMEM)
@@ -31,27 +29,28 @@
         yield head, staged[pl.ds(head, rows, stride=heads), :].astype(jnp.bfloat16)
 
 
-def pack_first_kernel(pool_k, pool_v, new_k, new_v, queries, out, held_kv, held_q, made, staged, in_sem, out_sem):
-    pages = pool_k.shape[0]
-    cores = new_k.shape[0]
-    _, shares, _, rows, heads, head_dim = queries.shape
+def pack_kernel(share_ref, *refs):
+    *caches, queries, out, held_kv, held_q, made, staged, in_sem, out_sem = refs
+    cores, _, rows, heads, head_dim = queries.shape
     group = heads // out.shape[0]
     tasks = []
-    for core, pool in enumerate((pool_k, pool_v)):
-        tasks += [(pool.at[page], core, page) for page in range(pages)]
-    for part, new in enumerate((new_k, new_v)):
-        tasks += [(new.at[core], core, pages + part) for core in range(cores)]
+    if caches:
+        pool_k, pool_v, new_k, new_v = caches
+        pages = pool_k.shape[0]
+        for core, pool in enumerate((pool_k, pool_v)):
+            tasks += [(pool.at[page], core, page) for page in range(pages)]
+        for part, new in enumerate((new_k, new_v)):
+            tasks += [(new.at[core], core, pages + part) for core in range(cores)]
     arrivals = [pltpu.make_async_copy(source, held_kv.at[i], in_sem.at[i]) for i, (source, _, _) in enumerate(tasks)]
     for core in range(cores):
-        at = len(tasks) + core
-        arrivals.append(pltpu.make_async_copy(queries.at[core, :, 0], held_q.at[core], in_sem.at[at]))
+        source = queries.at[core, share_ref[0]]
+        arrivals.append(pltpu.make_async_copy(source, held_q.at[core], in_sem.at[len(tasks) + core]))
     for arrival in arrivals:
         arrival.start()
     leaving = []
 
     def leave(core, part):
-        here = made.at[:, core, part]
-        leaving.append(pltpu.make_async_copy(here, out.at[:, core, part], out_sem.at[len(leaving)]))
+        leaving.append(pltpu.make_async_copy(made.at[:, core, part], out.at[:, core, part], out_sem.at[len(leaving)]))
         leaving[-1].start()
 
     for i, (_, core, part) in enumerate(tasks):
@@ -59,67 +58,46 @@
         for head, picked in split_heads(held_kv[i], staged.at[i % 2]):
             made[head, core, part] = picked
         leave(core, part)
+    last = out.shape[2] - 1
     for core in range(cores):
         arrivals[len(tasks) + core].wait()
-        source = held_q[core].reshape(shares * rows, heads, head_dim)
-        for head, picked in split_heads(source, staged.at[core % 2]):
-            first = head % group * shares * rows
-            made[head // group, core, pages + 2, first : first + shares * rows, :] = picked
-        leave(core, pages + 2)
+        for head, picked in split_heads(held_q[core], staged.at[core % 2]):
+            first = head % group * rows
+            made[head // group, core, last, first : first + rows, :] = picked
+        leave(core, last)
     for copy in leaving:
         copy.wait()
 
 
-def pack_first(pool_keys, pool_values, new_keys, new_values, queries):
-    cores, rows, kv_heads, head_dim = new_keys.shape
-    pages = pool_keys.shape[0]
-    parts = pages + 3
-    _, shares, _, chunk_rows, heads, _ = queries.shape
-    pieces = 2 * pages + 2 * cores
-    sources = [pltpu.with_memory_space_constraint(x, pltpu.HBM) for x in (pool_keys, pool_values, new_keys, new_values, queries)]
+def pack(share, queries, kv_heads, caches=()):
+    cores, _, rows, heads, head_dim = queries.shape
+    group = heads // kv_heads
+    parts, pieces, page_rows = 1, 0, group * rows
+    if caches:
+        pages = caches[0].shape[0]
+        parts, pieces = pages + 3, 2 * pages + 2 * cores
+    shape = (kv_heads, cores, parts, page_rows, head_dim)
+    operands = [pltpu.with_memory_space_constraint(x, pltpu.HBM) for x in (*caches, queries)]
     return pl.pallas_call(
-        pack_first_kernel,
-        in_specs=[in_hbm] * 5,
+        pack_kernel,
+        in_specs=[in_smem] + [in_hbm] * len(operands),
         out_specs=in_hbm,
-        out_shape=pltpu.HBM((kv_heads, cores, parts, rows, head_dim), jnp.bfloat16),
+        out_shape=pltpu.HBM(shape, jnp.bfloat16),
         scratch_shapes=[
-            pltpu.VMEM((pieces, rows, kv_heads, head_dim), jnp.bfloat16),
-            pltpu.VMEM((cores, shares, chunk_rows, heads, head_dim), jnp.bfloat16),
-            pltpu.VMEM((kv_heads, cores, parts, rows, head_dim), jnp.bfloat16),
-            pltpu.VMEM((2, max(rows * kv_heads, shares * chunk_rows * heads), head_dim), jnp.float32),
+            pltpu.VMEM((max(pieces, 1), page_rows, kv_heads, head_dim), jnp.bfloat16),
+            pltpu.VMEM((cores, rows, heads, head_dim), jnp.bfloat16),
+            pltpu.VMEM(shape, jnp.bfloat16),
+            pltpu.VMEM((2, rows * heads, head_dim), jnp.float32),
             pltpu.SemaphoreType.DMA((pieces + cores,)),
             pltpu.SemaphoreType.DMA((pieces + cores,)),
         ],
-        compiler_params=kernel_params(10),
-        cost_estimate=pl.CostEstimate(flops=0, bytes_accessed=6 * mib, transcendentals=0),
-        name="pack_first",
-    )(*sources)
-
-
-def pack_queries(queries, kv_heads, chunk):
-    steps, shares, _, rows, heads, head_dim = queries.shape
-    group = heads // kv_heads
-
-    def kernel(some_queries, out, staged):
-        source = some_queries[...].reshape(shares * rows, heads, head_dim)
-        for head, picked in split_heads(source, staged):
-            first = head % group * shares * rows
-            out[head // group, 0, 0, first : first + shares * rows, :] = picked
-
-    return pl.pallas_call(
-        kernel,
-        grid=(steps,),
-        in_specs=[pl.BlockSpec((1, shares, 1, rows, heads, head_dim), lambda i: (i, 0, chunk, 0, 0, 0))],
-        out_specs=pl.BlockSpec((kv_heads, 1, 1, group * shares * rows, head_dim), lambda i: (0, i, 0, 0, 0)),
-        out_shape=jax.ShapeDtypeStruct((kv_heads, steps, 1, group * shares * rows, head_dim), jnp.bfloat16),
-        scratch_shapes=[pltpu.VMEM((shares * rows * heads, head_dim), jnp.float32)],
-        compiler_params=kernel_params(6),
-        cost_estimate=pl.CostEstimate(flops=0, bytes_accessed=mib, transcendentals=0),
-        name="pack_queries",
-    )(pltpu.with_memory_space_constraint(queries, pltpu.HBM))
-
-
-def attend_kernel(pages, chunk, shares, core_ref, table_ref, len_ref, message, other, *rest):
+        compiler_params=kernel_params(12 if caches else 6),
+        cost_estimate=pl.CostEstimate(flops=0, bytes_accessed=parts * mib, transcendentals=0),
+        name="pack_cache" if caches else "pack_queries",
+    )(share, *operands)
+
+
+def attend_kernel(pages, core_ref, share_ref, table_ref, len_ref, message, other, *rest):
     out, cache_k, cache_v, new_v, total, made, held, others, in_sem, other_sem, out_sem = rest[-11:]
     fetch = pltpu.make_async_copy(other.at[:, 0:pages], others, other_sem)
     fetch.start()
@@ -131,7 +109,8 @@
     blocks, _, page_rows, head_dim = message.shape
     slots = table_ref.shape[1]
     group = out.shape[2] // head_dim
-    block_rows = out.shape[1] * group
+    per_head = out.shape[1]
+    block_rows = per_head * group
     core = core_ref[0]
     cached = len_ref[core]
     for block in range(blocks):
@@ -158,9 +137,7 @@
         weights = jnp.exp2((soft_cap * log2_e) * jnp.tanh(scores * (score_scale / soft_cap)))
         if causal:
             row = lax.broadcasted_iota(jnp.int32, weights.shape, 0)
-            in_chunk = block_rows // (group * shares)
-            offset = row // block_rows * page_rows + row // in_chunk % shares * (page_rows // shares)
-            offset += chunk * in_chunk + row % in_chunk
+            offset = row // block_rows * page_rows + row % per_head + share_ref[0] * per_head
             weights = jnp.where(lax.broadcasted_iota(jnp.int32, weights.shape, 1) <= offset, weights, 0.0)
         product = jnp.dot(weights.astype(jnp.bfloat16), values, preferred_element_type=jnp.float32)
         here = pl.ds(first_block * block_rows, rows)
@@ -180,7 +157,6 @@
             count = min(half, blocks - later)
             add(later, count, keys, values)
             later += count
-    per_head = block_rows // group
     copies = []
     for block in range(blocks):
         here = pl.ds(block * block_rows, block_rows)
@@ -195,18 +171,18 @@
         copy.wait()
 
 
-def attend(core, page_table, cache_len, message, other, queries, chunk, *, pages, shares, group):
+def attend(core, page_table, cache_len, message, other, queries, share, *, pages, group):
     blocks, _, page_rows, head_dim = message.shape
     slots = page_table.shape[1]
-    block_rows = page_rows * group // chunks
+    block_rows = page_rows
     operands = [message, pltpu.with_memory_space_constraint(other, pltpu.HBM)]
-    specs = [in_smem] * 3 + [in_vmem, in_hbm]
+    specs = [in_smem] * 4 + [in_vmem, in_hbm]
     if queries is not None:
         operands.append(pltpu.with_memory_space_constraint(queries, pltpu.HBM))
         specs.append(in_hbm)
     seen = blocks * block_rows * (slots + blocks // 2) * page_rows
     return pl.pallas_call(
-        functools.partial(attend_kernel, pages, chunk, shares),
+        functools.partial(attend_kernel, pages),
         in_specs=specs,
         out_specs=in_hbm,
         out_shape=pltpu.HBM((blocks, block_rows // group, group * head_dim), jnp.bfloat16),
@@ -225,93 +201,104 @@
         compiler_params=kernel_params(12),
         cost_estimate=pl.CostEstimate(flops=8 * seen * head_dim, bytes_accessed=8 * mib, transcendentals=2 * seen),
         name="attend",
-    )(core, page_table, cache_len, *operands)
-
-
-def project_kernel(shares, begin, place_ref, attended, weight, own, theirs, rows, held, sem):
+    )(core, share, page_table, cache_len, *operands)
+
+
+def project_kernel(begin, attended, weight, *refs):
+    (*arrived, out), (rows, held, sem) = refs[:-3], refs[-3:]
+    if arrived:
+        *arrived, out, squares_out = (*arrived, out)
     tiles, _, tile = held.shape
     arrivals = []
     for i in range(tiles):
         columns = pl.ds(begin + i * tile, tile)
         arrivals.append(pltpu.make_async_copy(weight.at[:, columns], held.at[i], sem.at[i]))
         arrivals[-1].start()
-    place = place_ref[0]
-    sources, share_rows, features = attended.shape
-    requests = 2
-    count = share_rows // shares
+    sources, count, features = attended.shape
+    requests = rows.shape[0] // count
     for source in range(sources):
-        first = source // requests * features
-        for share in range(shares):
-            at = pl.multiple_of((share ^ place) * (requests * count), requests * count) + source % requests * count
-            rows[pl.ds(at, count), first : first + features] = attended[source, share * count : (share + 1) * count, :]
+        at, first = source % requests * count, source // requests * features
+        rows[at : at + count, first : first + features] = attended[source]
+    squares = 0.0
     for i in range(tiles):
+        here = slice(i * tile, (i + 1) * tile)
         arrivals[i].wait()
         product = jnp.dot(rows[...], held[i], preferred_element_type=jnp.float32)
-        own[:, i * tile : (i + 1) * tile] = product[0 : requests * count, :]
-        theirs[:, i * tile : (i + 1) * tile] = product[requests * count :, :].astype(jnp.bfloat16)
-
-
-def project(place, attended, weight, shares, piece):
-    sources, share_rows, features = attended.shape
-    depth, width = weight.shape
-    columns = width // pieces
-    tile = columns // 3
-    rows = 2 * share_rows
+        at = i * tile
+        for piece in arrived:
+            if 0 <= at < piece.shape[1]:
+                product += piece[:, at : at + tile].astype(jnp.float32)
+                squares += squares_by_lane(product)
+            at -= piece.shape[1]
+        out[:, here] = product.astype(out.dtype)
+    if arrived:
+        squares_out[...] = squares
+
+
+def squares_by_lane(x):
+    return sum(x[:, i : i + 128] * x[:, i : i + 128] for i in range(0, x.shape[1], 128))
+
+
+def project(attended, weight, requests, begin, columns, tile, dtype, arrived=()):
+    sources, count, features = attended.shape
+    depth = weight.shape[0]
+    rows = requests * count
+    operands = [attended, pltpu.with_memory_space_constraint(weight, pltpu.HBM)]
+    outs = [jax.ShapeDtypeStruct((rows, columns), dtype)]
+    if arrived:
+        operands += arrived
+        outs.append(jax.ShapeDtypeStruct((rows, 128), jnp.float32))
     return pl.pallas_call(
-        functools.partial(project_kernel, shares, piece * columns),
-        in_specs=[in_smem, in_vmem, in_hbm],
-        out_specs=[in_vmem, in_vmem],
-        out_shape=[
-            jax.ShapeDtypeStruct((rows // shares, columns), jnp.float32),
-            jax.ShapeDtypeStruct((rows // shares, columns), jnp.bfloat16),
-        ],
+        functools.partial(project_kernel, begin),
+        in_specs=[in_vmem, in_hbm] + [in_vmem] * (len(operands) - 2),
+        out_specs=[in_vmem] * len(outs),
+        out_shape=outs,
         scratch_shapes=[
             pltpu.VMEM((rows, depth), jnp.bfloat16),
             pltpu.VMEM((columns // tile, depth, tile), jnp.bfloat16),
             pltpu.SemaphoreType.DMA((columns // tile,)),
         ],
-        compiler_params=kernel_params(16),
+        compiler_params=kernel_params(6 + 2 * depth * columns // mib),
         cost_estimate=pl.CostEstimate(flops=2 * rows * depth * columns, bytes_accessed=2 * depth * columns, transcendentals=0),
         name="project",
-    )(place, attended, pltpu.with_memory_space_constraint(weight, pltpu.HBM))
-
-
-def finish(own, arrived, residual, gain, chunk, earlier):
-    requests, per_req, width = residual.shape
-    rows = own[0].shape[0] // requests
-    columns = width // pieces
-    summed = [a + b.astype(jnp.float32) for a, b in zip(own[:-1], arrived[:-1])]
-
-    def kernel(*refs):
-        arrived_ref, residual_ref, gain_ref = refs[pieces : pieces + 3]
-        out = refs[-1]
-        projected = [ref[...] for ref in refs[0:pieces]]
-        projected[-1] += arrived_ref[...].astype(jnp.float32)
-        squares = sum(jnp.sum(x * x, axis=-1, keepdims=True) for x in projected)
+    )(*operands)
+
+
+def finish_kernel(projected, squares_ref, arrived, residual, gain, out, made, sem):
+    requests, count, width = residual.shape
+    rows = made.shape[1]
+    split = width - arrived.shape[1]
+    copies = []
+    for step in range(made.shape[0]):
+        request, first = step * rows // count, step * rows % count
+        here = slice(step * rows, (step + 1) * rows)
+        place = slice(first, first + rows)
+        last = projected[here, split:] + arrived[here, :].astype(jnp.float32)
+        squares = jnp.sum(squares_ref[here, :] + squares_by_lane(last), axis=-1, keepdims=True)
         inv_rms = lax.rsqrt(squares / width + norm_eps)
-        for i, x in enumerate(projected):
-            here = slice(i * columns, (i + 1) * columns)
-            mixed = residual_ref[0, :, here].astype(jnp.float32) + gain_ref[:, here] * x * inv_rms
-            out[0, :, here] = mixed.astype(jnp.bfloat16)
-
-    some = pl.BlockSpec((rows, columns), lambda i: (i, 0))
-    place = pl.BlockSpec((1, rows, width), lambda i: (i, chunk, 0))
-    operands = [*summed, own[-1], arrived[-1], residual, gain.reshape(1, width)]
-    specs = [some] * (pieces + 1) + [place, pl.BlockSpec((1, width), lambda i: (0, 0))]
-    if earlier is not None:
-        operands.append(earlier)
-        specs.append(pl.BlockSpec(memory_space=pl.ANY))
+        for columns, x in ((slice(0, split), projected[here, 0:split]), (slice(split, width), last)):
+            mixed = residual[request, place, columns].astype(jnp.float32) + gain[:, columns] * x * inv_rms
+            made[step, :, columns] = mixed.astype(jnp.bfloat16)
+        copies.append(pltpu.make_async_copy(made.at[step], out.at[request, place], sem.at[step]))
+        copies[-1].start()
+    for copy in copies:
+        copy.wait()
+
+
+def finish(projected, squares, arrived, residual, gain):
+    requests, count, width = residual.shape
+    rows = 32
+    steps = requests * count // rows
     return pl.pallas_call(
-        kernel,
-        grid=(requests,),
-        in_specs=specs,
-        out_specs=place,
-        out_shape=jax.ShapeDtypeStruct(residual.shape, jnp.bfloat16),
-        input_output_aliases={} if earlier is None else {len(operands) - 1: 0},
-        compiler_params=kernel_params(8),
-        cost_estimate=pl.CostEstimate(flops=0, bytes_accessed=4 * mib, transcendentals=0),
+        finish_kernel,
+        in_specs=[in_vmem] * 5,
+        out_specs=in_hbm,
+        out_shape=pltpu.HBM(residual.shape, jnp.bfloat16),
+        scratch_shapes=[pltpu.VMEM((steps, rows, width), jnp.bfloat16), pltpu.SemaphoreType.DMA((steps,))],
+        compiler_params=kernel_params(12),
+        cost_estimate=pl.CostEstimate(flops=0, bytes_accessed=6 * mib, transcendentals=0),
         name="finish",
-    )(*operands)
+    )(projected, squares, arrived, residual, gain.reshape(1, width))
 
 
 def by_heads(
@@ -333,35 +320,41 @@
     shares = lax.axis_size("head")
     group = heads_here // kv_here
     core = (lax.axis_index("blk") % 2)[None]
-    place = lax.axis_index("head")[None]
-    weight = out_weight.reshape(heads_here * head_dim, out_weight.shape[2])
-    queries = queries.reshape(req_count, shares, chunks, per_req // (shares * chunks), heads_here, head_dim)
+    mine = lax.axis_index("head")[None]
+    theirs = 1 - mine
+    width = out_weight.shape[2]
+    weight = out_weight.reshape(heads_here * head_dim, width)
+    queries = queries.reshape(req_count, shares, per_req // shares, heads_here, head_dim)
     exchange = functools.partial(lax.all_to_all, axis_name="blk", split_axis=0, concat_axis=0, tiled=True)
-    message = pack_first(pool_keys, pool_values, new_keys, new_values, queries)
-    message = exchange(message.reshape(blk_count, pages + 3, per_req, head_dim))
-    packed = pack_queries(queries, kv_here, 1)
+    message = pack(theirs, queries, kv_here, (pool_keys, pool_values, new_keys, new_values))
+    message = exchange(message.reshape((blk_count,) + message.shape[2:]))
+    packed = pack(mine, queries, kv_here)
     message, packed = lax.optimization_barrier((message, packed))
     asked = exchange(packed.reshape((blk_count,) + packed.shape[2:]))
     other = lax.ppermute(message, "blk", [(i, i ^ 1) for i in range(blk_count)])
-    attend_chunk = functools.partial(attend, core, page_table, cache_len, message, other, pages=pages, shares=shares, group=group)
-
-    def project_piece(gathered, piece):
-        own, theirs = project(place, gathered, weight, shares, piece)
-        return own, lax.ppermute(theirs, "head", [(0, 1), (1, 0)])
-
-    first = attend_chunk(None, 0)
+    attend_share = functools.partial(attend, core, page_table, cache_len, message, other, pages=pages, group=group)
+
+    first = attend_share(None, theirs)
     first, asked = lax.optimization_barrier((first, asked))
     first = exchange(first)
-    second = attend_chunk(asked, 1)
+    second = attend_share(asked, mine)
     first, second = lax.optimization_barrier((first, second))
-    second = exchange(second)
-    own, arrived = zip(*[project_piece(first, piece) for piece in range(pieces)])
-    own, second = lax.optimization_barrier((own, second))
-    begun = project_piece(second, 0)
-    mixed_out = finish(own, arrived, residual, post_gain, 0, None)
-    second, mixed_out = lax.optimization_barrier((second, mixed_out))
-    own, arrived = zip(begun, *[project_piece(second, piece) for piece in range(1, pieces)])
-    return finish(own, arrived, residual, post_gain, 1, mixed_out)
+    tile = width // 9
+    begin = 0
+    arrived = []
+    for piece, tiles in enumerate((2, 3, 4)):
+        if piece == 2:
+            first, arrived[0] = lax.optimization_barrier((first, arrived[0]))
+        (sent,) = project(first, weight, req_count, begin, tiles * tile, tile, jnp.bfloat16)
+        begin += tiles * tile
+        if piece == 0:
+            sent, second = lax.optimization_barrier((sent, second))
+            second = exchange(second)
+        else:
+            first, sent = lax.optimization_barrier((first, sent))
+        arrived.append(lax.ppermute(sent, "head", [(0, 1), (1, 0)]))
+    projected, squares = project(second, weight, req_count, 0, width, tile, jnp.float32, arrived[:2])
+    return finish(projected, squares, arrived[2], residual, post_gain)
 
 
 def group_pages(page_count, page_len):

time: 149 us -> 146 us (0.980)
  Pallas kernels: 46.1 us -> 43.9 us
    all_to_all x1, waiting for transfers between devices: 3.09 us -> 0.01 us  [by_heads(): second = exchange(second)]
    ppermute x4 -> x3, waiting for transfers between devices: 7.59 us -> 10.1 us  [by_heads(): arrived.append(lax.ppermute(sent, 'head', [(0, 1), (1, 0)]))]
    pallas_call x10 -> x9, Pallas kernels: 46.1 us -> 43.9 us  [the longest x2 20.1 us: attend(): pl.pallas_call(functools.partial(attend_kernel, pages), in_specs=specs, o...]
    all_to_all x1, waiting for transfers between devices: 2.53 us -> 4.3 us  [by_heads(): first = exchange(first)]
    ppermute x4 -> x3, starting transfers between devices: 4.8 us -> 3.74 us  [by_heads(): arrived.append(lax.ppermute(sent, 'head', [(0, 1), (1, 0)]))]
  transfers between devices with their start and end apart: 9 -> 8, of which waited for: 6 -> 6; matrix products, arithmetic and copies ran while one was open for 0% -> 0% of each run, Pallas kernels for 28% -> 25%
where the time goes in v4:
time: 146 us; the launch traced here: 145 us
  waiting for transfers between devices  67 us (46%)
  Pallas kernels  43.9 us (30%)
  starting transfers between devices  33 us (23%)
    all_to_all x1, waiting for transfers between devices, by_heads(): message = exchange(message.reshape((blk_count,) + message.shape[2:]))  48.1 us
    pallas_call x2, Pallas kernels, attend(): pl.pallas_call(functools.partial(attend_kernel, pages), in_specs=specs, o...  20.1 us
    pallas_call x4, Pallas kernels, project(): pl.pallas_call(functools.partial(project_kernel, begin), in_specs=[in_vme...  17.2 us
    all_to_all x1, starting transfers between devices, by_heads(): asked = exchange(packed.reshape((blk_count,) + packed.shape[2:]))  12.8 us
    ppermute x3, waiting for transfers between devices, by_heads(): arrived.append(lax.ppermute(sent, 'head', [(0, 1), (1, 0)]))  10.1 us
    all_to_all x1, starting transfers between devices, by_heads(): message = exchange(message.reshape((blk_count,) + message.shape[2:]))  7.37 us
    pallas_call x2, Pallas kernels, pack(): pl.pallas_call(pack_kernel, in_specs=[in_smem] + [in_hbm] * len(operands)...  5.2 us
    all_to_all x1, waiting for transfers between devices, by_heads(): asked = exchange(packed.reshape((blk_count,) + packed.shape[2:]))  4.43 us
  transfers between devices with their start and end apart: 8, of which 6 were waited for; matrix products, arithmetic and copies ran while one was open for 0% of the time, Pallas kernels for 25%

profile of v4, /device:TPU:0, one launch (start us, length us, event | category | flops | bytes accessed | tf_op | source)
XLA Modules:
  0.0 145.0 jit_solution(568163690486506852)
XLA Ops:
  0.0 3.1 %pack_cache.1 = bf16[8,2,5,128,128]{4,3,2,1,0:T(8,128)(2,1)} custom-call(s32[1]{0:T(128)S(6)} %sub.3.share_ref, bf16[2,128,8,128]{3,2,1,0:T(8,128)(2,1)} %refs_0_.1, bf16[2,128,8,128]{3,2,1,0:T(8,128)(2,1)} %refs_1_.1, bf16[2,128,8,128]{3,2,1,0:T(8,128)(2,1)} %refs_2_.1, bf16[2,128,8,128]{3,2,1,0:T(8,128)(2,1)} %refs_3_.1, bf16[2,2,64,16,128]{4,3,2,1,0:T(8,128)(2,1)} %bitcast.11), custom_call_target="tpu_custom_call" | custom-call | bytes 5242880 | tf_op jit(solution)/shard_map/pack_cache/pallas_call | solution.py:81
  3.1 7.4 %all-to-all-start = ((bf16[16,5,128,128]{3,2,1,0:T(8,128)(2,1)}), bf16[16,5,128,128]{3,2,1,0:T(8,128)(2,1)S(1)}, u32[]{:S(2)}, u32[]{:S(2)}) async-start(bf16[16,5,128,128]{3,2,1,0:T(8,128)(2,1)} %bitcast.10), calls=%async_computation | async-start | bytes 5242880 | tf_op jit(solution)/shard_map/all_to_all | solution.py:330
  10.5 0.0 copy-start.1
  10.5 0.0 copy-start.2
  10.5 2.1 %pack_queries.1 = bf16[8,2,1,128,128]{4,3,2,1,0:T(8,128)(2,1)} custom-call(s32[1]{0:T(128)} %bitcast.1.share_ref, bf16[2,2,64,16,128]{4,3,2,1,0:T(8,128)(2,1)} %bitcast.12), custom_call_target="tpu_custom_call" | custom-call | bytes 1048576 | tf_op jit(solution)/shard_map/pack_queries/pallas_call | solution.py:81
  12.6 48.1 %all-to-all-done.message = bf16[16,5,128,128]{3,2,1,0:T(8,128)(2,1)S(1)} async-done(((bf16[16,5,128,128]{3,2,1,0:T(8,128)(2,1)}), bf16[16,5,128,128]{3,2,1,0:T(8,128)(2,1)S(1)}, u32[]{:S(2)}, u32[]{:S(2)}) %all-to-all-start) | async-done | bytes 2621472 | tf_op jit(solution)/shard_map/all_to_all | solution.py:330
  60.7 0.8 collective-permute-start
  61.5 12.8 %all-to-all-start.1 = ((bf16[16,1,128,128]{3,2,1,0:T(8,128)(2,1)}), bf16[16,1,128,128]{3,2,1,0:T(8,128)(2,1)S(1)}, u32[]{:S(2)}, u32[]{:S(2)}) async-start(bf16[16,1,128,128]{3,2,1,0:T(8,128)(2,1)} %bitcast.13), calls=%async_computation.1 | async-start | bytes 1048576 | tf_op jit(solution)/shard_map/all_to_all | solution.py:333
  74.4 0.0 collective-permute-done.other
  74.4 0.0 copy-done.1
  74.4 10.0 %attend.2 = bf16[16,64,256]{2,1,0:T(8,128)(2,1)} custom-call(s32[1]{0:T(128)} %bitcast.core_ref, s32[1]{0:T(128)S(6)} %sub.3.share_ref, s32[2,16]{1,0:T(2,128)S(1)} %copy-done.1, s32[2]{0:T(128)S(1)} %copy-done.2, bf16[16,5,128,128]{3,2,1,0:T(8,128)(2,1)S(1)} %all-to-all-done.message, bf16[16,5,128,128]{3,2,1,0:T(8,128)(2,1)} %collective-permute-done.other), custom_call_target="tpu_custom_call" | custom-call | flops 6442450944 | bytes 8388608 | tf_op jit(solution)/shard_map/attend/pallas_call | solution.py:184
  84.4 4.4 %all-to-all-done.1.rest_0_ = bf16[16,1,128,128]{3,2,1,0:T(8,128)(2,1)S(1)} async-done(((bf16[16,1,128,128]{3,2,1,0:T(8,128)(2,1)}), bf16[16,1,128,128]{3,2,1,0:T(8,128)(2,1)S(1)}, u32[]{:S(2)}, u32[]{:S(2)}) %all-to-all-start.1) | async-done | bytes 524320 | tf_op jit(solution)/shard_map/all_to_all | solution.py:333
  88.8 0.8 copy-done.3
  89.6 4.1 %all-to-all-start.2 = ((bf16[16,64,256]{2,1,0:T(8,128)(2,1)}), bf16[16,64,256]{2,1,0:T(8,128)(2,1)S(1)}, u32[]{:S(2)}, u32[]{:S(2)}) async-start(bf16[16,64,256]{2,1,0:T(8,128)(2,1)} %attend.2), calls=%async_computation.2 | async-start | bytes 1048576 | tf_op jit(solution)/shard_map/all_to_all | solution.py:339
  93.7 10.2 %attend.3 = bf16[16,64,256]{2,1,0:T(8,128)(2,1)} custom-call(s32[1]{0:T(128)} %bitcast.core_ref, s32[1]{0:T(128)} %bitcast.1.share_ref, s32[2,16]{1,0:T(2,128)S(1)} %copy-done.1, s32[2]{0:T(128)S(1)} %copy-done.2, bf16[16,5,128,128]{3,2,1,0:T(8,128)(2,1)S(1)} %all-to-all-done.message, bf16[16,5,128,128]{3,2,1,0:T(8,128)(2,1)} %collective-permute-done.other, ...), custom_call_target="tpu_custom_call" | custom-call | flops 6442450944 | bytes 8388608 | tf_op jit(solution)/shard_map/attend/pallas_call | solution.py:184
  103.9 4.3 %all-to-all-done.2.attended = bf16[16,64,256]{2,1,0:T(8,128)(2,1)S(1)} async-done(((bf16[16,64,256]{2,1,0:T(8,128)(2,1)}), bf16[16,64,256]{2,1,0:T(8,128)(2,1)S(1)}, u32[]{:S(2)}, u32[]{:S(2)}) %all-to-all-start.2) | async-done | bytes 524320 | tf_op jit(solution)/shard_map/all_to_all | solution.py:339
  108.2 2.7 %project.4 = bf16[128,1024]{1,0:T(8,128)(2,1)S(1)} custom-call(bf16[16,64,256]{2,1,0:T(8,128)(2,1)S(1)} %all-to-all-done.2.attended, bf16[2048,4608]{1,0:T(8,128)(2,1)} %bitcast.6), custom_call_target="tpu_custom_call" | custom-call | flops 536870912 | bytes 4194304 | tf_op jit(solution)/shard_map/project/pallas_call | solution.py:251
  110.9 4.1 %all-to-all-start.3 = ((bf16[16,64,256]{2,1,0:T(8,128)(2,1)}), bf16[16,64,256]{2,1,0:T(8,128)(2,1)S(1)}, u32[]{:S(2)}, u32[]{:S(2)}) async-start(bf16[16,64,256]{2,1,0:T(8,128)(2,1)} %attend.3), calls=%async_computation.3 | async-start | bytes 1048576 | tf_op jit(solution)/shard_map/all_to_all | solution.py:352
  115.0 1.6 %collective-permute-start.1 = (bf16[128,1024]{1,0:T(8,128)(2,1)S(1)}, bf16[128,1024]{1,0:T(8,128)(2,1)S(1)}, u32[]{:S(2)}, u32[]{:S(2)}) collective-permute-start(bf16[128,1024]{1,0:T(8,128)(2,1)S(1)} %project.4), channel_id=1, source_target_pairs={{0,1},{1,0},{2,3},{3,2},{4,5},{5,4},{6,7},{7,6},{8,9},{9,8},{10,11... | collective-permute-start | bytes 786440 | tf_op jit(solution)/shard_map/ppermute | solution.py:355
  116.6 3.4 %project.5 = bf16[128,1536]{1,0:T(8,128)(2,1)S(1)} custom-call(bf16[16,64,256]{2,1,0:T(8,128)(2,1)S(1)} %all-to-all-done.2.attended, bf16[2048,4608]{1,0:T(8,128)(2,1)} %bitcast.7), custom_call_target="tpu_custom_call" | custom-call | flops 805306368 | bytes 6291456 | tf_op jit(solution)/shard_map/project/pallas_call | solution.py:251
  120.0 0.0 copy-start.4
  120.0 0.6 collective-permute-start.2
  120.6 3.6 %collective-permute-done.1.refs_0_ = bf16[128,1024]{1,0:T(8,128)(2,1)S(1)} collective-permute-done((bf16[128,1024]{1,0:T(8,128)(2,1)S(1)}, bf16[128,1024]{1,0:T(8,128)(2,1)S(1)}, u32[]{:S(2)}, u32[]{:S(2)}) %collective-permute-start.1) | collective-permute-done | bytes 262176 | tf_op jit(solution)/shard_map/ppermute | solution.py:355
  124.2 4.0 %project.7 = bf16[128,2048]{1,0:T(8,128)(2,1)S(1)} custom-call(bf16[16,64,256]{2,1,0:T(8,128)(2,1)S(1)} %all-to-all-done.2.attended, bf16[2048,4608]{1,0:T(8,128)(2,1)} %bitcast.8), custom_call_target="tpu_custom_call" | custom-call | flops 1073741824 | bytes 8388608 | tf_op jit(solution)/shard_map/project/pallas_call | solution.py:251
  128.2 1.6 %collective-permute-start.3 = (bf16[128,2048]{1,0:T(8,128)(2,1)S(1)}, bf16[128,2048]{1,0:T(8,128)(2,1)S(1)}, u32[]{:S(2)}, u32[]{:S(2)}) collective-permute-start(bf16[128,2048]{1,0:T(8,128)(2,1)S(1)} %project.7), channel_id=1, source_target_pairs={{0,1},{1,0},{2,3},{3,2},{4,5},{5,4},{6,7},{7,6},{8,9},{9,8},{10,11... | collective-permute-start | bytes 1572872 | tf_op jit(solution)/shard_map/ppermute | solution.py:355
  129.8 0.0 copy-start
  129.8 2.8 %collective-permute-done.2.refs_1_ = bf16[128,1536]{1,0:T(8,128)(2,1)S(1)} collective-permute-done((bf16[128,1536]{1,0:T(8,128)(2,1)S(1)}, bf16[128,1536]{1,0:T(8,128)(2,1)S(1)}, u32[]{:S(2)}, u32[]{:S(2)}) %collective-permute-start.2) | collective-permute-done | bytes 393248 | tf_op jit(solution)/shard_map/ppermute | solution.py:355
  132.6 0.0 all-to-all-done.3.attended
  132.7 7.1 %project.6 = (f32[128,4608]{1,0:T(8,128)S(1)}, f32[128,128]{1,0:T(8,128)S(1)}) custom-call(bf16[16,64,256]{2,1,0:T(8,128)(2,1)S(1)} %all-to-all-done.3.attended, bf16[2048,4608]{1,0:T(8,128)(2,1)} %bitcast.9, bf16[128,1024]{1,0:T(8,128)(2,1)S(1)} %collective-permute-done.1.refs_0_, bf16[128,1536]{1,0:T(8,128)(2,1)S(1)} %collective-permute-done.2.refs_1_), custom_call_target="tpu_custom_call" | custom-call | flops 2415919104 | bytes 18874368 | tf_op jit(solution)/shard_map/project/pallas_call | solution.py:251
  139.8 3.6 %collective-permute-done.3.arrived = bf16[128,2048]{1,0:T(8,128)(2,1)S(1)} collective-permute-done((bf16[128,2048]{1,0:T(8,128)(2,1)S(1)}, bf16[128,2048]{1,0:T(8,128)(2,1)S(1)}, u32[]{:S(2)}, u32[]{:S(2)}) %collective-permute-start.3) | collective-permute-done | bytes 524320 | tf_op jit(solution)/shard_map/ppermute | solution.py:355
  143.4 0.0 copy-done
  143.4 1.4 finish.1
  (4 shorter events, 0.0 us)
Async XLA Ops:
  3.1 57.6 %all-to-all-start = ((bf16[16,5,128,128]{3,2,1,0:T(8,128)(2,1)}), bf16[16,5,128,128]{3,2,1,0:T(8,128)(2,1)S(1)}, u32[]{:S(2)}, u32[]{:S(2)}) async-start(bf16[16,5,128,128]{3,2,1,0:T(8,128)(2,1)} %bitcast.10), calls=%async_computation | async-start | bytes 5242880 | tf_op jit(solution)/shard_map/all_to_all | solution.py:330
  10.5 63.9 %copy-start.1 = (s32[2,16]{1,0:T(2,128)S(1)}, s32[2,16]{1,0:T(2,128)}, u32[]{:S(2)}) copy-start(s32[2,16]{1,0:T(2,128)} %table_ref.3) | copy-start | bytes 388
  10.5 63.9 %copy-start.2 = (s32[2]{0:T(128)S(1)}, s32[2]{0:T(128)}, u32[]{:S(2)}) copy-start(s32[2]{0:T(128)} %len_ref.3) | copy-start | bytes 28
  60.7 13.6 %collective-permute-start = (bf16[16,5,128,128]{3,2,1,0:T(8,128)(2,1)S(1)}, bf16[16,5,128,128]{3,2,1,0:T(8,128)(2,1)}, u32[]{:S(2)}, u32[]{:S(2)}) collective-permute-start(bf16[16,5,128,128]{3,2,1,0:T(8,128)(2,1)S(1)} %all-to-all-done.message), channel_id=1, source_target_pairs={{0,2},{2,0},{4,6},{6,4},{8,10},{10,8},{12,14},{14,12},{16,18},{18,... | collective-permute-start | bytes 7864328 | tf_op jit(solution)/shard_map/ppermute | solution.py:334
  61.5 27.3 %all-to-all-start.1 = ((bf16[16,1,128,128]{3,2,1,0:T(8,128)(2,1)}), bf16[16,1,128,128]{3,2,1,0:T(8,128)(2,1)S(1)}, u32[]{:S(2)}, u32[]{:S(2)}) async-start(bf16[16,1,128,128]{3,2,1,0:T(8,128)(2,1)} %bitcast.13), calls=%async_computation.1 | async-start | bytes 1048576 | tf_op jit(solution)/shard_map/all_to_all | solution.py:333
  88.8 0.8 copy-start.3
  89.6 18.6 %all-to-all-start.2 = ((bf16[16,64,256]{2,1,0:T(8,128)(2,1)}), bf16[16,64,256]{2,1,0:T(8,128)(2,1)S(1)}, u32[]{:S(2)}, u32[]{:S(2)}) async-start(bf16[16,64,256]{2,1,0:T(8,128)(2,1)} %attend.2), calls=%async_computation.2 | async-start | bytes 1048576 | tf_op jit(solution)/shard_map/all_to_all | solution.py:339
  110.9 21.7 %all-to-all-start.3 = ((bf16[16,64,256]{2,1,0:T(8,128)(2,1)}), bf16[16,64,256]{2,1,0:T(8,128)(2,1)S(1)}, u32[]{:S(2)}, u32[]{:S(2)}) async-start(bf16[16,64,256]{2,1,0:T(8,128)(2,1)} %attend.3), calls=%async_computation.3 | async-start | bytes 1048576 | tf_op jit(solution)/shard_map/all_to_all | solution.py:352
  115.0 9.2 %collective-permute-start.1 = (bf16[128,1024]{1,0:T(8,128)(2,1)S(1)}, bf16[128,1024]{1,0:T(8,128)(2,1)S(1)}, u32[]{:S(2)}, u32[]{:S(2)}) collective-permute-start(bf16[128,1024]{1,0:T(8,128)(2,1)S(1)} %project.4), channel_id=1, source_target_pairs={{0,1},{1,0},{2,3},{3,2},{4,5},{5,4},{6,7},{7,6},{8,9},{9,8},{10,11... | collective-permute-start | bytes 786440 | tf_op jit(solution)/shard_map/ppermute | solution.py:355
  120.0 9.8 %copy-start.4 = (f32[4608]{0:T(1024)S(1)}, f32[4608]{0:T(1024)}, u32[]{:S(2)}) copy-start(f32[4608]{0:T(1024)} %param.19) | copy-start | bytes 55300
  120.0 12.6 %collective-permute-start.2 = (bf16[128,1536]{1,0:T(8,128)(2,1)S(1)}, bf16[128,1536]{1,0:T(8,128)(2,1)S(1)}, u32[]{:S(2)}, u32[]{:S(2)}) collective-permute-start(bf16[128,1536]{1,0:T(8,128)(2,1)S(1)} %project.5), channel_id=1, source_target_pairs={{0,1},{1,0},{2,3},{3,2},{4,5},{5,4},{6,7},{7,6},{8,9},{9,8},{10,11... | collective-permute-start | bytes 1179656 | tf_op jit(solution)/shard_map/ppermute | solution.py:355
  128.2 15.2 %collective-permute-start.3 = (bf16[128,2048]{1,0:T(8,128)(2,1)S(1)}, bf16[128,2048]{1,0:T(8,128)(2,1)S(1)}, u32[]{:S(2)}, u32[]{:S(2)}) collective-permute-start(bf16[128,2048]{1,0:T(8,128)(2,1)S(1)} %project.7), channel_id=1, source_target_pairs={{0,1},{1,0},{2,3},{3,2},{4,5},{5,4},{6,7},{7,6},{8,9},{9,8},{10,11... | collective-permute-start | bytes 1572872 | tf_op jit(solution)/shard_map/ppermute | solution.py:355
  129.8 13.6 %copy-start = (bf16[2,64,4608]{2,1,0:T(8,128)(2,1)S(1)}, bf16[2,64,4608]{2,1,0:T(8,128)(2,1)}, u32[]{:S(2)}) copy-start(bf16[2,64,4608]{2,1,0:T(8,128)(2,1)} %residual.1) | copy-start | bytes 3538948

commit v5 on v4

--- a/solution.py
+++ b/solution.py
@@ -97,21 +97,97 @@
     )(share, *operands)
 
 
-def attend_kernel(pages, core_ref, share_ref, table_ref, len_ref, message, other, *rest):
+def spread_kernel(place_ref, queries, got, keep, send, held, made, staged, sems):
+    core, share, side = place_ref[0], place_ref[1], place_ref[3]
+    own = pltpu.make_async_copy(queries.at[core, share], held.at[core], sems.at[0])
+    other = pltpu.make_async_copy(got, held.at[1 - core], sems.at[1])
+    own.start()
+    other.start()
+    own.wait()
+    other.wait()
+    rows, heads, _ = got.shape
+    group = heads // (2 * made.shape[1])
+    for block in range(2):
+        for head, picked in split_heads(held[block], staged.at[block]):
+            owner, first = head // group, head % group * rows
+            made[owner % 2, owner // 2, block, first : first + rows, :] = picked
+    copies = [
+        pltpu.make_async_copy(made.at[side], keep, sems.at[2]),
+        pltpu.make_async_copy(made.at[1 - side], send, sems.at[3]),
+    ]
+    for copy in copies:
+        copy.start()
+    for copy in copies:
+        copy.wait()
+
+
+def spread(place, queries, got, kv_heads):
+    rows, heads, head_dim = got.shape
+    shape = (kv_heads // 2, 2, heads // kv_heads * rows, head_dim)
+    return pl.pallas_call(
+        spread_kernel,
+        in_specs=[in_smem, in_hbm, in_hbm],
+        out_specs=[in_hbm, in_hbm],
+        out_shape=[pltpu.HBM(shape, jnp.bfloat16)] * 2,
+        scratch_shapes=[
+            pltpu.VMEM((2, rows, heads, head_dim), jnp.bfloat16),
+            pltpu.VMEM((2,) + shape, jnp.bfloat16),
+            pltpu.VMEM((2, rows * heads, head_dim), jnp.float32),
+            pltpu.SemaphoreType.DMA((4,)),
+        ],
+        compiler_params=kernel_params(6),
+        cost_estimate=pl.CostEstimate(flops=0, bytes_accessed=mib, transcendentals=0),
+        name="spread_queries",
+    )(place, *[pltpu.with_memory_space_constraint(x, pltpu.HBM) for x in (queries, got)])
+
+
+def gather_kernel(place_ref, keep, got, *refs):
+    *outs, sems = refs
+    side, level = place_ref[3], place_ref[2]
+    copies = []
+    for step, out in enumerate(outs):
+        copies.append(pltpu.make_async_copy(keep.at[level ^ step], out.at[side], sems.at[2 * step]))
+        copies.append(pltpu.make_async_copy(got.at[level ^ step], out.at[1 - side], sems.at[2 * step + 1]))
+    for copy in copies:
+        copy.start()
+    for copy in copies:
+        copy.wait()
+
+
+def gather(place, keep, got):
+    levels = keep.shape[0]
+    return pl.pallas_call(
+        gather_kernel,
+        in_specs=[in_smem, in_hbm, in_hbm],
+        out_specs=[in_hbm] * levels,
+        out_shape=[pltpu.HBM((2,) + keep.shape[1:], jnp.bfloat16)] * levels,
+        scratch_shapes=[pltpu.SemaphoreType.DMA((2 * levels,))],
+        compiler_params=kernel_params(1),
+        cost_estimate=pl.CostEstimate(flops=0, bytes_accessed=mib, transcendentals=0),
+        name="gather_queries",
+    )(place, *[pltpu.with_memory_space_constraint(x, pltpu.HBM) for x in (keep, got)])
+
+
+def attend_kernel(pages, own_share, place_ref, table_ref, len_ref, message, other, *rest):
     out, cache_k, cache_v, new_v, total, made, held, others, in_sem, other_sem, out_sem = rest[-11:]
     fetch = pltpu.make_async_copy(other.at[:, 0:pages], others, other_sem)
     fetch.start()
+    share = place_ref[1] if own_share else 1 - place_ref[1]
     queries, query_part = message, pages + 2
-    if len(rest) > 11:
+    arrivals = []
+    if own_share:
         queries, query_part = held, 0
-        arrival = pltpu.make_async_copy(rest[0], held, in_sem)
-        arrival.start()
+        for step, source in enumerate(rest[:-11]):
+            count = source.shape[0]
+            here = pl.ds((place_ref[2] ^ step) * count, count)
+            arrivals.append(pltpu.make_async_copy(source, held.at[here], in_sem.at[step]))
+            arrivals[-1].start()
     blocks, _, page_rows, head_dim = message.shape
     slots = table_ref.shape[1]
     group = out.shape[2] // head_dim
     per_head = out.shape[1]
     block_rows = per_head * group
-    core = core_ref[0]
+    core = place_ref[0]
     cached = len_ref[core]
     for block in range(blocks):
         new_v[block * page_rows : (block + 1) * page_rows, 0:head_dim] = message[block, pages + 1]
@@ -127,7 +203,7 @@
         values = jnp.where(core == 0, theirs, mine).astype(jnp.float32)
         cache_v[here, 0:head_dim] = jnp.where(seen, values, 0.0).astype(jnp.bfloat16)
         cache_v[here, head_dim : 2 * head_dim] = jnp.where(seen, 1.0, 0.0).astype(jnp.bfloat16)
-    if len(rest) > 11:
+    for arrival in arrivals:
         arrival.wait()
 
     def add(first_block, block_count, keys, values, begin=False, causal=False):
@@ -137,7 +213,7 @@
         weights = jnp.exp2((soft_cap * log2_e) * jnp.tanh(scores * (score_scale / soft_cap)))
         if causal:
             row = lax.broadcasted_iota(jnp.int32, weights.shape, 0)
-            offset = row // block_rows * page_rows + row % per_head + share_ref[0] * per_head
+            offset = row // block_rows * page_rows + row % per_head + share * per_head
             weights = jnp.where(lax.broadcasted_iota(jnp.int32, weights.shape, 1) <= offset, weights, 0.0)
         product = jnp.dot(weights.astype(jnp.bfloat16), values, preferred_element_type=jnp.float32)
         here = pl.ds(first_block * block_rows, rows)
@@ -171,18 +247,16 @@
         copy.wait()
 
 
-def attend(core, page_table, cache_len, message, other, queries, share, *, pages, group):
+def attend(place, page_table, cache_len, message, other, queries, *, pages, group):
     blocks, _, page_rows, head_dim = message.shape
     slots = page_table.shape[1]
     block_rows = page_rows
-    operands = [message, pltpu.with_memory_space_constraint(other, pltpu.HBM)]
-    specs = [in_smem] * 4 + [in_vmem, in_hbm]
-    if queries is not None:
-        operands.append(pltpu.with_memory_space_constraint(queries, pltpu.HBM))
-        specs.append(in_hbm)
+    operands = [message, other]
+    operands += [pltpu.with_memory_space_constraint(x, pltpu.HBM) for x in queries]
+    specs = [in_smem] * 3 + [in_vmem, pl.BlockSpec(memory_space=pl.ANY)] + [in_hbm] * len(queries)
     seen = blocks * block_rows * (slots + blocks // 2) * page_rows
     return pl.pallas_call(
-        functools.partial(attend_kernel, pages),
+        functools.partial(attend_kernel, pages, bool(queries)),
         in_specs=specs,
         out_specs=in_hbm,
         out_shape=pltpu.HBM((blocks, block_rows // group, group * head_dim), jnp.bfloat16),
@@ -192,16 +266,16 @@
             pltpu.VMEM((blocks * page_rows, 2 * head_dim), jnp.bfloat16),
             pltpu.VMEM((blocks * block_rows, 2 * head_dim), jnp.float32),
             pltpu.VMEM((blocks, block_rows // group, group * head_dim), jnp.bfloat16),
-            pltpu.VMEM((blocks, 1, block_rows, head_dim) if len(operands) > 2 else (8, 128), jnp.bfloat16),
+            pltpu.VMEM((blocks, 1, block_rows, head_dim) if queries else (8, 128), jnp.bfloat16),
             pltpu.VMEM((blocks, pages, page_rows, head_dim), jnp.bfloat16),
-            pltpu.SemaphoreType.DMA(()),
+            pltpu.SemaphoreType.DMA((max(len(queries), 1),)),
             pltpu.SemaphoreType.DMA(()),
             pltpu.SemaphoreType.DMA((2,)),
         ],
         compiler_params=kernel_params(12),
         cost_estimate=pl.CostEstimate(flops=8 * seen * head_dim, bytes_accessed=8 * mib, transcendentals=2 * seen),
         name="attend",
-    )(core, share, page_table, cache_len, *operands)
+    )(place, page_table, cache_len, *operands)
 
 
 def project_kernel(begin, attended, weight, *refs):
@@ -264,6 +338,18 @@
     )(*operands)
 
 
+def wait_here(x):
+    return pl.pallas_call(
+        lambda *_: None,
+        in_specs=[pl.BlockSpec(memory_space=pl.ANY)],
+        out_specs=pl.BlockSpec(memory_space=pl.ANY),
+        out_shape=jax.ShapeDtypeStruct(x.shape, x.dtype),
+        input_output_aliases={0: 0},
+        cost_estimate=pl.CostEstimate(flops=5000000000, bytes_accessed=0, transcendentals=0),
+        name="wait_here",
+    )(x)
+
+
 def finish_kernel(projected, squares_ref, arrived, residual, gain, out, made, sem):
     requests, count, width = residual.shape
     rows = made.shape[1]
@@ -319,32 +405,40 @@
     blk_count = lax.axis_size("blk")
     shares = lax.axis_size("head")
     group = heads_here // kv_here
-    core = (lax.axis_index("blk") % 2)[None]
-    mine = lax.axis_index("head")[None]
-    theirs = 1 - mine
+    blk = lax.axis_index("blk")
+    core, mine = blk % 2, lax.axis_index("head")
+    place = jnp.stack([core, mine, blk // 4, blk // 2 % 2])
     width = out_weight.shape[2]
     weight = out_weight.reshape(heads_here * head_dim, width)
     queries = queries.reshape(req_count, shares, per_req // shares, heads_here, head_dim)
     exchange = functools.partial(lax.all_to_all, axis_name="blk", split_axis=0, concat_axis=0, tiled=True)
-    message = pack(theirs, queries, kv_here, (pool_keys, pool_values, new_keys, new_values))
+
+    def across(x, bits):
+        return lax.ppermute(x, "blk", [(i, i ^ bits) for i in range(blk_count)])
+
+    message = pack((1 - mine)[None], queries, kv_here, (pool_keys, pool_values, new_keys, new_values))
     message = exchange(message.reshape((blk_count,) + message.shape[2:]))
-    packed = pack(mine, queries, kv_here)
-    message, packed = lax.optimization_barrier((message, packed))
-    asked = exchange(packed.reshape((blk_count,) + packed.shape[2:]))
-    other = lax.ppermute(message, "blk", [(i, i ^ 1) for i in range(blk_count)])
-    attend_share = functools.partial(attend, core, page_table, cache_len, message, other, pages=pages, group=group)
-
-    first = attend_share(None, theirs)
-    first, asked = lax.optimization_barrier((first, asked))
+    got = lax.dynamic_slice(queries, (1 - core, mine, 0, 0, 0), (1, 1) + queries.shape[2:])
+    got = across(got.reshape(queries.shape[2:]), 1)
+    keep, send = spread(place, queries, got, kv_here)
+    asked = gather(place, keep, across(send, 2))
+    message, *asked = lax.optimization_barrier((message, *asked))
+    other = across(message, 1)
+    asked = [across(x, 4 * step) if step else x for step, x in enumerate(asked)]
+    asked = [x.reshape(4, 1, *x.shape[2:]) for x in asked]
+    attend_share = functools.partial(attend, place, page_table, cache_len, message, other, pages=pages, group=group)
+
+    first = attend_share([])
+    first, *asked = lax.optimization_barrier((first, *asked))
     first = exchange(first)
-    second = attend_share(asked, mine)
+    second = attend_share(asked)
     first, second = lax.optimization_barrier((first, second))
     tile = width // 9
     begin = 0
     arrived = []
-    for piece, tiles in enumerate((2, 3, 4)):
+    for piece, tiles in enumerate((3, 3, 3)):
         if piece == 2:
-            first, arrived[0] = lax.optimization_barrier((first, arrived[0]))
+            first, arrived[0] = lax.optimization_barrier((first, wait_here(arrived[0])))
         (sent,) = project(first, weight, req_count, begin, tiles * tile, tile, jnp.bfloat16)
         begin += tiles * tile
         if piece == 0:
@@ -504,7 +598,7 @@
     )
     def one_device(queries, new_keys, *rest):
         requests, per_req = queries.shape[0], queries.shape[1]
-        owners = mesh.shape["blk"] == 2 * new_keys.shape[2] and mesh.shape["head"] == 2 and requests == 2
+        owners = mesh.shape["blk"] == 2 * new_keys.shape[2] == 16 and mesh.shape["head"] == 2 and requests == 2
         fits = rest[1].shape[1] == per_req == 128 and queries.shape[2] == 2 * new_keys.shape[2]
         return (by_heads if owners and fits else shards)(queries, new_keys, *rest)
 

time: 146 us -> 138 us (0.945)
  waiting for transfers between devices: 67 us -> 35.4 us
  Pallas kernels: 43.9 us -> 60.9 us
  local copies, waits for them, and re-layouts: 0.83 us -> 5.92 us
    all_to_all x1, waiting for transfers between devices: 48.1 us -> 3.71 us  [by_heads(): message = exchange(message.reshape((blk_count,) + message.shape[2:]))]
    ppermute x1 -> x6, waiting for transfers between devices: 0.01 us -> 23 us  [across(): return lax.ppermute(x, 'blk', [(i, i ^ bits) for i in range(blk_count)])]
    pallas_call x2 -> x5, Pallas kernels: 20.1 us -> 39.1 us  [the longest x2 18.8 us: attend(): pl.pallas_call(functools.partial(attend_kernel, pages, bool(queries)), in...]
    ppermute x1 -> x6, starting transfers between devices: 0.77 us -> 14.4 us  [across(): return lax.ppermute(x, 'blk', [(i, i ^ bits) for i in range(blk_count)])]
    all_to_all x1 -> x0, starting transfers between devices: 12.8 us -> none  [by_heads(): asked = exchange(packed.reshape((blk_count,) + packed.shape[2:]))]
    all_to_all x1 -> x0, waiting for transfers between devices: 4.43 us -> none  [by_heads(): asked = exchange(packed.reshape((blk_count,) + packed.shape[2:]))]
    ppermute x3, waiting for transfers between devices: 10.1 us -> 5.7 us  [by_heads(): arrived.append(lax.ppermute(sent, 'head', [(0, 1), (1, 0)]))]
    unnamed x10 -> x26, local copies, waits for them, and re-layouts: 0.82 us -> 4.93 us
  transfers between devices with their start and end apart: 8 -> 12, of which waited for: 6 -> 7; matrix products, arithmetic and copies ran while one was open for 0% -> 1% of each run, Pallas kernels for 25% -> 39%
where the time goes in v5:
time: 138 us; the launch traced here: 137 us
  Pallas kernels  60.9 us (44%)
  waiting for transfers between devices  35.4 us (26%)
  starting transfers between devices  34.4 us (25%)
  local copies, waits for them, and re-layouts  5.92 us (4%)
    ppermute x6, waiting for transfers between devices, across(): return lax.ppermute(x, 'blk', [(i, i ^ bits) for i in range(blk_count)])  23 us
    pallas_call x2, Pallas kernels, attend(): pl.pallas_call(functools.partial(attend_kernel, pages, bool(queries)), in...  18.8 us
    pallas_call x1, Pallas kernels, gather(): pl.pallas_call(gather_kernel, in_specs=[in_smem, in_hbm, in_hbm], out_spe...  17.6 us
    pallas_call x4, Pallas kernels, project(): pl.pallas_call(functools.partial(project_kernel, begin), in_specs=[in_vme...  17.2 us
    ppermute x6, starting transfers between devices, across(): return lax.ppermute(x, 'blk', [(i, i ^ bits) for i in range(blk_count)])  14.4 us
    all_to_all x1, starting transfers between devices, by_heads(): message = exchange(message.reshape((blk_count,) + message.shape[2:]))  7.37 us
    ppermute x3, waiting for transfers between devices, by_heads(): arrived.append(lax.ppermute(sent, 'head', [(0, 1), (1, 0)]))  5.7 us
    unnamed x26, local copies, waits for them, and re-layouts  4.93 us
  transfers between devices with their start and end apart: 12, of which 7 were waited for; matrix products, arithmetic and copies ran while one was open for 1% of the time, Pallas kernels for 39%

profile of v5, /device:TPU:0, one launch (start us, length us, event | category | flops | bytes accessed | tf_op | source)
XLA Modules:
  0.0 137.1 jit_solution(5944159682939012538)
XLA Ops:
  0.0 3.2 %pack_cache.1 = bf16[8,2,5,128,128]{4,3,2,1,0:T(8,128)(2,1)} custom-call(s32[1]{0:T(128)} %bitcast.4.share_ref, bf16[2,128,8,128]{3,2,1,0:T(8,128)(2,1)} %refs_0_.1, bf16[2,128,8,128]{3,2,1,0:T(8,128)(2,1)} %refs_1_.1, bf16[2,128,8,128]{3,2,1,0:T(8,128)(2,1)} %refs_2_.1, bf16[2,128,8,128]{3,2,1,0:T(8,128)(2,1)} %refs_3_.1, bf16[2,2,64,16,128]{4,3,2,1,0:T(8,128)(2,1)} %bitcast.19), custom_call_target="tpu_custom_call" | custom-call | bytes 5242880 | tf_op jit(solution)/shard_map/pack_cache/pallas_call | solution.py:81
  3.2 7.4 %all-to-all-start = ((bf16[16,5,128,128]{3,2,1,0:T(8,128)(2,1)}), bf16[16,5,128,128]{3,2,1,0:T(8,128)(2,1)S(1)}, u32[]{:S(2)}, u32[]{:S(2)}) async-start(bf16[16,5,128,128]{3,2,1,0:T(8,128)(2,1)} %bitcast.18), calls=%async_computation | async-start | bytes 5242880 | tf_op jit(solution)/shard_map/all_to_all | solution.py:420
  10.6 1.0 dynamic-slice_bitcast_fusion
  12.1 1.1 collective-permute-done.got
  13.2 0.7 copy-done.7
  13.9 2.8 %spread_queries.1 = (bf16[4,2,128,128]{3,2,1,0:T(8,128)(2,1)}, bf16[4,2,128,128]{3,2,1,0:T(8,128)(2,1)}) custom-call(s32[4]{0:T(128)S(1)} %pad_add_fusion.place_ref, bf16[2,2,64,16,128]{4,3,2,1,0:T(8,128)(2,1)} %bitcast.21, bf16[64,16,128]{2,1,0:T(8,128)(2,1)} %copy-done.7), custom_call_target="tpu_custom_call" | custom-call | bytes 1048576 | tf_op jit(solution)/shard_map/spread_queries/pallas_call | solution.py:127
  16.7 2.0 %collective-permute-start.1 = (bf16[4,2,128,128]{3,2,1,0:T(8,128)(2,1)}, bf16[4,2,128,128]{3,2,1,0:T(8,128)(2,1)S(1)}, u32[]{:S(2)}, u32[]{:S(2)}) collective-permute-start(bf16[4,2,128,128]{3,2,1,0:T(8,128)(2,1)} %get-tuple-element.33), channel_id=1, source_target_pairs={{0,4},{2,6},{4,0},{6,2},{8,12},{10,14},{12,8},{14,10},{16,20},{18,... | collective-permute-start | bytes 786440 | tf_op jit(solution)/shard_map/ppermute | solution.py:417
  18.6 20.2 %collective-permute-done.1.got = bf16[4,2,128,128]{3,2,1,0:T(8,128)(2,1)S(1)} collective-permute-done((bf16[4,2,128,128]{3,2,1,0:T(8,128)(2,1)}, bf16[4,2,128,128]{3,2,1,0:T(8,128)(2,1)S(1)}, u32[]{:S(2)}, u32[]{:S(2)}) %collective-permute-start.1) | collective-permute-done | bytes 262176 | tf_op jit(solution)/shard_map/ppermute | solution.py:417
  38.8 0.7 copy-done.8
  39.5 17.6 %gather_queries.1 = (bf16[2,2,128,128]{3,2,1,0:T(8,128)(2,1)}, bf16[2,2,128,128]{3,2,1,0:T(8,128)(2,1)}, bf16[2,2,128,128]{3,2,1,0:T(8,128)(2,1)}, bf16[2,2,128,128]{3,2,1,0:T(8,128)(2,1)}) custom-call(s32[4]{0:T(128)S(1)} %pad_add_fusion.place_ref, bf16[4,2,128,128]{3,2,1,0:T(8,128)(2,1)} %get-tuple-element.32.keep, bf16[4,2,128,128]{3,2,1,0:T(8,128)(2,1)} %copy-done.8), custom_call_target="tpu_custom_call" | custom-call | bytes 1048576 | tf_op jit(solution)/shard_map/gather_queries/pallas_call | solution.py:159
  57.1 3.7 %all-to-all-done.message = bf16[16,5,128,128]{3,2,1,0:T(8,128)(2,1)S(1)} async-done(((bf16[16,5,128,128]{3,2,1,0:T(8,128)(2,1)}), bf16[16,5,128,128]{3,2,1,0:T(8,128)(2,1)S(1)}, u32[]{:S(2)}, u32[]{:S(2)}) %all-to-all-start) | async-done | bytes 2621472 | tf_op jit(solution)/shard_map/all_to_all | solution.py:420
  60.8 0.8 collective-permute-start.2
  61.6 10.7 %collective-permute-start.4 = (bf16[2,2,128,128]{3,2,1,0:T(8,128)(2,1)}, bf16[2,2,128,128]{3,2,1,0:T(8,128)(2,1)S(1)}, u32[]{:S(2)}, u32[]{:S(2)}) collective-permute-start(bf16[2,2,128,128]{3,2,1,0:T(8,128)(2,1)} %get-tuple-element.41), channel_id=1, source_target_pairs={{0,16},{2,18},{4,20},{6,22},{8,24},{10,26},{12,28},{14,30},{16,0},... | collective-permute-start | bytes 393224 | tf_op jit(solution)/shard_map/ppermute | solution.py:417
  72.9 9.0 %attend.2 = bf16[16,64,256]{2,1,0:T(8,128)(2,1)} custom-call(s32[4]{0:T(128)S(1)} %pad_add_fusion.place_ref, s32[2,16]{1,0:T(2,128)S(1)} %copy-done.5, s32[2]{0:T(128)S(1)} %copy-done.6, bf16[16,5,128,128]{3,2,1,0:T(8,128)(2,1)S(1)} %all-to-all-done.message, bf16[16,5,128,128]{3,2,1,0:T(8,128)(2,1)S(1)} %collective-permute-done.2.other), custom_call_target="tpu_custom_call" | custom-call | flops 6442450944 | bytes 8388608 | tf_op jit(solution)/shard_map/attend/pallas_call | solution.py:258
  81.9 1.7 %collective-permute-done.3 = bf16[2,2,128,128]{3,2,1,0:T(8,128)(2,1)S(1)} collective-permute-done((bf16[2,2,128,128]{3,2,1,0:T(8,128)(2,1)}, bf16[2,2,128,128]{3,2,1,0:T(8,128)(2,1)S(1)}, u32[]{:S(2)}, u32[]{:S(2)}) %collective-permute-start.3) | collective-permute-done | bytes 131104 | tf_op jit(solution)/shard_map/ppermute | solution.py:417
  83.6 4.8 %all-to-all-start.1 = ((bf16[16,64,256]{2,1,0:T(8,128)(2,1)}), bf16[16,64,256]{2,1,0:T(8,128)(2,1)S(1)}, u32[]{:S(2)}, u32[]{:S(2)}) async-start(bf16[16,64,256]{2,1,0:T(8,128)(2,1)} %attend.2), calls=%async_computation.1 | async-start | bytes 1048576 | tf_op jit(solution)/shard_map/all_to_all | solution.py:433
  88.5 1.7 %copy-done.4 = bf16[16,5,128,128]{3,2,1,0:T(8,128)(2,1)S(1)} copy-done((bf16[16,5,128,128]{3,2,1,0:T(8,128)(2,1)S(1)}, bf16[16,5,128,128]{3,2,1,0:T(8,128)(2,1)}, u32[]{:S(2)}) %copy-start.4) | copy-done | bytes 2621464
  90.2 9.7 %attend.3 = bf16[16,64,256]{2,1,0:T(8,128)(2,1)} custom-call(s32[4]{0:T(128)S(1)} %pad_add_fusion.place_ref, s32[2,16]{1,0:T(2,128)S(1)} %copy-done.5, s32[2]{0:T(128)S(1)} %copy-done.6, bf16[16,5,128,128]{3,2,1,0:T(8,128)(2,1)S(1)} %all-to-all-done.message, bf16[16,5,128,128]{3,2,1,0:T(8,128)(2,1)S(1)} %copy-done.4, bf16[4,1,128,128]{3,2,1,0:T(8,128)(2,1)} %bitcast.22, ...), custom_call_target="tpu_custom_call" | custom-call | flops 6442450944 | bytes 8388608 | tf_op jit(solution)/shard_map/attend/pallas_call | solution.py:258
  99.9 2.9 %all-to-all-done.1.attended = bf16[16,64,256]{2,1,0:T(8,128)(2,1)S(1)} async-done(((bf16[16,64,256]{2,1,0:T(8,128)(2,1)}), bf16[16,64,256]{2,1,0:T(8,128)(2,1)S(1)}, u32[]{:S(2)}, u32[]{:S(2)}) %all-to-all-start.1) | async-done | bytes 524320 | tf_op jit(solution)/shard_map/all_to_all | solution.py:433
  102.9 3.4 %project.4 = bf16[128,1536]{1,0:T(8,128)(2,1)S(1)} custom-call(bf16[16,64,256]{2,1,0:T(8,128)(2,1)S(1)} %all-to-all-done.1.attended, bf16[2048,4608]{1,0:T(8,128)(2,1)} %bitcast.14), custom_call_target="tpu_custom_call" | custom-call | flops 805306368 | bytes 6291456 | tf_op jit(solution)/shard_map/project/pallas_call | solution.py:325
  106.2 1.6 %collective-permute-start.6 = (bf16[128,1536]{1,0:T(8,128)(2,1)S(1)}, bf16[128,1536]{1,0:T(8,128)(2,1)S(1)}, u32[]{:S(2)}, u32[]{:S(2)}) collective-permute-start(bf16[128,1536]{1,0:T(8,128)(2,1)S(1)} %project.4), channel_id=1, source_target_pairs={{0,1},{1,0},{2,3},{3,2},{4,5},{5,4},{6,7},{7,6},{8,9},{9,8},{10,11... | collective-permute-start | bytes 1179656 | tf_op jit(solution)/shard_map/ppermute | solution.py:449
  107.8 4.1 %all-to-all-start.2 = ((bf16[16,64,256]{2,1,0:T(8,128)(2,1)}), bf16[16,64,256]{2,1,0:T(8,128)(2,1)S(1)}, u32[]{:S(2)}, u32[]{:S(2)}) async-start(bf16[16,64,256]{2,1,0:T(8,128)(2,1)} %attend.3), calls=%async_computation.2 | async-start | bytes 1048576 | tf_op jit(solution)/shard_map/all_to_all | solution.py:446
  111.9 3.4 %project.5 = bf16[128,1536]{1,0:T(8,128)(2,1)S(1)} custom-call(bf16[16,64,256]{2,1,0:T(8,128)(2,1)S(1)} %all-to-all-done.1.attended, bf16[2048,4608]{1,0:T(8,128)(2,1)} %bitcast.15), custom_call_target="tpu_custom_call" | custom-call | flops 805306368 | bytes 6291456 | tf_op jit(solution)/shard_map/project/pallas_call | solution.py:325
  115.3 0.6 collective-permute-start.7
  115.9 1.5 %collective-permute-done.6.__0_ = bf16[128,1536]{1,0:T(8,128)(2,1)S(1)} collective-permute-done((bf16[128,1536]{1,0:T(8,128)(2,1)S(1)}, bf16[128,1536]{1,0:T(8,128)(2,1)S(1)}, u32[]{:S(2)}, u32[]{:S(2)}) %collective-permute-start.6) | collective-permute-done | bytes 393248 | tf_op jit(solution)/shard_map/ppermute | solution.py:449
  117.3 0.8 copy-done.1
  118.1 3.4 %project.7 = bf16[128,1536]{1,0:T(8,128)(2,1)S(1)} custom-call(bf16[16,64,256]{2,1,0:T(8,128)(2,1)S(1)} %all-to-all-done.1.attended, bf16[2048,4608]{1,0:T(8,128)(2,1)} %bitcast.16), custom_call_target="tpu_custom_call" | custom-call | flops 805306368 | bytes 6291456 | tf_op jit(solution)/shard_map/project/pallas_call | solution.py:325
  121.5 1.6 %collective-permute-start.8 = (bf16[128,1536]{1,0:T(8,128)(2,1)S(1)}, bf16[128,1536]{1,0:T(8,128)(2,1)S(1)}, u32[]{:S(2)}, u32[]{:S(2)}) collective-permute-start(bf16[128,1536]{1,0:T(8,128)(2,1)S(1)} %project.7), channel_id=1, source_target_pairs={{0,1},{1,0},{2,3},{3,2},{4,5},{5,4},{6,7},{7,6},{8,9},{9,8},{10,11... | collective-permute-start | bytes 1179656 | tf_op jit(solution)/shard_map/ppermute | solution.py:449
  123.1 4.2 %collective-permute-done.7.refs_1_ = bf16[128,1536]{1,0:T(8,128)(2,1)S(1)} collective-permute-done((bf16[128,1536]{1,0:T(8,128)(2,1)S(1)}, bf16[128,1536]{1,0:T(8,128)(2,1)S(1)}, u32[]{:S(2)}, u32[]{:S(2)}) %collective-permute-start.7) | collective-permute-done | bytes 393248 | tf_op jit(solution)/shard_map/ppermute | solution.py:449
  127.4 1.0 copy-done.2
  128.3 7.1 %project.6 = (f32[128,4608]{1,0:T(8,128)S(1)}, f32[128,128]{1,0:T(8,128)S(1)}) custom-call(bf16[16,64,256]{2,1,0:T(8,128)(2,1)S(1)} %all-to-all-done.2.attended, bf16[2048,4608]{1,0:T(8,128)(2,1)} %bitcast.17, bf16[128,1536]{1,0:T(8,128)(2,1)S(1)} %copy-done.2, bf16[128,1536]{1,0:T(8,128)(2,1)S(1)} %collective-permute-done.7.refs_1_), custom_call_target="tpu_custom_call" | custom-call | flops 2415919104 | bytes 18874368 | tf_op jit(solution)/shard_map/project/pallas_call | solution.py:325
  135.5 1.4 %finish.1 = bf16[2,64,4608]{2,1,0:T(8,128)(2,1)} custom-call(f32[128,4608]{1,0:T(8,128)S(1)} %get-tuple-element.55.projected, f32[128,128]{1,0:T(8,128)S(1)} %get-tuple-element.56.squares_ref, bf16[128,1536]{1,0:T(8,128)(2,1)S(1)} %collective-permute-done.8.arrived, bf16[2,64,4608]{2,1,0:T(8,128)(2,1)S(1)} %copy-done, f32[1,4608]{1,0:T(1,128)S(1)} %reshape.35.gain), custom_call_target="tpu_custom_call" | custom-call | bytes 6291456 | tf_op jit(solution)/shard_map/finish/pallas_call | solution.py:378
  (32 shorter events, 1.2 us)
Async XLA Ops:
  3.2 69.7 %copy-start.5 = (s32[2,16]{1,0:T(2,128)S(1)}, s32[2,16]{1,0:T(2,128)}, u32[]{:S(2)}) copy-start(s32[2,16]{1,0:T(2,128)} %table_ref.3) | copy-start | bytes 388
  3.2 69.7 %copy-start.6 = (s32[2]{0:T(128)S(1)}, s32[2]{0:T(128)}, u32[]{:S(2)}) copy-start(s32[2]{0:T(128)} %len_ref.3) | copy-start | bytes 28
  3.2 57.7 %all-to-all-start = ((bf16[16,5,128,128]{3,2,1,0:T(8,128)(2,1)}), bf16[16,5,128,128]{3,2,1,0:T(8,128)(2,1)S(1)}, u32[]{:S(2)}, u32[]{:S(2)}) async-start(bf16[16,5,128,128]{3,2,1,0:T(8,128)(2,1)} %bitcast.18), calls=%async_computation | async-start | bytes 5242880 | tf_op jit(solution)/shard_map/all_to_all | solution.py:420
  11.6 1.6 %collective-permute-start = (bf16[64,16,128]{2,1,0:T(8,128)(2,1)S(1)}, bf16[64,16,128]{2,1,0:T(8,128)(2,1)S(1)}, u32[]{:S(2)}, u32[]{:S(2)}) collective-permute-start(bf16[64,16,128]{2,1,0:T(8,128)(2,1)S(1)} %dynamic-slice_bitcast_fusion), channel_id=1, source_target_pairs={{0,2},{2,0},{4,6},{6,4},{8,10},{10,8},{12,14},{14,12},{16,18},{18,... | collective-permute-start | bytes 786440 | tf_op jit(solution)/shard_map/ppermute | solution.py:417
  13.2 0.7 copy-start.7
  16.7 22.2 %collective-permute-start.1 = (bf16[4,2,128,128]{3,2,1,0:T(8,128)(2,1)}, bf16[4,2,128,128]{3,2,1,0:T(8,128)(2,1)S(1)}, u32[]{:S(2)}, u32[]{:S(2)}) collective-permute-start(bf16[4,2,128,128]{3,2,1,0:T(8,128)(2,1)} %get-tuple-element.33), channel_id=1, source_target_pairs={{0,4},{2,6},{4,0},{6,2},{8,12},{10,14},{12,8},{14,10},{16,20},{18,... | collective-permute-start | bytes 786440 | tf_op jit(solution)/shard_map/ppermute | solution.py:417
  38.8 0.7 copy-start.8
  60.8 12.0 %collective-permute-start.2 = (bf16[16,5,128,128]{3,2,1,0:T(8,128)(2,1)S(1)}, bf16[16,5,128,128]{3,2,1,0:T(8,128)(2,1)S(1)}, u32[]{:S(2)}, u32[]{:S(2)}) collective-permute-start(bf16[16,5,128,128]{3,2,1,0:T(8,128)(2,1)S(1)} %all-to-all-done.message), channel_id=1, source_target_pairs={{0,2},{2,0},{4,6},{6,4},{8,10},{10,8},{12,14},{14,12},{16,18},{18,... | collective-permute-start | bytes 7864328 | tf_op jit(solution)/shard_map/ppermute | solution.py:417
  61.6 20.3 %collective-permute-start.4 = (bf16[2,2,128,128]{3,2,1,0:T(8,128)(2,1)}, bf16[2,2,128,128]{3,2,1,0:T(8,128)(2,1)S(1)}, u32[]{:S(2)}, u32[]{:S(2)}) collective-permute-start(bf16[2,2,128,128]{3,2,1,0:T(8,128)(2,1)} %get-tuple-element.41), channel_id=1, source_target_pairs={{0,16},{2,18},{4,20},{6,22},{8,24},{10,26},{12,28},{14,30},{16,0},... | collective-permute-start | bytes 393224 | tf_op jit(solution)/shard_map/ppermute | solution.py:417
  72.3 9.6 %collective-permute-start.5 = (bf16[2,2,128,128]{3,2,1,0:T(8,128)(2,1)}, bf16[2,2,128,128]{3,2,1,0:T(8,128)(2,1)S(1)}, u32[]{:S(2)}, u32[]{:S(2)}) collective-permute-start(bf16[2,2,128,128]{3,2,1,0:T(8,128)(2,1)} %get-tuple-element.42), channel_id=1, source_target_pairs={{0,24},{2,26},{4,28},{6,30},{8,16},{10,18},{12,20},{14,22},{16,8},... | collective-permute-start | bytes 393224 | tf_op jit(solution)/shard_map/ppermute | solution.py:417
  72.3 11.4 %collective-permute-start.3 = (bf16[2,2,128,128]{3,2,1,0:T(8,128)(2,1)}, bf16[2,2,128,128]{3,2,1,0:T(8,128)(2,1)S(1)}, u32[]{:S(2)}, u32[]{:S(2)}) collective-permute-start(bf16[2,2,128,128]{3,2,1,0:T(8,128)(2,1)} %get-tuple-element.40), channel_id=1, source_target_pairs={{0,8},{2,10},{4,12},{6,14},{8,0},{10,2},{12,4},{14,6},{16,24},{18,... | collective-permute-start | bytes 393224 | tf_op jit(solution)/shard_map/ppermute | solution.py:417
  72.9 9.0 %copy-start.3 = (bf16[16,5,128,128]{3,2,1,0:T(8,128)(2,1)}, bf16[16,5,128,128]{3,2,1,0:T(8,128)(2,1)S(1)}, u32[]{:S(2)}) copy-start(bf16[16,5,128,128]{3,2,1,0:T(8,128)(2,1)S(1)} %collective-permute-done.2.other) | copy-start | bytes 7864324
  81.9 6.5 %copy-start.10 = (bf16[2,2,128,128]{3,2,1,0:T(8,128)(2,1)}, bf16[2,2,128,128]{3,2,1,0:T(8,128)(2,1)S(1)}, u32[]{:S(2)}) copy-start(bf16[2,2,128,128]{3,2,1,0:T(8,128)(2,1)S(1)} %collective-permute-done.4) | copy-start | bytes 393220
  81.9 6.5 %copy-start.11 = (bf16[2,2,128,128]{3,2,1,0:T(8,128)(2,1)}, bf16[2,2,128,128]{3,2,1,0:T(8,128)(2,1)S(1)}, u32[]{:S(2)}) copy-start(bf16[2,2,128,128]{3,2,1,0:T(8,128)(2,1)S(1)} %collective-permute-done.5) | copy-start | bytes 393220
  83.6 4.8 %copy-start.12 = (bf16[2,2,128,128]{3,2,1,0:T(8,128)(2,1)}, bf16[2,2,128,128]{3,2,1,0:T(8,128)(2,1)S(1)}, u32[]{:S(2)}) copy-start(bf16[2,2,128,128]{3,2,1,0:T(8,128)(2,1)S(1)} %collective-permute-done.3) | copy-start | bytes 393220
  83.6 19.2 %all-to-all-start.1 = ((bf16[16,64,256]{2,1,0:T(8,128)(2,1)}), bf16[16,64,256]{2,1,0:T(8,128)(2,1)S(1)}, u32[]{:S(2)}, u32[]{:S(2)}) async-start(bf16[16,64,256]{2,1,0:T(8,128)(2,1)} %attend.2), calls=%async_computation.1 | async-start | bytes 1048576 | tf_op jit(solution)/shard_map/all_to_all | solution.py:433
  88.4 1.7 %copy-start.4 = (bf16[16,5,128,128]{3,2,1,0:T(8,128)(2,1)S(1)}, bf16[16,5,128,128]{3,2,1,0:T(8,128)(2,1)}, u32[]{:S(2)}) copy-start(bf16[16,5,128,128]{3,2,1,0:T(8,128)(2,1)} %copy-done.3) | copy-start | bytes 7864324
  106.2 11.1 %collective-permute-start.6 = (bf16[128,1536]{1,0:T(8,128)(2,1)S(1)}, bf16[128,1536]{1,0:T(8,128)(2,1)S(1)}, u32[]{:S(2)}, u32[]{:S(2)}) collective-permute-start(bf16[128,1536]{1,0:T(8,128)(2,1)S(1)} %project.4), channel_id=1, source_target_pairs={{0,1},{1,0},{2,3},{3,2},{4,5},{5,4},{6,7},{7,6},{8,9},{9,8},{10,11... | collective-permute-start | bytes 1179656 | tf_op jit(solution)/shard_map/ppermute | solution.py:449
  107.8 19.5 %all-to-all-start.2 = ((bf16[16,64,256]{2,1,0:T(8,128)(2,1)}), bf16[16,64,256]{2,1,0:T(8,128)(2,1)S(1)}, u32[]{:S(2)}, u32[]{:S(2)}) async-start(bf16[16,64,256]{2,1,0:T(8,128)(2,1)} %attend.3), calls=%async_computation.2 | async-start | bytes 1048576 | tf_op jit(solution)/shard_map/all_to_all | solution.py:446
  115.3 12.0 %collective-permute-start.7 = (bf16[128,1536]{1,0:T(8,128)(2,1)S(1)}, bf16[128,1536]{1,0:T(8,128)(2,1)S(1)}, u32[]{:S(2)}, u32[]{:S(2)}) collective-permute-start(bf16[128,1536]{1,0:T(8,128)(2,1)S(1)} %project.5), channel_id=1, source_target_pairs={{0,1},{1,0},{2,3},{3,2},{4,5},{5,4},{6,7},{7,6},{8,9},{9,8},{10,11... | collective-permute-start | bytes 1179656 | tf_op jit(solution)/shard_map/ppermute | solution.py:449
  117.3 0.8 copy-start.1
  118.1 5.0 %copy-start.9 = (f32[4608]{0:T(1024)S(1)}, f32[4608]{0:T(1024)}, u32[]{:S(2)}) copy-start(f32[4608]{0:T(1024)} %param.19) | copy-start | bytes 55300
  121.5 14.0 %collective-permute-start.8 = (bf16[128,1536]{1,0:T(8,128)(2,1)S(1)}, bf16[128,1536]{1,0:T(8,128)(2,1)S(1)}, u32[]{:S(2)}, u32[]{:S(2)}) collective-permute-start(bf16[128,1536]{1,0:T(8,128)(2,1)S(1)} %project.7), channel_id=1, source_target_pairs={{0,1},{1,0},{2,3},{3,2},{4,5},{5,4},{6,7},{7,6},{8,9},{9,8},{10,11... | collective-permute-start | bytes 1179656 | tf_op jit(solution)/shard_map/ppermute | solution.py:449
  123.1 12.4 %copy-start = (bf16[2,64,4608]{2,1,0:T(8,128)(2,1)S(1)}, bf16[2,64,4608]{2,1,0:T(8,128)(2,1)}, u32[]{:S(2)}) copy-start(bf16[2,64,4608]{2,1,0:T(8,128)(2,1)} %residual.1) | copy-start | bytes 3538948
  127.3 1.0 copy-start.2

commit v6 on v5

--- a/solution.py
+++ b/solution.py
@@ -91,7 +91,7 @@
             pltpu.SemaphoreType.DMA((pieces + cores,)),
             pltpu.SemaphoreType.DMA((pieces + cores,)),
         ],
-        compiler_params=kernel_params(12 if caches else 6),
+        compiler_params=kernel_params(16),
         cost_estimate=pl.CostEstimate(flops=0, bytes_accessed=parts * mib, transcendentals=0),
         name="pack_cache" if caches else "pack_queries",
     )(share, *operands)
@@ -135,7 +135,7 @@
             pltpu.VMEM((2, rows * heads, head_dim), jnp.float32),
             pltpu.SemaphoreType.DMA((4,)),
         ],
-        compiler_params=kernel_params(6),
+        compiler_params=kernel_params(12),
         cost_estimate=pl.CostEstimate(flops=0, bytes_accessed=mib, transcendentals=0),
         name="spread_queries",
     )(place, *[pltpu.with_memory_space_constraint(x, pltpu.HBM) for x in (queries, got)])
@@ -162,26 +162,79 @@
         out_specs=[in_hbm] * levels,
         out_shape=[pltpu.HBM((2,) + keep.shape[1:], jnp.bfloat16)] * levels,
         scratch_shapes=[pltpu.SemaphoreType.DMA((2 * levels,))],
-        compiler_params=kernel_params(1),
+        compiler_params=kernel_params(4),
         cost_estimate=pl.CostEstimate(flops=0, bytes_accessed=mib, transcendentals=0),
         name="gather_queries",
     )(place, *[pltpu.with_memory_space_constraint(x, pltpu.HBM) for x in (keep, got)])
 
 
-def attend_kernel(pages, own_share, place_ref, table_ref, len_ref, message, other, *rest):
-    out, cache_k, cache_v, new_v, total, made, held, others, in_sem, other_sem, out_sem = rest[-11:]
+def add_keys(
+    queries, query_part, total, per_head, group, share, page_rows, first_block, block_count, keys, values, start=None, causal=False
+):
+    block_rows = per_head * group
+    rows = block_count * block_rows
+    query = queries[first_block : first_block + block_count, query_part].reshape(rows, keys.shape[1])
+    scores = lax.dot_general(query, keys, (((1,), (1,)), ((), ())), preferred_element_type=jnp.float32)
+    weights = jnp.exp2((soft_cap * log2_e) * jnp.tanh(scores * (score_scale / soft_cap)))
+    if causal:
+        row = lax.broadcasted_iota(jnp.int32, weights.shape, 0)
+        offset = row // block_rows * page_rows + row % per_head + share * per_head
+        weights = jnp.where(lax.broadcasted_iota(jnp.int32, weights.shape, 1) <= offset, weights, 0.0)
+    product = jnp.dot(weights.astype(jnp.bfloat16), values, preferred_element_type=jnp.float32)
+    here = pl.ds(first_block * block_rows, rows)
+    total[here, :] = product if start is None else start[here, :] + product
+
+
+def add_new_keys(add, message, pages):
+    blocks, _, page_rows, head_dim = message.shape
+    half, tile_blocks = blocks // 2, key_tile // page_rows
+    ones = jnp.ones((key_tile, head_dim), jnp.bfloat16)
+    for block in range(0, blocks, tile_blocks):
+        keys = message[block : block + tile_blocks, pages].reshape(key_tile, head_dim)
+        values = message[block : block + tile_blocks, pages + 1].reshape(key_tile, head_dim)
+        values = jnp.concatenate([values, ones], axis=1)
+        start = None if block == 0 else add.args[2]
+        add(block, tile_blocks, keys, values, start=start, causal=True)
+        later = block + tile_blocks
+        while later < blocks:
+            count = min(half, blocks - later)
+            add(later, count, keys, values, start=start)
+            later += count
+
+
+def new_kernel(pages, group, place_ref, message, total):
+    page_rows = message.shape[2]
+    per_head = page_rows // group
+    share = 1 - place_ref[1]
+    add_new_keys(functools.partial(add_keys, message, pages + 2, total, per_head, group, share, page_rows), message, pages)
+
+
+def attend_new(place, message, *, pages, group):
+    blocks, _, page_rows, head_dim = message.shape
+    seen = blocks * page_rows * blocks // 2 * page_rows
+    return pl.pallas_call(
+        functools.partial(new_kernel, pages, group),
+        in_specs=[in_smem, in_vmem],
+        out_specs=in_vmem,
+        out_shape=jax.ShapeDtypeStruct((blocks * page_rows, 2 * head_dim), jnp.float32),
+        compiler_params=kernel_params(20),
+        cost_estimate=pl.CostEstimate(flops=8 * seen * head_dim, bytes_accessed=4 * mib, transcendentals=2 * seen),
+        name="attend_new",
+    )(place, message)
+
+
+def attend_kernel(pages, own_share, given, place_ref, table_ref, len_ref, message, other, *rest):
+    out, cache_k, cache_v, total, made, held, others, in_sem, other_sem, out_sem = rest[-10:]
     fetch = pltpu.make_async_copy(other.at[:, 0:pages], others, other_sem)
     fetch.start()
     share = place_ref[1] if own_share else 1 - place_ref[1]
-    queries, query_part = message, pages + 2
+    queries, query_part = (held, 0) if own_share else (message, pages + 2)
     arrivals = []
-    if own_share:
-        queries, query_part = held, 0
-        for step, source in enumerate(rest[:-11]):
-            count = source.shape[0]
-            here = pl.ds((place_ref[2] ^ step) * count, count)
-            arrivals.append(pltpu.make_async_copy(source, held.at[here], in_sem.at[step]))
-            arrivals[-1].start()
+    for step, source in enumerate(rest[:-10] if own_share else ()):
+        count = source.shape[0]
+        here = pl.ds((place_ref[2] ^ step) * count, count)
+        arrivals.append(pltpu.make_async_copy(source, held.at[here], in_sem.at[step]))
+        arrivals[-1].start()
     blocks, _, page_rows, head_dim = message.shape
     slots = table_ref.shape[1]
     group = out.shape[2] // head_dim
@@ -189,81 +242,66 @@
     block_rows = per_head * group
     core = place_ref[0]
     cached = len_ref[core]
-    for block in range(blocks):
-        new_v[block * page_rows : (block + 1) * page_rows, 0:head_dim] = message[block, pages + 1]
-    new_v[:, head_dim : 2 * head_dim] = jnp.ones((blocks * page_rows, head_dim), jnp.bfloat16)
-    fetch.wait()
-    for slot in range(slots):
-        page = table_ref[core, slot]
-        mine = message[page // pages, page % pages]
-        theirs = others[page // pages, page % pages]
-        seen = slot * page_rows + lax.broadcasted_iota(jnp.int32, (page_rows, head_dim), 0) < cached
-        here = pl.ds(slot * page_rows, page_rows)
-        cache_k[here, :] = jnp.where(core == 0, mine, theirs)
-        values = jnp.where(core == 0, theirs, mine).astype(jnp.float32)
-        cache_v[here, 0:head_dim] = jnp.where(seen, values, 0.0).astype(jnp.bfloat16)
-        cache_v[here, head_dim : 2 * head_dim] = jnp.where(seen, 1.0, 0.0).astype(jnp.bfloat16)
+    half = blocks // 2
+    tile_blocks = key_tile // page_rows
+    copies = []
+
+    add = functools.partial(add_keys, queries, query_part, total, per_head, group, share, page_rows)
+
+    def leave(first):
+        for block in range(first, first + half):
+            here = pl.ds(block * block_rows, block_rows)
+            attended = (total[here, 0:head_dim] / total[here, head_dim : 2 * head_dim]).astype(jnp.bfloat16)
+            for head in range(group):
+                made[block, :, head * head_dim : (head + 1) * head_dim] = attended[head * per_head : (head + 1) * per_head, :]
+        here = pl.ds(first, half)
+        copies.append(pltpu.make_async_copy(made.at[here], out.at[here], out_sem.at[len(copies)]))
+        copies[-1].start()
+
     for arrival in arrivals:
         arrival.wait()
-
-    def add(first_block, block_count, keys, values, begin=False, causal=False):
-        rows = block_count * block_rows
-        query = queries[first_block : first_block + block_count, query_part].reshape(rows, head_dim)
-        scores = lax.dot_general(query, keys, (((1,), (1,)), ((), ())), preferred_element_type=jnp.float32)
-        weights = jnp.exp2((soft_cap * log2_e) * jnp.tanh(scores * (score_scale / soft_cap)))
-        if causal:
-            row = lax.broadcasted_iota(jnp.int32, weights.shape, 0)
-            offset = row // block_rows * page_rows + row % per_head + share * per_head
-            weights = jnp.where(lax.broadcasted_iota(jnp.int32, weights.shape, 1) <= offset, weights, 0.0)
-        product = jnp.dot(weights.astype(jnp.bfloat16), values, preferred_element_type=jnp.float32)
-        here = pl.ds(first_block * block_rows, rows)
-        total[here, :] = product if begin else total[here, :] + product
-
-    half = blocks // 2
-    for first in (0, half):
-        for tile in range(0, slots * page_rows, key_tile):
-            add(first, half, cache_k[tile : tile + key_tile, :], cache_v[tile : tile + key_tile, :], begin=tile == 0)
-    tile_blocks = key_tile // page_rows
-    for block in range(0, blocks, tile_blocks):
-        keys = message[block : block + tile_blocks, pages].reshape(key_tile, head_dim)
-        values = new_v[block * page_rows : block * page_rows + key_tile, :]
-        add(block, tile_blocks, keys, values, causal=True)
-        later = block + tile_blocks
-        while later < blocks:
-            count = min(half, blocks - later)
-            add(later, count, keys, values)
-            later += count
-    copies = []
-    for block in range(blocks):
-        here = pl.ds(block * block_rows, block_rows)
-        attended = (total[here, 0:head_dim] / total[here, head_dim : 2 * head_dim]).astype(jnp.bfloat16)
-        for head in range(group):
-            made[block, :, head * head_dim : (head + 1) * head_dim] = attended[head * per_head : (head + 1) * per_head, :]
-        if block % half == half - 1:
-            here = pl.ds(block + 1 - half, half)
-            copies.append(pltpu.make_async_copy(made.at[here], out.at[here], out_sem.at[len(copies)]))
-            copies[-1].start()
+    if not given:
+        add_new_keys(add, message, pages)
+    fetch.wait()
+    for tile in range(0, slots, tile_blocks):
+        for slot in range(tile, tile + tile_blocks):
+            page = table_ref[core, slot]
+            mine = message[page // pages, page % pages]
+            theirs = others[page // pages, page % pages]
+            seen = slot * page_rows + lax.broadcasted_iota(jnp.int32, (page_rows, head_dim), 0) < cached
+            here = pl.ds(slot * page_rows, page_rows)
+            cache_k[here, :] = jnp.where(core == 0, mine, theirs)
+            values = jnp.where(core == 0, theirs, mine).astype(jnp.float32)
+            cache_v[here, 0:head_dim] = jnp.where(seen, values, 0.0).astype(jnp.bfloat16)
+            cache_v[here, head_dim : 2 * head_dim] = jnp.where(seen, 1.0, 0.0).astype(jnp.bfloat16)
+        here = slice(tile * page_rows, tile * page_rows + key_tile)
+        for first in (0, half):
+            add(first, half, cache_k[here, :], cache_v[here, :], start=rest[0] if given and tile == 0 else total)
+            if tile + tile_blocks == slots:
+                leave(first)
     for copy in copies:
         copy.wait()
 
 
-def attend(place, page_table, cache_len, message, other, queries, *, pages, group):
+def attend(place, page_table, cache_len, message, other, queries, given=None, *, pages, group):
     blocks, _, page_rows, head_dim = message.shape
     slots = page_table.shape[1]
     block_rows = page_rows
     operands = [message, other]
     operands += [pltpu.with_memory_space_constraint(x, pltpu.HBM) for x in queries]
     specs = [in_smem] * 3 + [in_vmem, pl.BlockSpec(memory_space=pl.ANY)] + [in_hbm] * len(queries)
+    if given is not None:
+        operands.append(given)
+        specs.append(in_vmem)
     seen = blocks * block_rows * (slots + blocks // 2) * page_rows
     return pl.pallas_call(
-        functools.partial(attend_kernel, pages, bool(queries)),
+        functools.partial(attend_kernel, pages, bool(queries), given is not None),
         in_specs=specs,
         out_specs=in_hbm,
         out_shape=pltpu.HBM((blocks, block_rows // group, group * head_dim), jnp.bfloat16),
         scratch_shapes=[
             pltpu.VMEM((slots * page_rows, head_dim), jnp.bfloat16),
             pltpu.VMEM((slots * page_rows, 2 * head_dim), jnp.bfloat16),
-            pltpu.VMEM((blocks * page_rows, 2 * head_dim), jnp.bfloat16),
             pltpu.VMEM((blocks * block_rows, 2 * head_dim), jnp.float32),
             pltpu.VMEM((blocks, block_rows // group, group * head_dim), jnp.bfloat16),
             pltpu.VMEM((blocks, 1, block_rows, head_dim) if queries else (8, 128), jnp.bfloat16),
@@ -272,7 +310,7 @@
             pltpu.SemaphoreType.DMA(()),
             pltpu.SemaphoreType.DMA((2,)),
         ],
-        compiler_params=kernel_params(12),
+        compiler_params=kernel_params(24),
         cost_estimate=pl.CostEstimate(flops=8 * seen * head_dim, bytes_accessed=8 * mib, transcendentals=2 * seen),
         name="attend",
     )(place, page_table, cache_len, *operands)
@@ -332,7 +370,7 @@
             pltpu.VMEM((columns // tile, depth, tile), jnp.bfloat16),
             pltpu.SemaphoreType.DMA((columns // tile,)),
         ],
-        compiler_params=kernel_params(6 + 2 * depth * columns // mib),
+        compiler_params=kernel_params(12 + 2 * depth * columns // mib),
         cost_estimate=pl.CostEstimate(flops=2 * rows * depth * columns, bytes_accessed=2 * depth * columns, transcendentals=0),
         name="project",
     )(*operands)
@@ -350,19 +388,25 @@
     )(x)
 
 
-def finish_kernel(projected, squares_ref, arrived, residual, gain, out, made, sem):
+def finish_kernel(projected, squares_ref, *refs):
+    *arrived, residual, gain, out, made, sem = refs
     requests, count, width = residual.shape
     rows = made.shape[1]
-    split = width - arrived.shape[1]
+    split = width - sum(piece.shape[1] for piece in arrived)
     copies = []
     for step in range(made.shape[0]):
         request, first = step * rows // count, step * rows % count
         here = slice(step * rows, (step + 1) * rows)
         place = slice(first, first + rows)
-        last = projected[here, split:] + arrived[here, :].astype(jnp.float32)
-        squares = jnp.sum(squares_ref[here, :] + squares_by_lane(last), axis=-1, keepdims=True)
-        inv_rms = lax.rsqrt(squares / width + norm_eps)
-        for columns, x in ((slice(0, split), projected[here, 0:split]), (slice(split, width), last)):
+        parts, squares, begin = [(slice(0, split), projected[here, 0:split])], squares_ref[here, :], split
+        for piece in arrived:
+            columns = slice(begin, begin + piece.shape[1])
+            x = projected[here, columns] + piece[here, :].astype(jnp.float32)
+            parts.append((columns, x))
+            squares += squares_by_lane(x)
+            begin = columns.stop
+        inv_rms = lax.rsqrt(jnp.sum(squares, axis=-1, keepdims=True) / width + norm_eps)
+        for columns, x in parts:
             mixed = residual[request, place, columns].astype(jnp.float32) + gain[:, columns] * x * inv_rms
             made[step, :, columns] = mixed.astype(jnp.bfloat16)
         copies.append(pltpu.make_async_copy(made.at[step], out.at[request, place], sem.at[step]))
@@ -377,14 +421,14 @@
     steps = requests * count // rows
     return pl.pallas_call(
         finish_kernel,
-        in_specs=[in_vmem] * 5,
+        in_specs=[in_vmem] * (len(arrived) + 4),
         out_specs=in_hbm,
         out_shape=pltpu.HBM(residual.shape, jnp.bfloat16),
         scratch_shapes=[pltpu.VMEM((steps, rows, width), jnp.bfloat16), pltpu.SemaphoreType.DMA((steps,))],
-        compiler_params=kernel_params(12),
+        compiler_params=kernel_params(16),
         cost_estimate=pl.CostEstimate(flops=0, bytes_accessed=6 * mib, transcendentals=0),
         name="finish",
-    )(projected, squares, arrived, residual, gain.reshape(1, width))
+    )(projected, squares, *arrived, residual, gain.reshape(1, width))
 
 
 def by_heads(
@@ -421,14 +465,15 @@
     got = lax.dynamic_slice(queries, (1 - core, mine, 0, 0, 0), (1, 1) + queries.shape[2:])
     got = across(got.reshape(queries.shape[2:]), 1)
     keep, send = spread(place, queries, got, kv_here)
-    asked = gather(place, keep, across(send, 2))
+    asked = list(gather(place, keep, across(send, 2)))
+    asked[1] = across(asked[1], 4)
     message, *asked = lax.optimization_barrier((message, *asked))
     other = across(message, 1)
-    asked = [across(x, 4 * step) if step else x for step, x in enumerate(asked)]
+    asked = [across(x, 4 * step) if step > 1 else x for step, x in enumerate(asked)]
     asked = [x.reshape(4, 1, *x.shape[2:]) for x in asked]
     attend_share = functools.partial(attend, place, page_table, cache_len, message, other, pages=pages, group=group)
 
-    first = attend_share([])
+    first = attend_share([], attend_new(place, message, pages=pages, group=group))
     first, *asked = lax.optimization_barrier((first, *asked))
     first = exchange(first)
     second = attend_share(asked)
@@ -447,8 +492,8 @@
         else:
             first, sent = lax.optimization_barrier((first, sent))
         arrived.append(lax.ppermute(sent, "head", [(0, 1), (1, 0)]))
-    projected, squares = project(second, weight, req_count, 0, width, tile, jnp.float32, arrived[:2])
-    return finish(projected, squares, arrived[2], residual, post_gain)
+    projected, squares = project(second, weight, req_count, 0, width, tile, jnp.float32, arrived[:1])
+    return finish(projected, squares, arrived[1:], residual, post_gain)
 
 
 def group_pages(page_count, page_len):

time: 138 us -> 137 us (level)
  starting transfers between devices: 34.4 us -> 29.6 us
  waiting for transfers between devices: 35.4 us -> 38.7 us
    ppermute x6, waiting for transfers between devices: 23 us -> 30.8 us  [across(): return lax.ppermute(x, 'blk', [(i, i ^ bits) for i in range(blk_count)])]
    ppermute x6, starting transfers between devices: 14.4 us -> 8.15 us  [across(): return lax.ppermute(x, 'blk', [(i, i ^ bits) for i in range(blk_count)])]
    all_to_all x1, waiting for transfers between devices: 3.71 us -> 0.01 us  [by_heads(): message = exchange(message.reshape((blk_count,) + message.shape[2:]))]
    ppermute x3, waiting for transfers between devices: 5.7 us -> 2.16 us  [by_heads(): arrived.append(lax.ppermute(sent, 'head', [(0, 1), (1, 0)]))]
    all_to_all x1, waiting for transfers between devices: 0.01 us -> 3.3 us  [by_heads(): second = exchange(second)]
    all_to_all x1, starting transfers between devices: 4.76 us -> 6.2 us  [by_heads(): first = exchange(first)]
    pallas_call x3 -> x4, Pallas kernels: 20.2 us -> 21.4 us  [the longest x2 16.7 us: attend(): pl.pallas_call(functools.partial(attend_kernel, pages, bool(queries), giv...]
  transfers between devices with their start and end apart: 12 -> 12, of which waited for: 7 -> 7; matrix products, arithmetic and copies ran while one was open for 1% -> 1% of each run, Pallas kernels for 39% -> 40%
where the time goes in v6:
time: 137 us
  Pallas kernels  62.1 us (45%)
  waiting for transfers between devices  38.7 us (28%)
  starting transfers between devices  29.6 us (22%)
  local copies, waits for them, and re-layouts  5.91 us (4%)
    ppermute x6, waiting for transfers between devices, across(): return lax.ppermute(x, 'blk', [(i, i ^ bits) for i in range(blk_count)])  30.8 us
    pallas_call x1, Pallas kernels, gather(): pl.pallas_call(gather_kernel, in_specs=[in_smem, in_hbm, in_hbm], out_spe...  17.6 us
    pallas_call x4, Pallas kernels, project(): pl.pallas_call(functools.partial(project_kernel, begin), in_specs=[in_vme...  17.2 us
    pallas_call x2, Pallas kernels, attend(): pl.pallas_call(functools.partial(attend_kernel, pages, bool(queries), giv...  16.7 us
    ppermute x6, starting transfers between devices, across(): return lax.ppermute(x, 'blk', [(i, i ^ bits) for i in range(blk_count)])  8.15 us
    all_to_all x1, starting transfers between devices, by_heads(): message = exchange(message.reshape((blk_count,) + message.shape[2:]))  7.37 us
    all_to_all x1, starting transfers between devices, by_heads(): first = exchange(first)  6.2 us
    unnamed x26, local copies, waits for them, and re-layouts  4.93 us
  transfers between devices with their start and end apart: 12, of which 7 were waited for; matrix products, arithmetic and copies ran while one was open for 1% of the time, Pallas kernels for 40%

profile of v6, /device:TPU:0, one launch (start us, length us, event | category | flops | bytes accessed | tf_op | source)
XLA Modules:
  0.0 136.8 jit_solution(15523078523329543465)
XLA Ops:
  0.0 3.2 %pack_cache.1 = bf16[8,2,5,128,128]{4,3,2,1,0:T(8,128)(2,1)} custom-call(s32[1]{0:T(128)} %bitcast.4.share_ref, bf16[2,128,8,128]{3,2,1,0:T(8,128)(2,1)} %refs_0_.1, bf16[2,128,8,128]{3,2,1,0:T(8,128)(2,1)} %refs_1_.1, bf16[2,128,8,128]{3,2,1,0:T(8,128)(2,1)} %refs_2_.2, bf16[2,128,8,128]{3,2,1,0:T(8,128)(2,1)} %refs_3_.1, bf16[2,2,64,16,128]{4,3,2,1,0:T(8,128)(2,1)} %bitcast.19), custom_call_target="tpu_custom_call" | custom-call | bytes 5242880 | tf_op jit(solution)/shard_map/pack_cache/pallas_call | solution.py:81
  3.2 7.4 %all-to-all-start = ((bf16[16,5,128,128]{3,2,1,0:T(8,128)(2,1)}), bf16[16,5,128,128]{3,2,1,0:T(8,128)(2,1)S(1)}, u32[]{:S(2)}, u32[]{:S(2)}) async-start(bf16[16,5,128,128]{3,2,1,0:T(8,128)(2,1)} %bitcast.18), calls=%async_computation | async-start | bytes 5242880 | tf_op jit(solution)/shard_map/all_to_all | solution.py:464
  10.6 1.0 dynamic-slice_bitcast_fusion
  12.1 1.1 collective-permute-done.got
  13.2 0.7 copy-done.7
  13.9 2.8 %spread_queries.1 = (bf16[4,2,128,128]{3,2,1,0:T(8,128)(2,1)}, bf16[4,2,128,128]{3,2,1,0:T(8,128)(2,1)}) custom-call(s32[4]{0:T(128)S(1)} %pad_add_fusion.place_ref, bf16[2,2,64,16,128]{4,3,2,1,0:T(8,128)(2,1)} %bitcast.21, bf16[64,16,128]{2,1,0:T(8,128)(2,1)} %copy-done.7), custom_call_target="tpu_custom_call" | custom-call | bytes 1048576 | tf_op jit(solution)/shard_map/spread_queries/pallas_call | solution.py:127
  16.6 2.0 %collective-permute-start.1 = (bf16[4,2,128,128]{3,2,1,0:T(8,128)(2,1)}, bf16[4,2,128,128]{3,2,1,0:T(8,128)(2,1)S(1)}, u32[]{:S(2)}, u32[]{:S(2)}) collective-permute-start(bf16[4,2,128,128]{3,2,1,0:T(8,128)(2,1)} %get-tuple-element.33), channel_id=1, source_target_pairs={{0,4},{2,6},{4,0},{6,2},{8,12},{10,14},{12,8},{14,10},{16,20},{18,... | collective-permute-start | bytes 786440 | tf_op jit(solution)/shard_map/ppermute | solution.py:461
  18.6 20.2 %collective-permute-done.1.got = bf16[4,2,128,128]{3,2,1,0:T(8,128)(2,1)S(1)} collective-permute-done((bf16[4,2,128,128]{3,2,1,0:T(8,128)(2,1)}, bf16[4,2,128,128]{3,2,1,0:T(8,128)(2,1)S(1)}, u32[]{:S(2)}, u32[]{:S(2)}) %collective-permute-start.1) | collective-permute-done | bytes 262176 | tf_op jit(solution)/shard_map/ppermute | solution.py:461
  38.8 0.7 copy-done.8
  39.5 17.6 %gather_queries.1 = (bf16[2,2,128,128]{3,2,1,0:T(8,128)(2,1)}, bf16[2,2,128,128]{3,2,1,0:T(8,128)(2,1)}, bf16[2,2,128,128]{3,2,1,0:T(8,128)(2,1)}, bf16[2,2,128,128]{3,2,1,0:T(8,128)(2,1)}) custom-call(s32[4]{0:T(128)S(1)} %pad_add_fusion.place_ref, bf16[4,2,128,128]{3,2,1,0:T(8,128)(2,1)} %get-tuple-element.32.keep, bf16[4,2,128,128]{3,2,1,0:T(8,128)(2,1)} %copy-done.8), custom_call_target="tpu_custom_call" | custom-call | bytes 1048576 | tf_op jit(solution)/shard_map/gather_queries/pallas_call | solution.py:159
  57.2 9.5 %collective-permute-done.2 = bf16[2,2,128,128]{3,2,1,0:T(8,128)(2,1)S(1)} collective-permute-done((bf16[2,2,128,128]{3,2,1,0:T(8,128)(2,1)}, bf16[2,2,128,128]{3,2,1,0:T(8,128)(2,1)S(1)}, u32[]{:S(2)}, u32[]{:S(2)}) %collective-permute-start.2) | collective-permute-done | bytes 131104 | tf_op jit(solution)/shard_map/ppermute | solution.py:461
  66.8 5.6 %collective-permute-start.4 = (bf16[2,2,128,128]{3,2,1,0:T(8,128)(2,1)}, bf16[2,2,128,128]{3,2,1,0:T(8,128)(2,1)S(1)}, u32[]{:S(2)}, u32[]{:S(2)}) collective-permute-start(bf16[2,2,128,128]{3,2,1,0:T(8,128)(2,1)} %get-tuple-element.41), channel_id=1, source_target_pairs={{0,16},{2,18},{4,20},{6,22},{8,24},{10,26},{12,28},{14,30},{16,0},... | collective-permute-start | bytes 393224 | tf_op jit(solution)/shard_map/ppermute | solution.py:461
  72.4 3.3 %attend_new.1.rest_0_ = f32[2048,256]{1,0:T(8,128)S(1)} custom-call(s32[4]{0:T(128)S(1)} %pad_add_fusion.place_ref, bf16[16,5,128,128]{3,2,1,0:T(8,128)(2,1)S(1)} %all-to-all-done.message), custom_call_target="tpu_custom_call" | custom-call | flops 2147483648 | bytes 4194304 | tf_op jit(solution)/shard_map/attend_new/pallas_call | solution.py:215
  75.7 6.4 %attend.2 = bf16[16,64,256]{2,1,0:T(8,128)(2,1)} custom-call(s32[4]{0:T(128)S(1)} %pad_add_fusion.place_ref, s32[2,16]{1,0:T(2,128)S(1)} %copy-done.5, s32[2]{0:T(128)S(1)} %copy-done.6, bf16[16,5,128,128]{3,2,1,0:T(8,128)(2,1)S(1)} %all-to-all-done.message, bf16[16,5,128,128]{3,2,1,0:T(8,128)(2,1)S(1)} %collective-permute-done.3.other, ...), custom_call_target="tpu_custom_call" | custom-call | flops 6442450944 | bytes 8388608 | tf_op jit(solution)/shard_map/attend/pallas_call | solution.py:297
  82.2 6.2 %all-to-all-start.1 = ((bf16[16,64,256]{2,1,0:T(8,128)(2,1)}), bf16[16,64,256]{2,1,0:T(8,128)(2,1)S(1)}, u32[]{:S(2)}, u32[]{:S(2)}) async-start(bf16[16,64,256]{2,1,0:T(8,128)(2,1)} %attend.2), calls=%async_computation.1 | async-start | bytes 1048576 | tf_op jit(solution)/shard_map/all_to_all | solution.py:478
  88.4 1.7 %copy-done.4 = bf16[16,5,128,128]{3,2,1,0:T(8,128)(2,1)S(1)} copy-done((bf16[16,5,128,128]{3,2,1,0:T(8,128)(2,1)S(1)}, bf16[16,5,128,128]{3,2,1,0:T(8,128)(2,1)}, u32[]{:S(2)}) %copy-start.4) | copy-done | bytes 2621464
  90.1 10.3 %attend.3 = bf16[16,64,256]{2,1,0:T(8,128)(2,1)} custom-call(s32[4]{0:T(128)S(1)} %pad_add_fusion.place_ref, s32[2,16]{1,0:T(2,128)S(1)} %copy-done.5, s32[2]{0:T(128)S(1)} %copy-done.6, bf16[16,5,128,128]{3,2,1,0:T(8,128)(2,1)S(1)} %all-to-all-done.message, bf16[16,5,128,128]{3,2,1,0:T(8,128)(2,1)S(1)} %copy-done.4, bf16[4,1,128,128]{3,2,1,0:T(8,128)(2,1)} %bitcast.22, ...), custom_call_target="tpu_custom_call" | custom-call | flops 6442450944 | bytes 8388608 | tf_op jit(solution)/shard_map/attend/pallas_call | solution.py:297
  100.4 2.4 %all-to-all-done.1.attended = bf16[16,64,256]{2,1,0:T(8,128)(2,1)S(1)} async-done(((bf16[16,64,256]{2,1,0:T(8,128)(2,1)}), bf16[16,64,256]{2,1,0:T(8,128)(2,1)S(1)}, u32[]{:S(2)}, u32[]{:S(2)}) %all-to-all-start.1) | async-done | bytes 524320 | tf_op jit(solution)/shard_map/all_to_all | solution.py:478
  102.8 3.4 %project.4 = bf16[128,1536]{1,0:T(8,128)(2,1)S(1)} custom-call(bf16[16,64,256]{2,1,0:T(8,128)(2,1)S(1)} %all-to-all-done.1.attended, bf16[2048,4608]{1,0:T(8,128)(2,1)} %bitcast.14), custom_call_target="tpu_custom_call" | custom-call | flops 805306368 | bytes 6291456 | tf_op jit(solution)/shard_map/project/pallas_call | solution.py:363
  106.2 1.6 %collective-permute-start.6 = (bf16[128,1536]{1,0:T(8,128)(2,1)S(1)}, bf16[128,1536]{1,0:T(8,128)(2,1)S(1)}, u32[]{:S(2)}, u32[]{:S(2)}) collective-permute-start(bf16[128,1536]{1,0:T(8,128)(2,1)S(1)} %project.4), channel_id=1, source_target_pairs={{0,1},{1,0},{2,3},{3,2},{4,5},{5,4},{6,7},{7,6},{8,9},{9,8},{10,11... | collective-permute-start | bytes 1179656 | tf_op jit(solution)/shard_map/ppermute | solution.py:494
  107.8 4.1 %all-to-all-start.2 = ((bf16[16,64,256]{2,1,0:T(8,128)(2,1)}), bf16[16,64,256]{2,1,0:T(8,128)(2,1)S(1)}, u32[]{:S(2)}, u32[]{:S(2)}) async-start(bf16[16,64,256]{2,1,0:T(8,128)(2,1)} %attend.3), calls=%async_computation.2 | async-start | bytes 1048576 | tf_op jit(solution)/shard_map/all_to_all | solution.py:491
  111.9 3.4 %project.5 = bf16[128,1536]{1,0:T(8,128)(2,1)S(1)} custom-call(bf16[16,64,256]{2,1,0:T(8,128)(2,1)S(1)} %all-to-all-done.1.attended, bf16[2048,4608]{1,0:T(8,128)(2,1)} %bitcast.15), custom_call_target="tpu_custom_call" | custom-call | flops 805306368 | bytes 6291456 | tf_op jit(solution)/shard_map/project/pallas_call | solution.py:363
  115.3 0.6 collective-permute-start.7
  115.8 1.5 %collective-permute-done.6.__0_ = bf16[128,1536]{1,0:T(8,128)(2,1)S(1)} collective-permute-done((bf16[128,1536]{1,0:T(8,128)(2,1)S(1)}, bf16[128,1536]{1,0:T(8,128)(2,1)S(1)}, u32[]{:S(2)}, u32[]{:S(2)}) %collective-permute-start.6) | collective-permute-done | bytes 393248 | tf_op jit(solution)/shard_map/ppermute | solution.py:494
  117.3 0.8 copy-done.1
  118.1 3.4 %project.7 = bf16[128,1536]{1,0:T(8,128)(2,1)S(1)} custom-call(bf16[16,64,256]{2,1,0:T(8,128)(2,1)S(1)} %all-to-all-done.1.attended, bf16[2048,4608]{1,0:T(8,128)(2,1)} %bitcast.16), custom_call_target="tpu_custom_call" | custom-call | flops 805306368 | bytes 6291456 | tf_op jit(solution)/shard_map/project/pallas_call | solution.py:363
  121.4 1.6 %collective-permute-start.8 = (bf16[128,1536]{1,0:T(8,128)(2,1)S(1)}, bf16[128,1536]{1,0:T(8,128)(2,1)S(1)}, u32[]{:S(2)}, u32[]{:S(2)}) collective-permute-start(bf16[128,1536]{1,0:T(8,128)(2,1)S(1)} %project.7), channel_id=1, source_target_pairs={{0,1},{1,0},{2,3},{3,2},{4,5},{5,4},{6,7},{7,6},{8,9},{9,8},{10,11... | collective-permute-start | bytes 1179656 | tf_op jit(solution)/shard_map/ppermute | solution.py:494
  123.1 3.3 %all-to-all-done.2.attended = bf16[16,64,256]{2,1,0:T(8,128)(2,1)S(1)} async-done(((bf16[16,64,256]{2,1,0:T(8,128)(2,1)}), bf16[16,64,256]{2,1,0:T(8,128)(2,1)S(1)}, u32[]{:S(2)}, u32[]{:S(2)}) %all-to-all-start.2) | async-done | bytes 524320 | tf_op jit(solution)/shard_map/all_to_all | solution.py:491
  126.4 1.0 copy-done.2
  127.4 7.1 %project.6 = (f32[128,4608]{1,0:T(8,128)S(1)}, f32[128,128]{1,0:T(8,128)S(1)}) custom-call(bf16[16,64,256]{2,1,0:T(8,128)(2,1)S(1)} %all-to-all-done.2.attended, bf16[2048,4608]{1,0:T(8,128)(2,1)} %bitcast.17, bf16[128,1536]{1,0:T(8,128)(2,1)S(1)} %copy-done.2), custom_call_target="tpu_custom_call" | custom-call | flops 2415919104 | bytes 18874368 | tf_op jit(solution)/shard_map/project/pallas_call | solution.py:363
  134.5 0.7 collective-permute-done.8.refs_1_
  135.2 1.5 %finish.1 = bf16[2,64,4608]{2,1,0:T(8,128)(2,1)} custom-call(f32[128,4608]{1,0:T(8,128)S(1)} %get-tuple-element.54.projected, f32[128,128]{1,0:T(8,128)S(1)} %get-tuple-element.55.squares_ref, bf16[128,1536]{1,0:T(8,128)(2,1)S(1)} %collective-permute-done.7.refs_0_, bf16[128,1536]{1,0:T(8,128)(2,1)S(1)} %collective-permute-done.8.refs_1_, ...), custom_call_target="tpu_custom_call" | custom-call | bytes 6291456 | tf_op jit(solution)/shard_map/finish/pallas_call | solution.py:422
  (33 shorter events, 0.7 us)
Async XLA Ops:
  3.2 63.5 %all-to-all-start = ((bf16[16,5,128,128]{3,2,1,0:T(8,128)(2,1)}), bf16[16,5,128,128]{3,2,1,0:T(8,128)(2,1)S(1)}, u32[]{:S(2)}, u32[]{:S(2)}) async-start(bf16[16,5,128,128]{3,2,1,0:T(8,128)(2,1)} %bitcast.18), calls=%async_computation | async-start | bytes 5242880 | tf_op jit(solution)/shard_map/all_to_all | solution.py:464
  11.5 1.6 %collective-permute-start = (bf16[64,16,128]{2,1,0:T(8,128)(2,1)S(1)}, bf16[64,16,128]{2,1,0:T(8,128)(2,1)S(1)}, u32[]{:S(2)}, u32[]{:S(2)}) collective-permute-start(bf16[64,16,128]{2,1,0:T(8,128)(2,1)S(1)} %dynamic-slice_bitcast_fusion), channel_id=1, source_target_pairs={{0,2},{2,0},{4,6},{6,4},{8,10},{10,8},{12,14},{14,12},{16,18},{18,... | collective-permute-start | bytes 786440 | tf_op jit(solution)/shard_map/ppermute | solution.py:461
  13.2 0.7 copy-start.7
  16.6 22.2 %collective-permute-start.1 = (bf16[4,2,128,128]{3,2,1,0:T(8,128)(2,1)}, bf16[4,2,128,128]{3,2,1,0:T(8,128)(2,1)S(1)}, u32[]{:S(2)}, u32[]{:S(2)}) collective-permute-start(bf16[4,2,128,128]{3,2,1,0:T(8,128)(2,1)} %get-tuple-element.33), channel_id=1, source_target_pairs={{0,4},{2,6},{4,0},{6,2},{8,12},{10,14},{12,8},{14,10},{16,20},{18,... | collective-permute-start | bytes 786440 | tf_op jit(solution)/shard_map/ppermute | solution.py:461
  38.8 0.7 copy-start.8
  57.1 9.6 %collective-permute-start.2 = (bf16[2,2,128,128]{3,2,1,0:T(8,128)(2,1)}, bf16[2,2,128,128]{3,2,1,0:T(8,128)(2,1)S(1)}, u32[]{:S(2)}, u32[]{:S(2)}) collective-permute-start(bf16[2,2,128,128]{3,2,1,0:T(8,128)(2,1)} %get-tuple-element.35), channel_id=1, source_target_pairs={{0,8},{2,10},{4,12},{6,14},{8,0},{10,2},{12,4},{14,6},{16,24},{18,... | collective-permute-start | bytes 393224 | tf_op jit(solution)/shard_map/ppermute | solution.py:461
  66.7 9.0 %copy-start.10 = (bf16[2,2,128,128]{3,2,1,0:T(8,128)(2,1)}, bf16[2,2,128,128]{3,2,1,0:T(8,128)(2,1)S(1)}, u32[]{:S(2)}) copy-start(bf16[2,2,128,128]{3,2,1,0:T(8,128)(2,1)S(1)} %collective-permute-done.2) | copy-start | bytes 393220
  66.7 9.0 %copy-start.5 = (s32[2,16]{1,0:T(2,128)S(1)}, s32[2,16]{1,0:T(2,128)}, u32[]{:S(2)}) copy-start(s32[2,16]{1,0:T(2,128)} %table_ref.3) | copy-start | bytes 388
  66.7 9.0 %copy-start.6 = (s32[2]{0:T(128)S(1)}, s32[2]{0:T(128)}, u32[]{:S(2)}) copy-start(s32[2]{0:T(128)} %len_ref.3) | copy-start | bytes 28
  66.7 9.0 %collective-permute-start.3 = (bf16[16,5,128,128]{3,2,1,0:T(8,128)(2,1)S(1)}, bf16[16,5,128,128]{3,2,1,0:T(8,128)(2,1)S(1)}, u32[]{:S(2)}, u32[]{:S(2)}) collective-permute-start(bf16[16,5,128,128]{3,2,1,0:T(8,128)(2,1)S(1)} %all-to-all-done.message), channel_id=1, source_target_pairs={{0,2},{2,0},{4,6},{6,4},{8,10},{10,8},{12,14},{14,12},{16,18},{18,... | collective-permute-start | bytes 7864328 | tf_op jit(solution)/shard_map/ppermute | solution.py:461
  66.8 15.4 %collective-permute-start.4 = (bf16[2,2,128,128]{3,2,1,0:T(8,128)(2,1)}, bf16[2,2,128,128]{3,2,1,0:T(8,128)(2,1)S(1)}, u32[]{:S(2)}, u32[]{:S(2)}) collective-permute-start(bf16[2,2,128,128]{3,2,1,0:T(8,128)(2,1)} %get-tuple-element.41), channel_id=1, source_target_pairs={{0,16},{2,18},{4,20},{6,22},{8,24},{10,26},{12,28},{14,30},{16,0},... | collective-permute-start | bytes 393224 | tf_op jit(solution)/shard_map/ppermute | solution.py:461
  72.4 9.8 %collective-permute-start.5 = (bf16[2,2,128,128]{3,2,1,0:T(8,128)(2,1)}, bf16[2,2,128,128]{3,2,1,0:T(8,128)(2,1)S(1)}, u32[]{:S(2)}, u32[]{:S(2)}) collective-permute-start(bf16[2,2,128,128]{3,2,1,0:T(8,128)(2,1)} %get-tuple-element.42), channel_id=1, source_target_pairs={{0,24},{2,26},{4,28},{6,30},{8,16},{10,18},{12,20},{14,22},{16,8},... | collective-permute-start | bytes 393224 | tf_op jit(solution)/shard_map/ppermute | solution.py:461
  75.7 6.4 %copy-start.3 = (bf16[16,5,128,128]{3,2,1,0:T(8,128)(2,1)}, bf16[16,5,128,128]{3,2,1,0:T(8,128)(2,1)S(1)}, u32[]{:S(2)}) copy-start(bf16[16,5,128,128]{3,2,1,0:T(8,128)(2,1)S(1)} %collective-permute-done.3.other) | copy-start | bytes 7864324
  82.1 6.2 %copy-start.11 = (bf16[2,2,128,128]{3,2,1,0:T(8,128)(2,1)}, bf16[2,2,128,128]{3,2,1,0:T(8,128)(2,1)S(1)}, u32[]{:S(2)}) copy-start(bf16[2,2,128,128]{3,2,1,0:T(8,128)(2,1)S(1)} %collective-permute-done.4) | copy-start | bytes 393220
  82.2 6.2 %copy-start.12 = (bf16[2,2,128,128]{3,2,1,0:T(8,128)(2,1)}, bf16[2,2,128,128]{3,2,1,0:T(8,128)(2,1)S(1)}, u32[]{:S(2)}) copy-start(bf16[2,2,128,128]{3,2,1,0:T(8,128)(2,1)S(1)} %collective-permute-done.5) | copy-start | bytes 393220
  82.2 20.7 %all-to-all-start.1 = ((bf16[16,64,256]{2,1,0:T(8,128)(2,1)}), bf16[16,64,256]{2,1,0:T(8,128)(2,1)S(1)}, u32[]{:S(2)}, u32[]{:S(2)}) async-start(bf16[16,64,256]{2,1,0:T(8,128)(2,1)} %attend.2), calls=%async_computation.1 | async-start | bytes 1048576 | tf_op jit(solution)/shard_map/all_to_all | solution.py:478
  88.4 1.7 %copy-start.4 = (bf16[16,5,128,128]{3,2,1,0:T(8,128)(2,1)S(1)}, bf16[16,5,128,128]{3,2,1,0:T(8,128)(2,1)}, u32[]{:S(2)}) copy-start(bf16[16,5,128,128]{3,2,1,0:T(8,128)(2,1)} %copy-done.3) | copy-start | bytes 7864324
  106.2 11.1 %collective-permute-start.6 = (bf16[128,1536]{1,0:T(8,128)(2,1)S(1)}, bf16[128,1536]{1,0:T(8,128)(2,1)S(1)}, u32[]{:S(2)}, u32[]{:S(2)}) collective-permute-start(bf16[128,1536]{1,0:T(8,128)(2,1)S(1)} %project.4), channel_id=1, source_target_pairs={{0,1},{1,0},{2,3},{3,2},{4,5},{5,4},{6,7},{7,6},{8,9},{9,8},{10,11... | collective-permute-start | bytes 1179656 | tf_op jit(solution)/shard_map/ppermute | solution.py:494
  107.8 18.6 %all-to-all-start.2 = ((bf16[16,64,256]{2,1,0:T(8,128)(2,1)}), bf16[16,64,256]{2,1,0:T(8,128)(2,1)S(1)}, u32[]{:S(2)}, u32[]{:S(2)}) async-start(bf16[16,64,256]{2,1,0:T(8,128)(2,1)} %attend.3), calls=%async_computation.2 | async-start | bytes 1048576 | tf_op jit(solution)/shard_map/all_to_all | solution.py:491
  115.3 19.2 %collective-permute-start.7 = (bf16[128,1536]{1,0:T(8,128)(2,1)S(1)}, bf16[128,1536]{1,0:T(8,128)(2,1)S(1)}, u32[]{:S(2)}, u32[]{:S(2)}) collective-permute-start(bf16[128,1536]{1,0:T(8,128)(2,1)S(1)} %project.5), channel_id=1, source_target_pairs={{0,1},{1,0},{2,3},{3,2},{4,5},{5,4},{6,7},{7,6},{8,9},{9,8},{10,11... | collective-permute-start | bytes 1179656 | tf_op jit(solution)/shard_map/ppermute | solution.py:494
  117.3 0.8 copy-start.1
  118.1 5.0 %copy-start.9 = (f32[4608]{0:T(1024)S(1)}, f32[4608]{0:T(1024)}, u32[]{:S(2)}) copy-start(f32[4608]{0:T(1024)} %param.19) | copy-start | bytes 55300
  121.4 13.7 %collective-permute-start.8 = (bf16[128,1536]{1,0:T(8,128)(2,1)S(1)}, bf16[128,1536]{1,0:T(8,128)(2,1)S(1)}, u32[]{:S(2)}, u32[]{:S(2)}) collective-permute-start(bf16[128,1536]{1,0:T(8,128)(2,1)S(1)} %project.7), channel_id=1, source_target_pairs={{0,1},{1,0},{2,3},{3,2},{4,5},{5,4},{6,7},{7,6},{8,9},{9,8},{10,11... | collective-permute-start | bytes 1179656 | tf_op jit(solution)/shard_map/ppermute | solution.py:494
  123.1 12.1 %copy-start = (bf16[2,64,4608]{2,1,0:T(8,128)(2,1)S(1)}, bf16[2,64,4608]{2,1,0:T(8,128)(2,1)}, u32[]{:S(2)}) copy-start(bf16[2,64,4608]{2,1,0:T(8,128)(2,1)} %refs_2_.3) | copy-start | bytes 3538948
  126.4 1.0 copy-start.2

commit v7 on v6

--- a/solution.py
+++ b/solution.py
@@ -317,9 +317,14 @@
 
 
 def project_kernel(begin, attended, weight, *refs):
-    (*arrived, out), (rows, held, sem) = refs[:-3], refs[-3:]
-    if arrived:
-        *arrived, out, squares_out = (*arrived, out)
+    arrived = []
+    if len(refs) == 4:
+        out, rows, held, sem = refs
+    else:
+        source, out, squares_out, rows, held, sem, piece, piece_sem = refs
+        arrived = [piece]
+        come = pltpu.make_async_copy(source, piece, piece_sem)
+        come.start()
     tiles, _, tile = held.shape
     arrivals = []
     for i in range(tiles):
@@ -332,6 +337,8 @@
         at, first = source % requests * count, source // requests * features
         rows[at : at + count, first : first + features] = attended[source]
     squares = 0.0
+    if arrived:
+        come.wait()
     for i in range(tiles):
         here = slice(i * tile, (i + 1) * tile)
         arrivals[i].wait()
@@ -362,14 +369,15 @@
         outs.append(jax.ShapeDtypeStruct((rows, 128), jnp.float32))
     return pl.pallas_call(
         functools.partial(project_kernel, begin),
-        in_specs=[in_vmem, in_hbm] + [in_vmem] * (len(operands) - 2),
+        in_specs=[in_vmem, in_hbm] + [pl.BlockSpec(memory_space=pl.ANY)] * len(arrived),
         out_specs=[in_vmem] * len(outs),
         out_shape=outs,
         scratch_shapes=[
             pltpu.VMEM((rows, depth), jnp.bfloat16),
             pltpu.VMEM((columns // tile, depth, tile), jnp.bfloat16),
             pltpu.SemaphoreType.DMA((columns // tile,)),
-        ],
+        ]
+        + [y for x in arrived for y in (pltpu.VMEM(x.shape, x.dtype), pltpu.SemaphoreType.DMA(()))],
         compiler_params=kernel_params(12 + 2 * depth * columns // mib),
         cost_estimate=pl.CostEstimate(flops=2 * rows * depth * columns, bytes_accessed=2 * depth * columns, transcendentals=0),
         name="project",
@@ -417,7 +425,7 @@
 
 def finish(projected, squares, arrived, residual, gain):
     requests, count, width = residual.shape
-    rows = 32
+    rows = 16
     steps = requests * count // rows
     return pl.pallas_call(
         finish_kernel,

time: 137 us -> 137 us (level)
  no operation moved by 1% of the time
where the time goes in v7:
time: 137 us
  Pallas kernels  62.2 us (45%)
  waiting for transfers between devices  38.5 us (28%)
  starting transfers between devices  29.6 us (22%)
  local copies, waits for them, and re-layouts  5.91 us (4%)
    ppermute x6, waiting for transfers between devices, across(): return lax.ppermute(x, 'blk', [(i, i ^ bits) for i in range(blk_count)])  30.8 us
    pallas_call x1, Pallas kernels, gather(): pl.pallas_call(gather_kernel, in_specs=[in_smem, in_hbm, in_hbm], out_spe...  17.6 us
    pallas_call x4, Pallas kernels, project(): pl.pallas_call(functools.partial(project_kernel, begin), in_specs=[in_vme...  17.4 us
    pallas_call x2, Pallas kernels, attend(): pl.pallas_call(functools.partial(attend_kernel, pages, bool(queries), giv...  16.7 us
    ppermute x6, starting transfers between devices, across(): return lax.ppermute(x, 'blk', [(i, i ^ bits) for i in range(blk_count)])  8.15 us
    all_to_all x1, starting transfers between devices, by_heads(): message = exchange(message.reshape((blk_count,) + message.shape[2:]))  7.37 us
    all_to_all x1, starting transfers between devices, by_heads(): first = exchange(first)  6.2 us
    unnamed x26, local copies, waits for them, and re-layouts  4.93 us
  transfers between devices with their start and end apart: 12, of which 7 were waited for; matrix products, arithmetic and copies ran while one was open for 1% of the time, Pallas kernels for 40%

profile of v7, /device:TPU:0, one launch (start us, length us, event | category | flops | bytes accessed | tf_op | source)
XLA Modules:
  0.0 136.7 jit_solution(14970163891178682791)
XLA Ops:
  0.0 3.2 %pack_cache.1 = bf16[8,2,5,128,128]{4,3,2,1,0:T(8,128)(2,1)} custom-call(s32[1]{0:T(128)} %bitcast.4.share_ref, bf16[2,128,8,128]{3,2,1,0:T(8,128)(2,1)} %refs_0_.1, bf16[2,128,8,128]{3,2,1,0:T(8,128)(2,1)} %refs_1_.1, bf16[2,128,8,128]{3,2,1,0:T(8,128)(2,1)} %refs_2_.2, bf16[2,128,8,128]{3,2,1,0:T(8,128)(2,1)} %refs_3_.1, bf16[2,2,64,16,128]{4,3,2,1,0:T(8,128)(2,1)} %bitcast.19), custom_call_target="tpu_custom_call" | custom-call | bytes 5242880 | tf_op jit(solution)/shard_map/pack_cache/pallas_call | solution.py:81
  3.2 7.4 %all-to-all-start = ((bf16[16,5,128,128]{3,2,1,0:T(8,128)(2,1)}), bf16[16,5,128,128]{3,2,1,0:T(8,128)(2,1)S(1)}, u32[]{:S(2)}, u32[]{:S(2)}) async-start(bf16[16,5,128,128]{3,2,1,0:T(8,128)(2,1)} %bitcast.18), calls=%async_computation | async-start | bytes 5242880 | tf_op jit(solution)/shard_map/all_to_all | solution.py:472
  10.6 1.0 dynamic-slice_bitcast_fusion
  12.1 1.1 collective-permute-done.got
  13.2 0.7 copy-done.7
  13.9 2.8 %spread_queries.1 = (bf16[4,2,128,128]{3,2,1,0:T(8,128)(2,1)}, bf16[4,2,128,128]{3,2,1,0:T(8,128)(2,1)}) custom-call(s32[4]{0:T(128)S(1)} %pad_add_fusion.place_ref, bf16[2,2,64,16,128]{4,3,2,1,0:T(8,128)(2,1)} %bitcast.21, bf16[64,16,128]{2,1,0:T(8,128)(2,1)} %copy-done.7), custom_call_target="tpu_custom_call" | custom-call | bytes 1048576 | tf_op jit(solution)/shard_map/spread_queries/pallas_call | solution.py:127
  16.6 2.0 %collective-permute-start.1 = (bf16[4,2,128,128]{3,2,1,0:T(8,128)(2,1)}, bf16[4,2,128,128]{3,2,1,0:T(8,128)(2,1)S(1)}, u32[]{:S(2)}, u32[]{:S(2)}) collective-permute-start(bf16[4,2,128,128]{3,2,1,0:T(8,128)(2,1)} %get-tuple-element.33), channel_id=1, source_target_pairs={{0,4},{2,6},{4,0},{6,2},{8,12},{10,14},{12,8},{14,10},{16,20},{18,... | collective-permute-start | bytes 786440 | tf_op jit(solution)/shard_map/ppermute | solution.py:469
  18.6 20.2 %collective-permute-done.1.got = bf16[4,2,128,128]{3,2,1,0:T(8,128)(2,1)S(1)} collective-permute-done((bf16[4,2,128,128]{3,2,1,0:T(8,128)(2,1)}, bf16[4,2,128,128]{3,2,1,0:T(8,128)(2,1)S(1)}, u32[]{:S(2)}, u32[]{:S(2)}) %collective-permute-start.1) | collective-permute-done | bytes 262176 | tf_op jit(solution)/shard_map/ppermute | solution.py:469
  38.8 0.7 copy-done.8
  39.5 17.6 %gather_queries.1 = (bf16[2,2,128,128]{3,2,1,0:T(8,128)(2,1)}, bf16[2,2,128,128]{3,2,1,0:T(8,128)(2,1)}, bf16[2,2,128,128]{3,2,1,0:T(8,128)(2,1)}, bf16[2,2,128,128]{3,2,1,0:T(8,128)(2,1)}) custom-call(s32[4]{0:T(128)S(1)} %pad_add_fusion.place_ref, bf16[4,2,128,128]{3,2,1,0:T(8,128)(2,1)} %get-tuple-element.32.keep, bf16[4,2,128,128]{3,2,1,0:T(8,128)(2,1)} %copy-done.8), custom_call_target="tpu_custom_call" | custom-call | bytes 1048576 | tf_op jit(solution)/shard_map/gather_queries/pallas_call | solution.py:159
  57.2 9.5 %collective-permute-done.2 = bf16[2,2,128,128]{3,2,1,0:T(8,128)(2,1)S(1)} collective-permute-done((bf16[2,2,128,128]{3,2,1,0:T(8,128)(2,1)}, bf16[2,2,128,128]{3,2,1,0:T(8,128)(2,1)S(1)}, u32[]{:S(2)}, u32[]{:S(2)}) %collective-permute-start.2) | collective-permute-done | bytes 131104 | tf_op jit(solution)/shard_map/ppermute | solution.py:469
  66.8 5.6 %collective-permute-start.4 = (bf16[2,2,128,128]{3,2,1,0:T(8,128)(2,1)}, bf16[2,2,128,128]{3,2,1,0:T(8,128)(2,1)S(1)}, u32[]{:S(2)}, u32[]{:S(2)}) collective-permute-start(bf16[2,2,128,128]{3,2,1,0:T(8,128)(2,1)} %get-tuple-element.41), channel_id=1, source_target_pairs={{0,16},{2,18},{4,20},{6,22},{8,24},{10,26},{12,28},{14,30},{16,0},... | collective-permute-start | bytes 393224 | tf_op jit(solution)/shard_map/ppermute | solution.py:469
  72.4 3.3 %attend_new.1.rest_0_ = f32[2048,256]{1,0:T(8,128)S(1)} custom-call(s32[4]{0:T(128)S(1)} %pad_add_fusion.place_ref, bf16[16,5,128,128]{3,2,1,0:T(8,128)(2,1)S(1)} %all-to-all-done.message), custom_call_target="tpu_custom_call" | custom-call | flops 2147483648 | bytes 4194304 | tf_op jit(solution)/shard_map/attend_new/pallas_call | solution.py:215
  75.7 6.4 %attend.2 = bf16[16,64,256]{2,1,0:T(8,128)(2,1)} custom-call(s32[4]{0:T(128)S(1)} %pad_add_fusion.place_ref, s32[2,16]{1,0:T(2,128)S(1)} %copy-done.5, s32[2]{0:T(128)S(1)} %copy-done.6, bf16[16,5,128,128]{3,2,1,0:T(8,128)(2,1)S(1)} %all-to-all-done.message, bf16[16,5,128,128]{3,2,1,0:T(8,128)(2,1)S(1)} %collective-permute-done.3.other, ...), custom_call_target="tpu_custom_call" | custom-call | flops 6442450944 | bytes 8388608 | tf_op jit(solution)/shard_map/attend/pallas_call | solution.py:297
  82.2 6.2 %all-to-all-start.1 = ((bf16[16,64,256]{2,1,0:T(8,128)(2,1)}), bf16[16,64,256]{2,1,0:T(8,128)(2,1)S(1)}, u32[]{:S(2)}, u32[]{:S(2)}) async-start(bf16[16,64,256]{2,1,0:T(8,128)(2,1)} %attend.2), calls=%async_computation.1 | async-start | bytes 1048576 | tf_op jit(solution)/shard_map/all_to_all | solution.py:486
  88.4 1.7 %copy-done.4 = bf16[16,5,128,128]{3,2,1,0:T(8,128)(2,1)S(1)} copy-done((bf16[16,5,128,128]{3,2,1,0:T(8,128)(2,1)S(1)}, bf16[16,5,128,128]{3,2,1,0:T(8,128)(2,1)}, u32[]{:S(2)}) %copy-start.4) | copy-done | bytes 2621464
  90.1 10.3 %attend.3 = bf16[16,64,256]{2,1,0:T(8,128)(2,1)} custom-call(s32[4]{0:T(128)S(1)} %pad_add_fusion.place_ref, s32[2,16]{1,0:T(2,128)S(1)} %copy-done.5, s32[2]{0:T(128)S(1)} %copy-done.6, bf16[16,5,128,128]{3,2,1,0:T(8,128)(2,1)S(1)} %all-to-all-done.message, bf16[16,5,128,128]{3,2,1,0:T(8,128)(2,1)S(1)} %copy-done.4, bf16[4,1,128,128]{3,2,1,0:T(8,128)(2,1)} %bitcast.22, ...), custom_call_target="tpu_custom_call" | custom-call | flops 6442450944 | bytes 8388608 | tf_op jit(solution)/shard_map/attend/pallas_call | solution.py:297
  100.4 2.4 %all-to-all-done.1.attended = bf16[16,64,256]{2,1,0:T(8,128)(2,1)S(1)} async-done(((bf16[16,64,256]{2,1,0:T(8,128)(2,1)}), bf16[16,64,256]{2,1,0:T(8,128)(2,1)S(1)}, u32[]{:S(2)}, u32[]{:S(2)}) %all-to-all-start.1) | async-done | bytes 524320 | tf_op jit(solution)/shard_map/all_to_all | solution.py:486
  102.8 3.4 %project.4 = bf16[128,1536]{1,0:T(8,128)(2,1)S(1)} custom-call(bf16[16,64,256]{2,1,0:T(8,128)(2,1)S(1)} %all-to-all-done.1.attended, bf16[2048,4608]{1,0:T(8,128)(2,1)} %bitcast.14), custom_call_target="tpu_custom_call" | custom-call | flops 805306368 | bytes 6291456 | tf_op jit(solution)/shard_map/project/pallas_call | solution.py:370
  106.2 1.6 %collective-permute-start.6 = (bf16[128,1536]{1,0:T(8,128)(2,1)S(1)}, bf16[128,1536]{1,0:T(8,128)(2,1)S(1)}, u32[]{:S(2)}, u32[]{:S(2)}) collective-permute-start(bf16[128,1536]{1,0:T(8,128)(2,1)S(1)} %project.4), channel_id=1, source_target_pairs={{0,1},{1,0},{2,3},{3,2},{4,5},{5,4},{6,7},{7,6},{8,9},{9,8},{10,11... | collective-permute-start | bytes 1179656 | tf_op jit(solution)/shard_map/ppermute | solution.py:502
  107.8 4.1 %all-to-all-start.2 = ((bf16[16,64,256]{2,1,0:T(8,128)(2,1)}), bf16[16,64,256]{2,1,0:T(8,128)(2,1)S(1)}, u32[]{:S(2)}, u32[]{:S(2)}) async-start(bf16[16,64,256]{2,1,0:T(8,128)(2,1)} %attend.3), calls=%async_computation.2 | async-start | bytes 1048576 | tf_op jit(solution)/shard_map/all_to_all | solution.py:499
  111.9 3.4 %project.5 = bf16[128,1536]{1,0:T(8,128)(2,1)S(1)} custom-call(bf16[16,64,256]{2,1,0:T(8,128)(2,1)S(1)} %all-to-all-done.1.attended, bf16[2048,4608]{1,0:T(8,128)(2,1)} %bitcast.15), custom_call_target="tpu_custom_call" | custom-call | flops 805306368 | bytes 6291456 | tf_op jit(solution)/shard_map/project/pallas_call | solution.py:370
  115.3 0.6 collective-permute-start.7
  115.8 1.5 %collective-permute-done.6.__0_ = bf16[128,1536]{1,0:T(8,128)(2,1)S(1)} collective-permute-done((bf16[128,1536]{1,0:T(8,128)(2,1)S(1)}, bf16[128,1536]{1,0:T(8,128)(2,1)S(1)}, u32[]{:S(2)}, u32[]{:S(2)}) %collective-permute-start.6) | collective-permute-done | bytes 393248 | tf_op jit(solution)/shard_map/ppermute | solution.py:502
  117.3 0.8 copy-done.1
  118.1 3.4 %project.7 = bf16[128,1536]{1,0:T(8,128)(2,1)S(1)} custom-call(bf16[16,64,256]{2,1,0:T(8,128)(2,1)S(1)} %all-to-all-done.1.attended, bf16[2048,4608]{1,0:T(8,128)(2,1)} %bitcast.16), custom_call_target="tpu_custom_call" | custom-call | flops 805306368 | bytes 6291456 | tf_op jit(solution)/shard_map/project/pallas_call | solution.py:370
  121.4 1.6 %collective-permute-start.8 = (bf16[128,1536]{1,0:T(8,128)(2,1)S(1)}, bf16[128,1536]{1,0:T(8,128)(2,1)S(1)}, u32[]{:S(2)}, u32[]{:S(2)}) collective-permute-start(bf16[128,1536]{1,0:T(8,128)(2,1)S(1)} %project.7), channel_id=1, source_target_pairs={{0,1},{1,0},{2,3},{3,2},{4,5},{5,4},{6,7},{7,6},{8,9},{9,8},{10,11... | collective-permute-start | bytes 1179656 | tf_op jit(solution)/shard_map/ppermute | solution.py:502
  123.1 3.3 %all-to-all-done.2.attended = bf16[16,64,256]{2,1,0:T(8,128)(2,1)S(1)} async-done(((bf16[16,64,256]{2,1,0:T(8,128)(2,1)}), bf16[16,64,256]{2,1,0:T(8,128)(2,1)S(1)}, u32[]{:S(2)}, u32[]{:S(2)}) %all-to-all-start.2) | async-done | bytes 524320 | tf_op jit(solution)/shard_map/all_to_all | solution.py:499
  126.4 1.0 copy-done.2
  127.4 7.3 %project.6 = (f32[128,4608]{1,0:T(8,128)S(1)}, f32[128,128]{1,0:T(8,128)S(1)}) custom-call(bf16[16,64,256]{2,1,0:T(8,128)(2,1)S(1)} %all-to-all-done.2.attended, bf16[2048,4608]{1,0:T(8,128)(2,1)} %bitcast.17, bf16[128,1536]{1,0:T(8,128)(2,1)S(1)} %copy-done.2), custom_call_target="tpu_custom_call" | custom-call | flops 2415919104 | bytes 18874368 | tf_op jit(solution)/shard_map/project/pallas_call | solution.py:370
  134.7 0.5 collective-permute-done.8.refs_1_
  135.2 1.3 finish.1
  (33 shorter events, 0.7 us)
Async XLA Ops:
  3.2 63.5 %all-to-all-start = ((bf16[16,5,128,128]{3,2,1,0:T(8,128)(2,1)}), bf16[16,5,128,128]{3,2,1,0:T(8,128)(2,1)S(1)}, u32[]{:S(2)}, u32[]{:S(2)}) async-start(bf16[16,5,128,128]{3,2,1,0:T(8,128)(2,1)} %bitcast.18), calls=%async_computation | async-start | bytes 5242880 | tf_op jit(solution)/shard_map/all_to_all | solution.py:472
  11.5 1.6 %collective-permute-start = (bf16[64,16,128]{2,1,0:T(8,128)(2,1)S(1)}, bf16[64,16,128]{2,1,0:T(8,128)(2,1)S(1)}, u32[]{:S(2)}, u32[]{:S(2)}) collective-permute-start(bf16[64,16,128]{2,1,0:T(8,128)(2,1)S(1)} %dynamic-slice_bitcast_fusion), channel_id=1, source_target_pairs={{0,2},{2,0},{4,6},{6,4},{8,10},{10,8},{12,14},{14,12},{16,18},{18,... | collective-permute-start | bytes 786440 | tf_op jit(solution)/shard_map/ppermute | solution.py:469
  13.2 0.7 copy-start.7
  16.6 22.2 %collective-permute-start.1 = (bf16[4,2,128,128]{3,2,1,0:T(8,128)(2,1)}, bf16[4,2,128,128]{3,2,1,0:T(8,128)(2,1)S(1)}, u32[]{:S(2)}, u32[]{:S(2)}) collective-permute-start(bf16[4,2,128,128]{3,2,1,0:T(8,128)(2,1)} %get-tuple-element.33), channel_id=1, source_target_pairs={{0,4},{2,6},{4,0},{6,2},{8,12},{10,14},{12,8},{14,10},{16,20},{18,... | collective-permute-start | bytes 786440 | tf_op jit(solution)/shard_map/ppermute | solution.py:469
  38.8 0.7 copy-start.8
  57.1 9.6 %collective-permute-start.2 = (bf16[2,2,128,128]{3,2,1,0:T(8,128)(2,1)}, bf16[2,2,128,128]{3,2,1,0:T(8,128)(2,1)S(1)}, u32[]{:S(2)}, u32[]{:S(2)}) collective-permute-start(bf16[2,2,128,128]{3,2,1,0:T(8,128)(2,1)} %get-tuple-element.35), channel_id=1, source_target_pairs={{0,8},{2,10},{4,12},{6,14},{8,0},{10,2},{12,4},{14,6},{16,24},{18,... | collective-permute-start | bytes 393224 | tf_op jit(solution)/shard_map/ppermute | solution.py:469
  66.7 9.0 %copy-start.10 = (bf16[2,2,128,128]{3,2,1,0:T(8,128)(2,1)}, bf16[2,2,128,128]{3,2,1,0:T(8,128)(2,1)S(1)}, u32[]{:S(2)}) copy-start(bf16[2,2,128,128]{3,2,1,0:T(8,128)(2,1)S(1)} %collective-permute-done.2) | copy-start | bytes 393220
  66.7 9.0 %copy-start.5 = (s32[2,16]{1,0:T(2,128)S(1)}, s32[2,16]{1,0:T(2,128)}, u32[]{:S(2)}) copy-start(s32[2,16]{1,0:T(2,128)} %table_ref.3) | copy-start | bytes 388
  66.7 9.0 %copy-start.6 = (s32[2]{0:T(128)S(1)}, s32[2]{0:T(128)}, u32[]{:S(2)}) copy-start(s32[2]{0:T(128)} %len_ref.3) | copy-start | bytes 28
  66.7 9.0 %collective-permute-start.3 = (bf16[16,5,128,128]{3,2,1,0:T(8,128)(2,1)S(1)}, bf16[16,5,128,128]{3,2,1,0:T(8,128)(2,1)S(1)}, u32[]{:S(2)}, u32[]{:S(2)}) collective-permute-start(bf16[16,5,128,128]{3,2,1,0:T(8,128)(2,1)S(1)} %all-to-all-done.message), channel_id=1, source_target_pairs={{0,2},{2,0},{4,6},{6,4},{8,10},{10,8},{12,14},{14,12},{16,18},{18,... | collective-permute-start | bytes 7864328 | tf_op jit(solution)/shard_map/ppermute | solution.py:469
  66.8 15.4 %collective-permute-start.4 = (bf16[2,2,128,128]{3,2,1,0:T(8,128)(2,1)}, bf16[2,2,128,128]{3,2,1,0:T(8,128)(2,1)S(1)}, u32[]{:S(2)}, u32[]{:S(2)}) collective-permute-start(bf16[2,2,128,128]{3,2,1,0:T(8,128)(2,1)} %get-tuple-element.41), channel_id=1, source_target_pairs={{0,16},{2,18},{4,20},{6,22},{8,24},{10,26},{12,28},{14,30},{16,0},... | collective-permute-start | bytes 393224 | tf_op jit(solution)/shard_map/ppermute | solution.py:469
  72.4 9.8 %collective-permute-start.5 = (bf16[2,2,128,128]{3,2,1,0:T(8,128)(2,1)}, bf16[2,2,128,128]{3,2,1,0:T(8,128)(2,1)S(1)}, u32[]{:S(2)}, u32[]{:S(2)}) collective-permute-start(bf16[2,2,128,128]{3,2,1,0:T(8,128)(2,1)} %get-tuple-element.42), channel_id=1, source_target_pairs={{0,24},{2,26},{4,28},{6,30},{8,16},{10,18},{12,20},{14,22},{16,8},... | collective-permute-start | bytes 393224 | tf_op jit(solution)/shard_map/ppermute | solution.py:469
  75.7 6.4 %copy-start.3 = (bf16[16,5,128,128]{3,2,1,0:T(8,128)(2,1)}, bf16[16,5,128,128]{3,2,1,0:T(8,128)(2,1)S(1)}, u32[]{:S(2)}) copy-start(bf16[16,5,128,128]{3,2,1,0:T(8,128)(2,1)S(1)} %collective-permute-done.3.other) | copy-start | bytes 7864324
  82.1 6.2 %copy-start.11 = (bf16[2,2,128,128]{3,2,1,0:T(8,128)(2,1)}, bf16[2,2,128,128]{3,2,1,0:T(8,128)(2,1)S(1)}, u32[]{:S(2)}) copy-start(bf16[2,2,128,128]{3,2,1,0:T(8,128)(2,1)S(1)} %collective-permute-done.4) | copy-start | bytes 393220
  82.2 6.2 %copy-start.12 = (bf16[2,2,128,128]{3,2,1,0:T(8,128)(2,1)}, bf16[2,2,128,128]{3,2,1,0:T(8,128)(2,1)S(1)}, u32[]{:S(2)}) copy-start(bf16[2,2,128,128]{3,2,1,0:T(8,128)(2,1)S(1)} %collective-permute-done.5) | copy-start | bytes 393220
  82.2 20.7 %all-to-all-start.1 = ((bf16[16,64,256]{2,1,0:T(8,128)(2,1)}), bf16[16,64,256]{2,1,0:T(8,128)(2,1)S(1)}, u32[]{:S(2)}, u32[]{:S(2)}) async-start(bf16[16,64,256]{2,1,0:T(8,128)(2,1)} %attend.2), calls=%async_computation.1 | async-start | bytes 1048576 | tf_op jit(solution)/shard_map/all_to_all | solution.py:486
  88.4 1.7 %copy-start.4 = (bf16[16,5,128,128]{3,2,1,0:T(8,128)(2,1)S(1)}, bf16[16,5,128,128]{3,2,1,0:T(8,128)(2,1)}, u32[]{:S(2)}) copy-start(bf16[16,5,128,128]{3,2,1,0:T(8,128)(2,1)} %copy-done.3) | copy-start | bytes 7864324
  106.2 11.1 %collective-permute-start.6 = (bf16[128,1536]{1,0:T(8,128)(2,1)S(1)}, bf16[128,1536]{1,0:T(8,128)(2,1)S(1)}, u32[]{:S(2)}, u32[]{:S(2)}) collective-permute-start(bf16[128,1536]{1,0:T(8,128)(2,1)S(1)} %project.4), channel_id=1, source_target_pairs={{0,1},{1,0},{2,3},{3,2},{4,5},{5,4},{6,7},{7,6},{8,9},{9,8},{10,11... | collective-permute-start | bytes 1179656 | tf_op jit(solution)/shard_map/ppermute | solution.py:502
  107.8 18.6 %all-to-all-start.2 = ((bf16[16,64,256]{2,1,0:T(8,128)(2,1)}), bf16[16,64,256]{2,1,0:T(8,128)(2,1)S(1)}, u32[]{:S(2)}, u32[]{:S(2)}) async-start(bf16[16,64,256]{2,1,0:T(8,128)(2,1)} %attend.3), calls=%async_computation.2 | async-start | bytes 1048576 | tf_op jit(solution)/shard_map/all_to_all | solution.py:499
  115.3 19.4 %collective-permute-start.7 = (bf16[128,1536]{1,0:T(8,128)(2,1)S(1)}, bf16[128,1536]{1,0:T(8,128)(2,1)S(1)}, u32[]{:S(2)}, u32[]{:S(2)}) collective-permute-start(bf16[128,1536]{1,0:T(8,128)(2,1)S(1)} %project.5), channel_id=1, source_target_pairs={{0,1},{1,0},{2,3},{3,2},{4,5},{5,4},{6,7},{7,6},{8,9},{9,8},{10,11... | collective-permute-start | bytes 1179656 | tf_op jit(solution)/shard_map/ppermute | solution.py:502
  117.3 0.8 copy-start.1
  118.1 5.0 %copy-start.9 = (f32[4608]{0:T(1024)S(1)}, f32[4608]{0:T(1024)}, u32[]{:S(2)}) copy-start(f32[4608]{0:T(1024)} %param.19) | copy-start | bytes 55300
  121.4 13.7 %collective-permute-start.8 = (bf16[128,1536]{1,0:T(8,128)(2,1)S(1)}, bf16[128,1536]{1,0:T(8,128)(2,1)S(1)}, u32[]{:S(2)}, u32[]{:S(2)}) collective-permute-start(bf16[128,1536]{1,0:T(8,128)(2,1)S(1)} %project.7), channel_id=1, source_target_pairs={{0,1},{1,0},{2,3},{3,2},{4,5},{5,4},{6,7},{7,6},{8,9},{9,8},{10,11... | collective-permute-start | bytes 1179656 | tf_op jit(solution)/shard_map/ppermute | solution.py:502
  123.1 12.1 %copy-start = (bf16[2,64,4608]{2,1,0:T(8,128)(2,1)S(1)}, bf16[2,64,4608]{2,1,0:T(8,128)(2,1)}, u32[]{:S(2)}) copy-start(bf16[2,64,4608]{2,1,0:T(8,128)(2,1)} %refs_2_.3) | copy-start | bytes 3538948
  126.4 1.0 copy-start.2

commit v8 on v6

--- a/solution.py
+++ b/solution.py
@@ -481,7 +481,7 @@
     tile = width // 9
     begin = 0
     arrived = []
-    for piece, tiles in enumerate((3, 3, 3)):
+    for piece, tiles in enumerate((3, 4, 2)):
         if piece == 2:
             first, arrived[0] = lax.optimization_barrier((first, wait_here(arrived[0])))
         (sent,) = project(first, weight, req_count, begin, tiles * tile, tile, jnp.bfloat16)

time: 137 us -> 141 us (1.029)
  waiting for transfers between devices: 38.7 us -> 42.1 us
    ppermute x3, waiting for transfers between devices: 2.16 us -> 8.88 us  [by_heads(): arrived.append(lax.ppermute(sent, 'head', [(0, 1), (1, 0)]))]
    all_to_all x1, waiting for transfers between devices: 3.3 us -> 0.01 us  [by_heads(): second = exchange(second)]
  transfers between devices with their start and end apart: 12 -> 12, of which waited for: 7 -> 6; matrix products, arithmetic and copies ran while one was open for 1% -> 1% of each run, Pallas kernels for 40% -> 39%
where the time goes in v8:
time: 141 us; the launch traced here: 140 us
  Pallas kernels  62.1 us (44%)
  waiting for transfers between devices  42.1 us (30%)
  starting transfers between devices  29.6 us (21%)
  local copies, waits for them, and re-layouts  6 us (4%)
    ppermute x6, waiting for transfers between devices, across(): return lax.ppermute(x, 'blk', [(i, i ^ bits) for i in range(blk_count)])  30.8 us
    pallas_call x1, Pallas kernels, gather(): pl.pallas_call(gather_kernel, in_specs=[in_smem, in_hbm, in_hbm], out_spe...  17.6 us
    pallas_call x4, Pallas kernels, project(): pl.pallas_call(functools.partial(project_kernel, begin), in_specs=[in_vme...  17.2 us
    pallas_call x2, Pallas kernels, attend(): pl.pallas_call(functools.partial(attend_kernel, pages, bool(queries), giv...  16.7 us
    ppermute x3, waiting for transfers between devices, by_heads(): arrived.append(lax.ppermute(sent, 'head', [(0, 1), (1, 0)]))  8.88 us
    ppermute x6, starting transfers between devices, across(): return lax.ppermute(x, 'blk', [(i, i ^ bits) for i in range(blk_count)])  8.15 us
    all_to_all x1, starting transfers between devices, by_heads(): message = exchange(message.reshape((blk_count,) + message.shape[2:]))  7.37 us
    all_to_all x1, starting transfers between devices, by_heads(): first = exchange(first)  6.2 us
  transfers between devices with their start and end apart: 12, of which 6 were waited for; matrix products, arithmetic and copies ran while one was open for 1% of the time, Pallas kernels for 39%

profile of v8, /device:TPU:0, one launch (start us, length us, event | category | flops | bytes accessed | tf_op | source)
XLA Modules:
  0.0 140.3 jit_solution(4086630248372571982)
XLA Ops:
  0.0 3.2 %pack_cache.1 = bf16[8,2,5,128,128]{4,3,2,1,0:T(8,128)(2,1)} custom-call(s32[1]{0:T(128)} %bitcast.4.share_ref, bf16[2,128,8,128]{3,2,1,0:T(8,128)(2,1)} %refs_0_.1, bf16[2,128,8,128]{3,2,1,0:T(8,128)(2,1)} %refs_1_.1, bf16[2,128,8,128]{3,2,1,0:T(8,128)(2,1)} %refs_2_.2, bf16[2,128,8,128]{3,2,1,0:T(8,128)(2,1)} %refs_3_.1, bf16[2,2,64,16,128]{4,3,2,1,0:T(8,128)(2,1)} %bitcast.19), custom_call_target="tpu_custom_call" | custom-call | bytes 5242880 | tf_op jit(solution)/shard_map/pack_cache/pallas_call | solution.py:81
  3.2 7.4 %all-to-all-start = ((bf16[16,5,128,128]{3,2,1,0:T(8,128)(2,1)}), bf16[16,5,128,128]{3,2,1,0:T(8,128)(2,1)S(1)}, u32[]{:S(2)}, u32[]{:S(2)}) async-start(bf16[16,5,128,128]{3,2,1,0:T(8,128)(2,1)} %bitcast.18), calls=%async_computation | async-start | bytes 5242880 | tf_op jit(solution)/shard_map/all_to_all | solution.py:464
  10.6 1.0 dynamic-slice_bitcast_fusion
  11.5 0.4 collective-permute-start
  12.1 1.1 collective-permute-done.got
  13.2 0.7 copy-done.7
  13.9 2.8 %spread_queries.1 = (bf16[4,2,128,128]{3,2,1,0:T(8,128)(2,1)}, bf16[4,2,128,128]{3,2,1,0:T(8,128)(2,1)}) custom-call(s32[4]{0:T(128)S(1)} %pad_add_fusion.place_ref, bf16[2,2,64,16,128]{4,3,2,1,0:T(8,128)(2,1)} %bitcast.21, bf16[64,16,128]{2,1,0:T(8,128)(2,1)} %copy-done.7), custom_call_target="tpu_custom_call" | custom-call | bytes 1048576 | tf_op jit(solution)/shard_map/spread_queries/pallas_call | solution.py:127
  16.6 2.0 %collective-permute-start.1 = (bf16[4,2,128,128]{3,2,1,0:T(8,128)(2,1)}, bf16[4,2,128,128]{3,2,1,0:T(8,128)(2,1)S(1)}, u32[]{:S(2)}, u32[]{:S(2)}) collective-permute-start(bf16[4,2,128,128]{3,2,1,0:T(8,128)(2,1)} %get-tuple-element.33), channel_id=1, source_target_pairs={{0,4},{2,6},{4,0},{6,2},{8,12},{10,14},{12,8},{14,10},{16,20},{18,... | collective-permute-start | bytes 786440 | tf_op jit(solution)/shard_map/ppermute | solution.py:461
  18.6 20.2 %collective-permute-done.1.got = bf16[4,2,128,128]{3,2,1,0:T(8,128)(2,1)S(1)} collective-permute-done((bf16[4,2,128,128]{3,2,1,0:T(8,128)(2,1)}, bf16[4,2,128,128]{3,2,1,0:T(8,128)(2,1)S(1)}, u32[]{:S(2)}, u32[]{:S(2)}) %collective-permute-start.1) | collective-permute-done | bytes 262176 | tf_op jit(solution)/shard_map/ppermute | solution.py:461
  38.8 0.7 copy-done.8
  39.5 17.6 %gather_queries.1 = (bf16[2,2,128,128]{3,2,1,0:T(8,128)(2,1)}, bf16[2,2,128,128]{3,2,1,0:T(8,128)(2,1)}, bf16[2,2,128,128]{3,2,1,0:T(8,128)(2,1)}, bf16[2,2,128,128]{3,2,1,0:T(8,128)(2,1)}) custom-call(s32[4]{0:T(128)S(1)} %pad_add_fusion.place_ref, bf16[4,2,128,128]{3,2,1,0:T(8,128)(2,1)} %get-tuple-element.32.keep, bf16[4,2,128,128]{3,2,1,0:T(8,128)(2,1)} %copy-done.8), custom_call_target="tpu_custom_call" | custom-call | bytes 1048576 | tf_op jit(solution)/shard_map/gather_queries/pallas_call | solution.py:159
  57.2 9.5 %collective-permute-done.2 = bf16[2,2,128,128]{3,2,1,0:T(8,128)(2,1)S(1)} collective-permute-done((bf16[2,2,128,128]{3,2,1,0:T(8,128)(2,1)}, bf16[2,2,128,128]{3,2,1,0:T(8,128)(2,1)S(1)}, u32[]{:S(2)}, u32[]{:S(2)}) %collective-permute-start.2) | collective-permute-done | bytes 131104 | tf_op jit(solution)/shard_map/ppermute | solution.py:461
  66.8 5.6 %collective-permute-start.4 = (bf16[2,2,128,128]{3,2,1,0:T(8,128)(2,1)}, bf16[2,2,128,128]{3,2,1,0:T(8,128)(2,1)S(1)}, u32[]{:S(2)}, u32[]{:S(2)}) collective-permute-start(bf16[2,2,128,128]{3,2,1,0:T(8,128)(2,1)} %get-tuple-element.41), channel_id=1, source_target_pairs={{0,16},{2,18},{4,20},{6,22},{8,24},{10,26},{12,28},{14,30},{16,0},... | collective-permute-start | bytes 393224 | tf_op jit(solution)/shard_map/ppermute | solution.py:461
  72.4 3.3 %attend_new.1.rest_0_ = f32[2048,256]{1,0:T(8,128)S(1)} custom-call(s32[4]{0:T(128)S(1)} %pad_add_fusion.place_ref, bf16[16,5,128,128]{3,2,1,0:T(8,128)(2,1)S(1)} %all-to-all-done.message), custom_call_target="tpu_custom_call" | custom-call | flops 2147483648 | bytes 4194304 | tf_op jit(solution)/shard_map/attend_new/pallas_call | solution.py:215
  75.7 6.4 %attend.2 = bf16[16,64,256]{2,1,0:T(8,128)(2,1)} custom-call(s32[4]{0:T(128)S(1)} %pad_add_fusion.place_ref, s32[2,16]{1,0:T(2,128)S(1)} %copy-done.5, s32[2]{0:T(128)S(1)} %copy-done.6, bf16[16,5,128,128]{3,2,1,0:T(8,128)(2,1)S(1)} %all-to-all-done.message, bf16[16,5,128,128]{3,2,1,0:T(8,128)(2,1)S(1)} %collective-permute-done.3.other, ...), custom_call_target="tpu_custom_call" | custom-call | flops 6442450944 | bytes 8388608 | tf_op jit(solution)/shard_map/attend/pallas_call | solution.py:297
  82.2 6.2 %all-to-all-start.1 = ((bf16[16,64,256]{2,1,0:T(8,128)(2,1)}), bf16[16,64,256]{2,1,0:T(8,128)(2,1)S(1)}, u32[]{:S(2)}, u32[]{:S(2)}) async-start(bf16[16,64,256]{2,1,0:T(8,128)(2,1)} %attend.2), calls=%async_computation.1 | async-start | bytes 1048576 | tf_op jit(solution)/shard_map/all_to_all | solution.py:478
  88.4 1.7 %copy-done.4 = bf16[16,5,128,128]{3,2,1,0:T(8,128)(2,1)S(1)} copy-done((bf16[16,5,128,128]{3,2,1,0:T(8,128)(2,1)S(1)}, bf16[16,5,128,128]{3,2,1,0:T(8,128)(2,1)}, u32[]{:S(2)}) %copy-start.4) | copy-done | bytes 2621464
  90.1 10.3 %attend.3 = bf16[16,64,256]{2,1,0:T(8,128)(2,1)} custom-call(s32[4]{0:T(128)S(1)} %pad_add_fusion.place_ref, s32[2,16]{1,0:T(2,128)S(1)} %copy-done.5, s32[2]{0:T(128)S(1)} %copy-done.6, bf16[16,5,128,128]{3,2,1,0:T(8,128)(2,1)S(1)} %all-to-all-done.message, bf16[16,5,128,128]{3,2,1,0:T(8,128)(2,1)S(1)} %copy-done.4, bf16[4,1,128,128]{3,2,1,0:T(8,128)(2,1)} %bitcast.22, ...), custom_call_target="tpu_custom_call" | custom-call | flops 6442450944 | bytes 8388608 | tf_op jit(solution)/shard_map/attend/pallas_call | solution.py:297
  100.4 2.4 %all-to-all-done.1.attended = bf16[16,64,256]{2,1,0:T(8,128)(2,1)S(1)} async-done(((bf16[16,64,256]{2,1,0:T(8,128)(2,1)}), bf16[16,64,256]{2,1,0:T(8,128)(2,1)S(1)}, u32[]{:S(2)}, u32[]{:S(2)}) %all-to-all-start.1) | async-done | bytes 524320 | tf_op jit(solution)/shard_map/all_to_all | solution.py:478
  102.8 3.4 %project.4 = bf16[128,1536]{1,0:T(8,128)(2,1)S(1)} custom-call(bf16[16,64,256]{2,1,0:T(8,128)(2,1)S(1)} %all-to-all-done.1.attended, bf16[2048,4608]{1,0:T(8,128)(2,1)} %bitcast.14), custom_call_target="tpu_custom_call" | custom-call | flops 805306368 | bytes 6291456 | tf_op jit(solution)/shard_map/project/pallas_call | solution.py:363
  106.2 4.1 %all-to-all-start.2 = ((bf16[16,64,256]{2,1,0:T(8,128)(2,1)}), bf16[16,64,256]{2,1,0:T(8,128)(2,1)S(1)}, u32[]{:S(2)}, u32[]{:S(2)}) async-start(bf16[16,64,256]{2,1,0:T(8,128)(2,1)} %attend.3), calls=%async_computation.2 | async-start | bytes 1048576 | tf_op jit(solution)/shard_map/all_to_all | solution.py:491
  110.3 1.6 %collective-permute-start.6 = (bf16[128,1536]{1,0:T(8,128)(2,1)S(1)}, bf16[128,1536]{1,0:T(8,128)(2,1)S(1)}, u32[]{:S(2)}, u32[]{:S(2)}) collective-permute-start(bf16[128,1536]{1,0:T(8,128)(2,1)S(1)} %project.4), channel_id=1, source_target_pairs={{0,1},{1,0},{2,3},{3,2},{4,5},{5,4},{6,7},{7,6},{8,9},{9,8},{10,11... | collective-permute-start | bytes 1179656 | tf_op jit(solution)/shard_map/ppermute | solution.py:494
  111.9 4.0 %project.5 = bf16[128,2048]{1,0:T(8,128)(2,1)S(1)} custom-call(bf16[16,64,256]{2,1,0:T(8,128)(2,1)S(1)} %all-to-all-done.1.attended, bf16[2048,4608]{1,0:T(8,128)(2,1)} %bitcast.15), custom_call_target="tpu_custom_call" | custom-call | flops 1073741824 | bytes 8388608 | tf_op jit(solution)/shard_map/project/pallas_call | solution.py:363
  115.9 0.6 collective-permute-start.7
  116.5 5.8 %collective-permute-done.6.__0_ = bf16[128,1536]{1,0:T(8,128)(2,1)S(1)} collective-permute-done((bf16[128,1536]{1,0:T(8,128)(2,1)S(1)}, bf16[128,1536]{1,0:T(8,128)(2,1)S(1)}, u32[]{:S(2)}, u32[]{:S(2)}) %collective-permute-start.6) | collective-permute-done | bytes 393248 | tf_op jit(solution)/shard_map/ppermute | solution.py:494
  122.3 0.8 copy-done.1
  123.1 2.7 %project.7 = bf16[128,1024]{1,0:T(8,128)(2,1)S(1)} custom-call(bf16[16,64,256]{2,1,0:T(8,128)(2,1)S(1)} %all-to-all-done.1.attended, bf16[2048,4608]{1,0:T(8,128)(2,1)} %bitcast.16), custom_call_target="tpu_custom_call" | custom-call | flops 536870912 | bytes 4194304 | tf_op jit(solution)/shard_map/project/pallas_call | solution.py:363
  125.8 1.6 %collective-permute-start.8 = (bf16[128,1024]{1,0:T(8,128)(2,1)S(1)}, bf16[128,1024]{1,0:T(8,128)(2,1)S(1)}, u32[]{:S(2)}, u32[]{:S(2)}) collective-permute-start(bf16[128,1024]{1,0:T(8,128)(2,1)S(1)} %project.7), channel_id=1, source_target_pairs={{0,1},{1,0},{2,3},{3,2},{4,5},{5,4},{6,7},{7,6},{8,9},{9,8},{10,11... | collective-permute-start | bytes 786440 | tf_op jit(solution)/shard_map/ppermute | solution.py:494
  127.4 1.1 copy-done.2
  128.5 7.1 %project.6 = (f32[128,4608]{1,0:T(8,128)S(1)}, f32[128,128]{1,0:T(8,128)S(1)}) custom-call(bf16[16,64,256]{2,1,0:T(8,128)(2,1)S(1)} %all-to-all-done.2.attended, bf16[2048,4608]{1,0:T(8,128)(2,1)} %bitcast.17, bf16[128,1536]{1,0:T(8,128)(2,1)S(1)} %copy-done.2), custom_call_target="tpu_custom_call" | custom-call | flops 2415919104 | bytes 18874368 | tf_op jit(solution)/shard_map/project/pallas_call | solution.py:363
  135.7 3.0 %collective-permute-done.8.refs_1_ = bf16[128,1024]{1,0:T(8,128)(2,1)S(1)} collective-permute-done((bf16[128,1024]{1,0:T(8,128)(2,1)S(1)}, bf16[128,1024]{1,0:T(8,128)(2,1)S(1)}, u32[]{:S(2)}, u32[]{:S(2)}) %collective-permute-start.8) | collective-permute-done | bytes 262176 | tf_op jit(solution)/shard_map/ppermute | solution.py:494
  138.7 1.5 %finish.1 = bf16[2,64,4608]{2,1,0:T(8,128)(2,1)} custom-call(f32[128,4608]{1,0:T(8,128)S(1)} %get-tuple-element.54.projected, f32[128,128]{1,0:T(8,128)S(1)} %get-tuple-element.55.squares_ref, bf16[128,2048]{1,0:T(8,128)(2,1)S(1)} %collective-permute-done.7.refs_0_, bf16[128,1024]{1,0:T(8,128)(2,1)S(1)} %collective-permute-done.8.refs_1_, ...), custom_call_target="tpu_custom_call" | custom-call | bytes 6291456 | tf_op jit(solution)/shard_map/finish/pallas_call | solution.py:422
  (33 shorter events, 0.3 us)
Async XLA Ops:
  3.2 63.5 %all-to-all-start = ((bf16[16,5,128,128]{3,2,1,0:T(8,128)(2,1)}), bf16[16,5,128,128]{3,2,1,0:T(8,128)(2,1)S(1)}, u32[]{:S(2)}, u32[]{:S(2)}) async-start(bf16[16,5,128,128]{3,2,1,0:T(8,128)(2,1)} %bitcast.18), calls=%async_computation | async-start | bytes 5242880 | tf_op jit(solution)/shard_map/all_to_all | solution.py:464
  11.5 1.6 %collective-permute-start = (bf16[64,16,128]{2,1,0:T(8,128)(2,1)S(1)}, bf16[64,16,128]{2,1,0:T(8,128)(2,1)S(1)}, u32[]{:S(2)}, u32[]{:S(2)}) collective-permute-start(bf16[64,16,128]{2,1,0:T(8,128)(2,1)S(1)} %dynamic-slice_bitcast_fusion), channel_id=1, source_target_pairs={{0,2},{2,0},{4,6},{6,4},{8,10},{10,8},{12,14},{14,12},{16,18},{18,... | collective-permute-start | bytes 786440 | tf_op jit(solution)/shard_map/ppermute | solution.py:461
  13.2 0.7 copy-start.7
  16.6 22.2 %collective-permute-start.1 = (bf16[4,2,128,128]{3,2,1,0:T(8,128)(2,1)}, bf16[4,2,128,128]{3,2,1,0:T(8,128)(2,1)S(1)}, u32[]{:S(2)}, u32[]{:S(2)}) collective-permute-start(bf16[4,2,128,128]{3,2,1,0:T(8,128)(2,1)} %get-tuple-element.33), channel_id=1, source_target_pairs={{0,4},{2,6},{4,0},{6,2},{8,12},{10,14},{12,8},{14,10},{16,20},{18,... | collective-permute-start | bytes 786440 | tf_op jit(solution)/shard_map/ppermute | solution.py:461
  38.8 0.7 copy-start.8
  57.1 9.6 %collective-permute-start.2 = (bf16[2,2,128,128]{3,2,1,0:T(8,128)(2,1)}, bf16[2,2,128,128]{3,2,1,0:T(8,128)(2,1)S(1)}, u32[]{:S(2)}, u32[]{:S(2)}) collective-permute-start(bf16[2,2,128,128]{3,2,1,0:T(8,128)(2,1)} %get-tuple-element.35), channel_id=1, source_target_pairs={{0,8},{2,10},{4,12},{6,14},{8,0},{10,2},{12,4},{14,6},{16,24},{18,... | collective-permute-start | bytes 393224 | tf_op jit(solution)/shard_map/ppermute | solution.py:461
  66.7 9.0 %copy-start.10 = (bf16[2,2,128,128]{3,2,1,0:T(8,128)(2,1)}, bf16[2,2,128,128]{3,2,1,0:T(8,128)(2,1)S(1)}, u32[]{:S(2)}) copy-start(bf16[2,2,128,128]{3,2,1,0:T(8,128)(2,1)S(1)} %collective-permute-done.2) | copy-start | bytes 393220
  66.7 9.0 %copy-start.5 = (s32[2,16]{1,0:T(2,128)S(1)}, s32[2,16]{1,0:T(2,128)}, u32[]{:S(2)}) copy-start(s32[2,16]{1,0:T(2,128)} %table_ref.3) | copy-start | bytes 388
  66.7 9.0 %copy-start.6 = (s32[2]{0:T(128)S(1)}, s32[2]{0:T(128)}, u32[]{:S(2)}) copy-start(s32[2]{0:T(128)} %len_ref.3) | copy-start | bytes 28
  66.7 9.0 %collective-permute-start.3 = (bf16[16,5,128,128]{3,2,1,0:T(8,128)(2,1)S(1)}, bf16[16,5,128,128]{3,2,1,0:T(8,128)(2,1)S(1)}, u32[]{:S(2)}, u32[]{:S(2)}) collective-permute-start(bf16[16,5,128,128]{3,2,1,0:T(8,128)(2,1)S(1)} %all-to-all-done.message), channel_id=1, source_target_pairs={{0,2},{2,0},{4,6},{6,4},{8,10},{10,8},{12,14},{14,12},{16,18},{18,... | collective-permute-start | bytes 7864328 | tf_op jit(solution)/shard_map/ppermute | solution.py:461
  66.8 15.4 %collective-permute-start.4 = (bf16[2,2,128,128]{3,2,1,0:T(8,128)(2,1)}, bf16[2,2,128,128]{3,2,1,0:T(8,128)(2,1)S(1)}, u32[]{:S(2)}, u32[]{:S(2)}) collective-permute-start(bf16[2,2,128,128]{3,2,1,0:T(8,128)(2,1)} %get-tuple-element.41), channel_id=1, source_target_pairs={{0,16},{2,18},{4,20},{6,22},{8,24},{10,26},{12,28},{14,30},{16,0},... | collective-permute-start | bytes 393224 | tf_op jit(solution)/shard_map/ppermute | solution.py:461
  72.4 9.8 %collective-permute-start.5 = (bf16[2,2,128,128]{3,2,1,0:T(8,128)(2,1)}, bf16[2,2,128,128]{3,2,1,0:T(8,128)(2,1)S(1)}, u32[]{:S(2)}, u32[]{:S(2)}) collective-permute-start(bf16[2,2,128,128]{3,2,1,0:T(8,128)(2,1)} %get-tuple-element.42), channel_id=1, source_target_pairs={{0,24},{2,26},{4,28},{6,30},{8,16},{10,18},{12,20},{14,22},{16,8},... | collective-permute-start | bytes 393224 | tf_op jit(solution)/shard_map/ppermute | solution.py:461
  75.7 6.4 %copy-start.3 = (bf16[16,5,128,128]{3,2,1,0:T(8,128)(2,1)}, bf16[16,5,128,128]{3,2,1,0:T(8,128)(2,1)S(1)}, u32[]{:S(2)}) copy-start(bf16[16,5,128,128]{3,2,1,0:T(8,128)(2,1)S(1)} %collective-permute-done.3.other) | copy-start | bytes 7864324
  82.1 6.2 %copy-start.11 = (bf16[2,2,128,128]{3,2,1,0:T(8,128)(2,1)}, bf16[2,2,128,128]{3,2,1,0:T(8,128)(2,1)S(1)}, u32[]{:S(2)}) copy-start(bf16[2,2,128,128]{3,2,1,0:T(8,128)(2,1)S(1)} %collective-permute-done.4) | copy-start | bytes 393220
  82.2 6.2 %copy-start.12 = (bf16[2,2,128,128]{3,2,1,0:T(8,128)(2,1)}, bf16[2,2,128,128]{3,2,1,0:T(8,128)(2,1)S(1)}, u32[]{:S(2)}) copy-start(bf16[2,2,128,128]{3,2,1,0:T(8,128)(2,1)S(1)} %collective-permute-done.5) | copy-start | bytes 393220
  82.2 20.7 %all-to-all-start.1 = ((bf16[16,64,256]{2,1,0:T(8,128)(2,1)}), bf16[16,64,256]{2,1,0:T(8,128)(2,1)S(1)}, u32[]{:S(2)}, u32[]{:S(2)}) async-start(bf16[16,64,256]{2,1,0:T(8,128)(2,1)} %attend.2), calls=%async_computation.1 | async-start | bytes 1048576 | tf_op jit(solution)/shard_map/all_to_all | solution.py:478
  88.4 1.7 %copy-start.4 = (bf16[16,5,128,128]{3,2,1,0:T(8,128)(2,1)S(1)}, bf16[16,5,128,128]{3,2,1,0:T(8,128)(2,1)}, u32[]{:S(2)}) copy-start(bf16[16,5,128,128]{3,2,1,0:T(8,128)(2,1)} %copy-done.3) | copy-start | bytes 7864324
  106.2 21.2 %all-to-all-start.2 = ((bf16[16,64,256]{2,1,0:T(8,128)(2,1)}), bf16[16,64,256]{2,1,0:T(8,128)(2,1)S(1)}, u32[]{:S(2)}, u32[]{:S(2)}) async-start(bf16[16,64,256]{2,1,0:T(8,128)(2,1)} %attend.3), calls=%async_computation.2 | async-start | bytes 1048576 | tf_op jit(solution)/shard_map/all_to_all | solution.py:491
  110.3 12.0 %collective-permute-start.6 = (bf16[128,1536]{1,0:T(8,128)(2,1)S(1)}, bf16[128,1536]{1,0:T(8,128)(2,1)S(1)}, u32[]{:S(2)}, u32[]{:S(2)}) collective-permute-start(bf16[128,1536]{1,0:T(8,128)(2,1)S(1)} %project.4), channel_id=1, source_target_pairs={{0,1},{1,0},{2,3},{3,2},{4,5},{5,4},{6,7},{7,6},{8,9},{9,8},{10,11... | collective-permute-start | bytes 1179656 | tf_op jit(solution)/shard_map/ppermute | solution.py:494
  115.9 19.7 %collective-permute-start.7 = (bf16[128,2048]{1,0:T(8,128)(2,1)S(1)}, bf16[128,2048]{1,0:T(8,128)(2,1)S(1)}, u32[]{:S(2)}, u32[]{:S(2)}) collective-permute-start(bf16[128,2048]{1,0:T(8,128)(2,1)S(1)} %project.5), channel_id=1, source_target_pairs={{0,1},{1,0},{2,3},{3,2},{4,5},{5,4},{6,7},{7,6},{8,9},{9,8},{10,11... | collective-permute-start | bytes 1572872 | tf_op jit(solution)/shard_map/ppermute | solution.py:494
  122.3 0.8 copy-start.1
  123.1 4.3 %copy-start.9 = (f32[4608]{0:T(1024)S(1)}, f32[4608]{0:T(1024)}, u32[]{:S(2)}) copy-start(f32[4608]{0:T(1024)} %param.19) | copy-start | bytes 55300
  125.8 12.9 %collective-permute-start.8 = (bf16[128,1024]{1,0:T(8,128)(2,1)S(1)}, bf16[128,1024]{1,0:T(8,128)(2,1)S(1)}, u32[]{:S(2)}, u32[]{:S(2)}) collective-permute-start(bf16[128,1024]{1,0:T(8,128)(2,1)S(1)} %project.7), channel_id=1, source_target_pairs={{0,1},{1,0},{2,3},{3,2},{4,5},{5,4},{6,7},{7,6},{8,9},{9,8},{10,11... | collective-permute-start | bytes 786440 | tf_op jit(solution)/shard_map/ppermute | solution.py:494
  127.4 11.3 %copy-start = (bf16[2,64,4608]{2,1,0:T(8,128)(2,1)S(1)}, bf16[2,64,4608]{2,1,0:T(8,128)(2,1)}, u32[]{:S(2)}) copy-start(bf16[2,64,4608]{2,1,0:T(8,128)(2,1)} %refs_2_.3) | copy-start | bytes 3538948
  127.4 1.1 copy-start.2
